TPU v7x, 512 devices: a whole 4x4x16 slice. The times are simulated.
512 devices in a mesh: dp: 32 (over z, core), tensor: 16 (over x, y).
Axes of the slice: x: 4, y: 4, z: 16, core: 2. Of those that a mesh axis runs over, the one named last changes fastest.
Arguments:
- resid: bfloat16 [4096, 8192], P('dp', 'tensor'), may hold values from -6 to 6
- context: bfloat16 [4096, 4096], P('dp', 'tensor'), may hold values from -6 to 6
- out_weight: bfloat16 [4096, 8192], P('tensor', 'dp'), may hold values from -0.1875 to 0.1875
- owners: int32 [4096, 1], P('dp'), may hold values from 0 to 31; in each aligned block of 128 rows (0 to 127, 128 to 255, ...) at most 8 rows name the same one
- query_lengths: int32 [32], replicated, may hold values from 96 to 128, as said below
- student_rows: bfloat16 [4096, 2048], P('dp'), may hold values from -6 to 6
- up_weight: bfloat16 [2048, 2816], P(None, 'tensor'), may hold values from -0.125 to 0.125
- down_weight: bfloat16 [2048, 2816], P(None, 'tensor'), may hold values from -0.109375 to 0.109375
- proj_weight: bfloat16 [2048, 8192], P(None, 'tensor'), may hold values from -0.125 to 0.125
Outputs:
- owner_loss: float32 [32], P('dp')
- grad_up: float32 [2048, 2816], P('dp', 'tensor')
- grad_down: float32 [2048, 2816], P('dp', 'tensor')
Inputs may be any that keep to these rules, and one draw needn't show every extreme that they name: `owners`: among the rows of one index of dp no owner is named more than 8 times, a bound that some block reaches. `query_lengths`: some index of dp has all 128 rows live.
All inputs are finite; a program needn't handle non-finite values.
Results may differ from a plain program's by a relative error of at most 0.0075.
Values may be sent and summed in bfloat16 or wider, within the bound.
No kernel may reach another device: no remote copies, remote signals or barrier semaphores. Data moves between devices by JAX's collectives and lax.ppermute only.
A program may use at most 64 MiB of HBM per device.

v0:
```python
import jax
import jax.numpy as jnp
from jax import lax
from jax.sharding import PartitionSpec as P

D = 8192
DS = 2048


def on_device(
    resid,
    context,
    out_weight,
    owners,
    query_lengths,
    student_rows,
    up_weight,
    down_weight,
    proj_weight,
):
    partial_value = jnp.dot(
        context,
        lax.all_gather(out_weight, "dp", axis=1, tiled=True),
        preferred_element_type=jnp.float32,
    )
    groups = lax.axis_size("tensor")
    query_rows = resid.shape[0]
    pieces = partial_value.astype(jnp.bfloat16).reshape(
        query_rows, groups, partial_value.shape[1] // groups
    )
    received = lax.all_to_all(pieces, "tensor", split_axis=1, concat_axis=1, tiled=True)
    summed = jnp.sum(received.astype(jnp.float32), axis=1)
    target = (resid.astype(jnp.float32) + summed).astype(jnp.bfloat16)
    owner_count = lax.axis_size("dp")
    capacity = 2 * query_rows // owner_count
    slot_total = owner_count * capacity
    owner_ids = owners[:, 0]
    position = jnp.arange(query_rows, dtype=jnp.int32)
    own_length = query_lengths[lax.axis_index("dp")]
    valid = position < own_length
    same = (
        (owner_ids[:, None] == owner_ids[None, :])
        & valid[None, :]
        & (position[None, :] < position[:, None])
    )
    rank_index = jnp.sum(same.astype(jnp.int32), axis=1)
    slot_index = owner_ids * capacity + rank_index
    picker = (
        (slot_index[None, :] == jnp.arange(slot_total, dtype=jnp.int32)[:, None]) & valid[None, :]
    ).astype(jnp.bfloat16)
    send_target = jnp.dot(picker, target, preferred_element_type=jnp.float32).astype(jnp.bfloat16)
    send_target = send_target.reshape(owner_count, capacity, target.shape[1])
    send_live = (
        jnp.sum(picker.astype(jnp.float32), axis=1)
        .astype(jnp.bfloat16)
        .reshape(owner_count, capacity)
    )
    send_student = jnp.dot(picker, student_rows, preferred_element_type=jnp.float32).astype(
        jnp.bfloat16
    )
    send_student = send_student.reshape(owner_count, capacity, student_rows.shape[1])
    got_target, got_student, got_live = (
        lax.all_to_all(send_target, "dp", split_axis=0, concat_axis=0, tiled=True),
        lax.all_to_all(send_student, "dp", split_axis=0, concat_axis=0, tiled=True),
        lax.all_to_all(send_live, "dp", split_axis=0, concat_axis=0, tiled=True),
    )
    student_in = got_student.reshape(slot_total, DS)
    target_rows = got_target.reshape(slot_total, target.shape[1])
    live_rows = got_live.reshape(slot_total).astype(jnp.float32)
    total_live = jnp.sum(query_lengths).astype(jnp.float32)
    loss_scale = owner_count / (total_live * D)
    inputs = student_in.astype(jnp.float32)
    normed = (inputs * lax.rsqrt(jnp.mean(inputs * inputs, axis=-1, keepdims=True) + 1e-05)).astype(
        jnp.bfloat16
    )
    preact = jnp.dot(normed, up_weight, preferred_element_type=jnp.float32)
    hidden = jax.nn.silu(preact).astype(jnp.bfloat16)
    mixed_part = lax.dot_general(
        hidden, down_weight, (((1,), (1,)), ((), ())), preferred_element_type=jnp.float32
    )
    mixed = lax.psum(mixed_part, "tensor")
    updated = (inputs + mixed).astype(jnp.bfloat16)
    projected = jnp.dot(updated, proj_weight, preferred_element_type=jnp.float32)
    residue = projected - target_rows.astype(jnp.float32)
    squares_part = jnp.sum(live_rows * jnp.sum(residue * residue, axis=-1))
    cotangent = (2.0 * loss_scale * live_rows[:, None] * residue).astype(jnp.bfloat16)
    back_part = lax.dot_general(
        cotangent, proj_weight, (((1,), (1,)), ((), ())), preferred_element_type=jnp.float32
    )
    back_sum, squares = lax.psum((back_part, squares_part), "tensor")
    owner_loss = jnp.reshape(squares * loss_scale, (1,))
    out_grad = back_sum.astype(jnp.bfloat16)
    down_term = lax.dot_general(
        out_grad, hidden, (((0,), (0,)), ((), ())), preferred_element_type=jnp.float32
    )
    hidden_grad = jnp.dot(out_grad, down_weight, preferred_element_type=jnp.float32)
    gate_sig = jax.nn.sigmoid(preact)
    pre_grad = (hidden_grad * gate_sig * (1.0 + preact * (1.0 - gate_sig))).astype(jnp.bfloat16)
    up_term = lax.dot_general(
        normed, pre_grad, (((0,), (0,)), ((), ())), preferred_element_type=jnp.float32
    )
    grad_up, grad_down = (
        lax.psum_scatter(up_term, "dp", scatter_dimension=0, tiled=True),
        lax.psum_scatter(down_term, "dp", scatter_dimension=0, tiled=True),
    )
    return (owner_loss, grad_up, grad_down)


def solution(mesh):
    return jax.shard_map(
        on_device,
        mesh=mesh,
        in_specs=(
            P("dp", "tensor"),
            P("dp", "tensor"),
            P("tensor", "dp"),
            P("dp", None),
            P(),
            P("dp", None),
            P(None, "tensor"),
            P(None, "tensor"),
            P(None, "tensor"),
        ),
        out_specs=(P("dp"), P("dp", "tensor"), P("dp", "tensor")),
        check_vma=False,
    )
```

profile of v0, /device:TPU:1, one launch (start us, length us, event | category | flops | bytes accessed | tf_op | source)
XLA Modules:
  0.0 592.8 jit_solution(5863982692545060659)
XLA Ops:
  8.0 0.0 copy-start
  8.0 0.0 copy-start.4
  8.0 0.0 all-gather.2.cloned.1.call-start
  8.1 0.7 all-gather.2.cloned.1.call-update
  8.8 1.2 dynamic_slice.3
  10.0 0.6 iota_compare_fusion.2
  10.7 0.9 convert_reduce_fusion.1
  11.6 0.7 multiply_add_fusion
  12.2 2.5 fusion.2
  14.7 16.7 %all-to-all-start.1 = ((bf16[32,8,2048]{2,1,0:T(8,128)(2,1)}), bf16[32,8,2048]{2,1,0:T(8,128)(2,1)S(1)}, u32[]{:S(2)}, u32[]{:S(2)}) async-start(bf16[32,8,2048]{2,1,0:T(8,128)(2,1)} %fusion.2), calls=%async_computation.1 | async-start | bytes 2097152 | tf_op jit(solution)/shard_map/all_to_all | solution.py:64
  31.5 98.7 %all-gather.2.cloned.1.call-done = bf16[256,8192]{1,0:T(8,128)(2,1)} async-done(((bf16[256,256]{1,0:T(8,128)(2,1)}), bf16[256,8192]{1,0:T(8,128)(2,1)}) %all-gather.2.cloned.1.call-update) | async-done | bytes 4194320 | tf_op jit(solution)/shard_map/all_gather | solution.py:23
  130.1 0.0 copy-done.4
  130.1 2.9 convolution_convert_fusion
  133.0 1.6 copy.22
  134.6 0.0 all-to-all-done.1
  134.6 7.0 %all-to-all-start.2 = ((bf16[128,16,512]{2,0,1:T(8,128)(2,1)}), bf16[128,16,512]{2,0,1:T(8,128)(2,1)}, u32[]{:S(2)}, u32[]{:S(2)}) async-start(bf16[128,16,512]{2,0,1:T(8,128)(2,1)} %bitcast.43), calls=%async_computation.2 | async-start | bytes 4194304 | tf_op jit(solution)/shard_map/all_to_all | solution.py:31
  141.6 0.0 all-reduce.4.cloned.1.call-start
  141.7 0.3 fusion.5
  142.0 0.1 rsqrt.12
  142.1 0.0 copy-start.2
  142.1 1.7 fusion.16
  143.8 0.0 copy-done.2
  143.8 1.8 fusion.36
  145.6 0.0 copy-start.3
  145.6 0.0 all-reduce.4.cloned.1.call-update
  145.6 0.0 copy-start.5
  145.6 24.8 %all-to-all-done.2 = bf16[128,16,512]{2,0,1:T(8,128)(2,1)} async-done(((bf16[128,16,512]{2,0,1:T(8,128)(2,1)}), bf16[128,16,512]{2,0,1:T(8,128)(2,1)}, u32[]{:S(2)}, u32[]{:S(2)}) %all-to-all-start.2) | async-done | bytes 2097184 | tf_op jit(solution)/shard_map/all_to_all | solution.py:31
  170.4 1.9 convert_reduce_fusion
  172.3 0.0 copy-done.3
  172.3 0.9 fusion.6
  173.3 9.7 %all-to-all-start.3 = ((bf16[32,8,512]{2,1,0:T(8,128)(2,1)}), bf16[32,8,512]{2,1,0:T(8,128)(2,1)}, u32[]{:S(2)}, u32[]{:S(2)}) async-start(bf16[32,8,512]{2,1,0:T(8,128)(2,1)} %fusion.6), calls=%async_computation.3 | async-start | bytes 524288 | tf_op jit(solution)/shard_map/all_to_all | solution.py:63
  183.0 0.0 copy-done.5
  183.0 0.6 reduce_sum.75
  184.3 0.1 fusion.28
  184.4 0.7 all_to_all.20
  185.2 19.9 %all-to-all-done.3 = bf16[32,8,512]{2,1,0:T(8,128)(2,1)} async-done(((bf16[32,8,512]{2,1,0:T(8,128)(2,1)}), bf16[32,8,512]{2,1,0:T(8,128)(2,1)}, u32[]{:S(2)}, u32[]{:S(2)}) %all-to-all-start.3) | async-done | bytes 262176 | tf_op jit(solution)/shard_map/all_to_all | solution.py:63
  205.0 4.5 all-to-all-start
  209.5 0.0 reduce-scatter.3.cloned.1.call-start
  209.6 55.9 %all-reduce.4.cloned.1.call-done = f32[256,2048]{1,0:T(8,128)} async-done(((f32[256,2048]{1,0:T(8,128)}), f32[256,2048]{1,0:T(8,128)}) %all-reduce.4.cloned.1.call-update) | async-done | bytes 2097168 | tf_op jit(solution)/shard_map/psum | solution.py:81
  265.5 0.0 copy-done
  265.5 3.1 multiply_reduce_fusion
  268.6 0.1 reduce_sum.73
  268.7 0.0 all-to-all-done
  268.7 0.6 convert_multiply_fusion.1
  269.3 0.1 mul.84
  269.4 3.1 fusion.18
  272.5 80.0 %all-reduce.5 = (f32[]{:T(128)}, bf16[256,2048]{1,0:T(8,128)(2,1)}) all-reduce(f32[]{:T(128)} %get-tuple-element.6, f32[256,2048]{1,0:T(8,128)} %fusion.18), channel_id=1, replica_groups=mesh['dp'=32,'tensor'=16] {'tensor'}, use_global_device_ids=true, to_apply=%region_7.8 | all-reduce | flops 524289 | bytes 3145736 | tf_op jit(solution)/shard_map/psum | solution.py:90
  352.5 4.2 fusion.9
  356.6 0.0 copy-start.1
  356.6 0.0 reduce-scatter.3.cloned.1.call-update
  356.7 0.0 reduce-scatter.5.cloned.1.call-start
  356.7 1.1 copy-done.1
  357.9 1.8 fusion.11
  359.7 0.0 reduce-scatter.5.cloned.1.call-update
  360.3 113.3 %reduce-scatter.3.cloned.1.call-done = f32[64,176]{1,0:T(8,128)} async-done(((f32[2048,176]{1,0:T(8,128)}), f32[64,176]{1,0:T(8,128)}) %reduce-scatter.3.cloned.1.call-update) | async-done | bytes 45072 | tf_op jit(solution)/shard_map/reduce_scatter | solution.py:103
  473.7 110.9 %reduce-scatter.5.cloned.1.call-done = f32[64,176]{1,0:T(8,128)} async-done(((f32[2048,176]{1,0:T(8,128)}), f32[64,176]{1,0:T(8,128)}) %reduce-scatter.5.cloned.1.call-update) | async-done | bytes 45072 | tf_op jit(solution)/shard_map/reduce_scatter | solution.py:104
  (1 shorter events, 0.0 us)
Async XLA Ops:
  8.0 257.5 %copy-start = (bf16[2048,512]{1,0:T(8,128)(2,1)S(1)}, bf16[2048,512]{1,0:T(8,128)(2,1)}, u32[]{:S(2)}) copy-start(bf16[2048,512]{1,0:T(8,128)(2,1)} %param.17) | copy-start | bytes 6291460
  8.0 122.1 %copy-start.4 = (bf16[128,256]{1,0:T(8,128)(2,1)S(1)}, bf16[128,256]{1,0:T(8,128)(2,1)}, u32[]{:S(2)}) copy-start(bf16[128,256]{1,0:T(8,128)(2,1)} %param.10) | copy-start | bytes 196612
  8.0 122.1 %all-gather.2.cloned.1.call-start = ((), (), s32[]{:S(2)}) async-start(), calls=%async_computation.7 | async-start | bytes 4325376 | tf_op jit(solution)/shard_map/all_gather | solution.py:23
  14.7 119.9 %all-to-all-start.1 = ((bf16[32,8,2048]{2,1,0:T(8,128)(2,1)}), bf16[32,8,2048]{2,1,0:T(8,128)(2,1)S(1)}, u32[]{:S(2)}, u32[]{:S(2)}) async-start(bf16[32,8,2048]{2,1,0:T(8,128)(2,1)} %fusion.2), calls=%async_computation.1 | async-start | bytes 2097152 | tf_op jit(solution)/shard_map/all_to_all | solution.py:64
  134.6 35.8 %all-to-all-start.2 = ((bf16[128,16,512]{2,0,1:T(8,128)(2,1)}), bf16[128,16,512]{2,0,1:T(8,128)(2,1)}, u32[]{:S(2)}, u32[]{:S(2)}) async-start(bf16[128,16,512]{2,0,1:T(8,128)(2,1)} %bitcast.43), calls=%async_computation.2 | async-start | bytes 4194304 | tf_op jit(solution)/shard_map/all_to_all | solution.py:31
  141.6 123.9 %all-reduce.4.cloned.1.call-start = ((), (), s32[]{:S(2)}) async-start(), calls=%async_computation.6 | async-start | bytes 4194304 | tf_op jit(solution)/shard_map/psum | solution.py:81
  142.1 1.8 copy-start.2
  145.6 26.7 %copy-start.3 = (bf16[128,512]{1,0:T(8,128)(2,1)S(1)}, bf16[128,512]{1,0:T(8,128)(2,1)}, u32[]{:S(2)}) copy-start(bf16[128,512]{1,0:T(8,128)(2,1)} %param.9) | copy-start | bytes 393220
  145.6 37.4 %copy-start.5 = (s32[32]{0:T(128)S(1)}, s32[32]{0:T(128)}, u32[]{:S(2)}) copy-start(s32[32]{0:T(128)} %param.13) | copy-start | bytes 388
  173.3 31.8 %all-to-all-start.3 = ((bf16[32,8,512]{2,1,0:T(8,128)(2,1)}), bf16[32,8,512]{2,1,0:T(8,128)(2,1)}, u32[]{:S(2)}, u32[]{:S(2)}) async-start(bf16[32,8,512]{2,1,0:T(8,128)(2,1)} %fusion.6), calls=%async_computation.3 | async-start | bytes 524288 | tf_op jit(solution)/shard_map/all_to_all | solution.py:63
  205.0 63.6 %all-to-all-start = ((bf16[32,1,8]{2,1,0:T(2,128)(2,1)}), bf16[32,1,8]{2,1,0:T(2,128)(2,1)S(1)}, u32[]{:S(2)}, u32[]{:S(2)}) async-start(bf16[32,1,8]{2,1,0:T(2,128)(2,1)} %all_to_all.20), calls=%async_computation | async-start | bytes 32768 | tf_op jit(solution)/shard_map/all_to_all | solution.py:65
  209.5 264.1 %reduce-scatter.3.cloned.1.call-start = ((), (), s32[]{:S(2)}) async-start(), calls=%async_computation.8 | async-start | bytes 2162688 | tf_op jit(solution)/shard_map/reduce_scatter | solution.py:103
  356.6 1.2 copy-start.1
  356.7 227.9 %reduce-scatter.5.cloned.1.call-start = ((), (), s32[]{:S(2)}) async-start(), calls=%async_computation.9 | async-start | bytes 2162688 | tf_op jit(solution)/shard_map/reduce_scatter | solution.py:104
Sparse Core Ops, SparseCore 0:
  10.9 119.1 all-gather.1
  356.8 116.8 reduce-scatter.2
  477.1 107.4 reduce-scatter.4
Sparse Core Ops, SparseCore 1:
  145.7 119.7 all-reduce.3
where the time goes:
time: 596 us; the launch traced here: 593 us
  waiting for transfers between devices  424 us (71%)
  blocking collectives  80 us (13%)
  starting transfers between devices  38.1 us (6%)
  matrix products  22 us (4%)
  between operations  17.8 us (3%)
    reduce_scatter x1, waiting for transfers between devices, on_device(): lax.psum_scatter(up_term, 'dp', scatter_dimension=0, tiled=True)  113 us
    reduce_scatter x1, waiting for transfers between devices, on_device(): lax.psum_scatter(down_term, 'dp', scatter_dimension=0, tiled=True)  111 us
    all_gather x1, waiting for transfers between devices, on_device(): lax.all_gather(out_weight, 'dp', axis=1, tiled=True)  98.7 us
    psum x1, blocking collectives, on_device(): back_sum, squares = lax.psum((back_part, squares_part), 'tensor')  80 us
    psum x1, waiting for transfers between devices, on_device(): mixed = lax.psum(mixed_part, 'tensor')  55.9 us
    all_to_all x1, waiting for transfers between devices, on_device(): lax.all_to_all(pieces, 'tensor', split_axis=1, concat_axis=1, tiled=True)  24.8 us
    all_to_all x1, waiting for transfers between devices, on_device(): lax.all_to_all(send_target, 'dp', split_axis=0, concat_axis=0, tiled=True)  19.9 us
    all_to_all x1, starting transfers between devices, on_device(): lax.all_to_all(send_student, 'dp', split_axis=0, concat_axis=0, tiled=True)  16.7 us
  transfers between devices with their start and end apart: 8, of which 6 were waited for; matrix products, arithmetic and copies ran while one was open for 4% of the time, Pallas kernels for 0%

commit v1 on v0

v1 whole, which is shorter than its diff:
```python
import jax
import jax.numpy as jnp
from jax import lax
from jax.sharding import PartitionSpec as P

D = 8192
F32 = jnp.float32
BF16 = jnp.bfloat16

CORES = [(d, d ^ 1) for d in range(32)]
NEAR = [[8 * h + 2 * l + c for l in range(4)] for h in range(4) for c in range(2)]
FAR = [[8 * h + 2 * l + c for h in range(4)] for l in range(4) for c in range(2)]


def flat(zh, zl, c, x, y):
    return (8 * zh + 2 * zl + c) * 16 + 4 * x + y


HOME = [
    (flat(zh, zl, c, x, y), flat(x, zl, c, zh, y))
    for zh in range(4)
    for zl in range(4)
    for c in range(2)
    for x in range(4)
    for y in range(4)
]


def swap_all(x, axis, groups=None):
    return lax.all_to_all(x, axis, split_axis=0, concat_axis=0, tiled=True, axis_index_groups=groups)


def spread(x, axis, count, groups=None):
    return swap_all(jnp.broadcast_to(x[None], (count,) + x.shape), axis, groups)


def sum_rows(part, beside=None):
    rows, width = part.shape
    pieces = part.astype(BF16).reshape(16, rows // 16, width)
    if beside is not None:
        beside = jnp.broadcast_to(beside[None, None, :], (16, rows // 16, beside.shape[0]))
        pieces = jnp.concatenate([pieces, beside], axis=2)
    return jnp.sum(swap_all(pieces, "tensor").astype(F32), axis=0)


def halves(x):
    high = lax.reduce_precision(x, 8, 7)
    return high.astype(BF16), (x - high).astype(BF16)


def packed(terms, loss):
    high, low = (part[..., None, None] for part in halves(loss))
    lane = jnp.arange(32, dtype=jnp.int32)
    side = jnp.where(lane == 0, high, jnp.where(lane == 1, low, jnp.zeros((), BF16)))
    side = jnp.broadcast_to(side, terms.shape[:-1] + (32,))
    return jnp.concatenate([terms.astype(BF16), side], axis=-1)


def unpacked(x):
    return x[..., :352], x[..., 0, 352] + x[..., 0, 353]


def all_rows(x):
    return spread(x, "tensor", 16).reshape(16 * x.shape[0], x.shape[1])


def on_device(
    resid,
    context,
    out_weight,
    owners,
    query_lengths,
    student_rows,
    up_weight,
    down_weight,
    proj_weight,
):
    dp = lax.axis_index("dp")
    tensor = lax.axis_index("tensor")
    core = dp % 2
    rows4 = lax.all_gather(context, "dp", axis_index_groups=FAR).reshape(512, 256)
    cols4 = lax.all_gather(out_weight, "dp", axis_index_groups=NEAR)
    cols4_other = lax.ppermute(cols4, "dp", CORES)
    first = jnp.where(core == 0, cols4, cols4_other)
    second = jnp.where(core == 0, cols4_other, cols4)
    wide = jnp.stack([first, second], axis=2)
    head = lax.dot_general(rows4, wide, (((1,), (1,)), ((), ())), preferred_element_type=F32)
    head = head.astype(BF16).reshape(4, 128, 4, 512).transpose(0, 2, 1, 3).reshape(16, 128, 512)
    head_sum = jnp.sum(swap_all(head, "tensor").astype(F32), axis=0).astype(BF16)
    head_sum = lax.ppermute(head_sum, ("dp", "tensor"), HOME)
    target = (resid.astype(F32) + head_sum.astype(F32)).astype(BF16)

    inputs = student_rows.astype(F32)
    normed = (inputs * lax.rsqrt(jnp.mean(inputs * inputs, axis=-1, keepdims=True) + 1e-05)).astype(
        BF16
    )
    preact = jnp.dot(normed, up_weight, preferred_element_type=F32)
    hidden = jax.nn.silu(preact).astype(BF16)
    mixed_part = lax.dot_general(
        hidden, down_weight, (((1,), (1,)), ((), ())), preferred_element_type=F32
    )
    own_inputs = lax.dynamic_slice_in_dim(student_rows, tensor * 8, 8, axis=0).astype(F32)
    updated = all_rows((own_inputs + sum_rows(mixed_part)).astype(BF16))
    projected = jnp.dot(updated, proj_weight, preferred_element_type=F32)

    total_live = jnp.sum(query_lengths).astype(F32)
    loss_scale = 32.0 / (total_live * D)
    own_length = lax.dynamic_index_in_dim(query_lengths, dp, keepdims=False)
    live = (jnp.arange(128, dtype=jnp.int32) < own_length).astype(F32)
    residue = projected - target.astype(F32)
    squares = live * jnp.sum(residue * residue, axis=-1)
    named = (owners == jnp.arange(32, dtype=jnp.int32)[None, :]).astype(F32)
    loss_part = jnp.sum(named * squares[:, None], axis=0)

    cotangent = (2.0 * loss_scale * live[:, None] * residue).astype(BF16)
    back_part = lax.dot_general(
        cotangent, proj_weight, (((1,), (1,)), ((), ())), preferred_element_type=F32
    )
    side = jnp.concatenate(halves(loss_part) + (jnp.zeros((64,), BF16),))
    back_sum = sum_rows(back_part, side)
    out_grad = all_rows(back_sum[:, :2048].astype(BF16))
    losses = back_sum[0, 2048:2080] + back_sum[0, 2080:2112]
    hidden_grad = jnp.dot(out_grad, down_weight, preferred_element_type=F32)
    gate_sig = jax.nn.sigmoid(preact)
    pre_grad = (hidden_grad * gate_sig * (1.0 + preact * (1.0 - gate_sig))).astype(BF16)
    down_term = lax.dot_general(
        out_grad, hidden, (((0,), (0,)), ((), ())), preferred_element_type=F32
    )
    up_term = lax.dot_general(
        normed, pre_grad, (((0,), (0,)), ((), ())), preferred_element_type=F32
    )
    terms = jnp.concatenate([up_term, down_term], axis=1).astype(BF16)
    terms = terms.reshape(4, 4, 2, 64, 352)
    losses = losses.reshape(4, 4, 2)
    mine, other = (
        packed(
            jnp.where(core == which, terms[:, :, 0], terms[:, :, 1]),
            jnp.where(core == which, losses[:, :, 0], losses[:, :, 1]),
        )
        for which in (0, 1)
    )
    pair = mine.astype(F32) + lax.ppermute(other, "dp", CORES).astype(F32)
    pair = packed(*unpacked(pair)).transpose(1, 0, 2, 3)
    near = jnp.sum(swap_all(pair, "dp", NEAR).astype(F32), axis=0)
    total = jnp.sum(swap_all(packed(*unpacked(near)), "dp", FAR).astype(F32), axis=0)
    total, loss = unpacked(total)
    return (jnp.reshape(loss * loss_scale, (1,)), total[:, :176], total[:, 176:])


def solution(mesh):
    return jax.shard_map(
        on_device,
        mesh=mesh,
        in_specs=(
            P("dp", "tensor"),
            P("dp", "tensor"),
            P("tensor", "dp"),
            P("dp", None),
            P(),
            P("dp", None),
            P(None, "tensor"),
            P(None, "tensor"),
            P(None, "tensor"),
        ),
        out_specs=(P("dp"), P("dp", "tensor"), P("dp", "tensor")),
        check_vma=False,
    )
```

time: 596 us -> 240 us (0.40)
  waiting for transfers between devices: 424 us -> 44.9 us
  starting transfers between devices: 38.1 us -> 58.5 us
  between operations: 17.8 us -> 4.17 us
  local copies, waits for them, and re-layouts: 4.95 us -> 17.9 us
  matrix products: 22 us -> 12.6 us
  other arithmetic: 5.79 us -> 12.4 us
    reduce_scatter x2 -> x0, waiting for transfers between devices: 224 us -> none  [the longest x1 113 us: on_device(): lax.psum_scatter(up_term, 'dp', scatter_dimension=0, tiled=True)]
    all_gather x1 -> x0, waiting for transfers between devices: 98.7 us -> none  [on_device(): lax.all_gather(out_weight, 'dp', axis=1, tiled=True)]
    psum x1 -> x0, blocking collectives: 80 us -> none  [on_device(): back_sum, squares = lax.psum((back_part, squares_part), 'tensor')]
    psum x1 -> x0, waiting for transfers between devices: 55.9 us -> none  [on_device(): mixed = lax.psum(mixed_part, 'tensor')]
    all_to_all x0 -> x2, blocking collectives: none -> 43.5 us  [swap_all(): lax.all_to_all(x, axis, split_axis=0, concat_axis=0, tiled=True, axis_ind...]
    all_gather x0 -> x2, blocking collectives: none -> 41.7 us  [the longest x1 23.8 us: on_device(): lax.all_gather(context, 'dp', axis_index_groups=FAR).reshape(512, 256)]
    ppermute x0 -> x3, starting transfers between devices: none -> 16.9 us  [the longest x1 7.4 us: on_device(): cols4_other = lax.ppermute(cols4, 'dp', CORES)]
    reshape x1 -> x2, local copies, waits for them, and re-layouts: 1.56 us -> 8.22 us  [on_device(): head.astype(BF16).reshape(4, 128, 4, 512).transpose(0, 2, 1, 3)]
  transfers between devices with their start and end apart: 8 -> 8, of which waited for: 6 -> 5; matrix products, arithmetic and copies ran while one was open for 4% -> 9% of each run, Pallas kernels for 0% -> 0%
where the time goes in v1:
time: 240 us; the launch traced here: 236 us
  blocking collectives  85.2 us (36%)
  starting transfers between devices  58.5 us (24%)
  waiting for transfers between devices  44.9 us (19%)
  local copies, waits for them, and re-layouts  17.9 us (7%)
  matrix products  12.6 us (5%)
  other arithmetic  12.4 us (5%)
  between operations  4.17 us (2%)
    all_to_all x5, waiting for transfers between devices, swap_all(): lax.all_to_all(x, axis, split_axis=0, concat_axis=0, tiled=True, axis_ind...  43.6 us
    all_to_all x2, blocking collectives, swap_all(): lax.all_to_all(x, axis, split_axis=0, concat_axis=0, tiled=True, axis_ind...  43.5 us
    all_to_all x5, starting transfers between devices, swap_all(): lax.all_to_all(x, axis, split_axis=0, concat_axis=0, tiled=True, axis_ind...  41.6 us
    all_gather x1, blocking collectives, on_device(): lax.all_gather(context, 'dp', axis_index_groups=FAR).reshape(512, 256)  23.8 us
    all_gather x1, blocking collectives, on_device(): cols4 = lax.all_gather(out_weight, 'dp', axis_index_groups=NEAR)  18 us
    reshape x2, local copies, waits for them, and re-layouts, on_device(): head.astype(BF16).reshape(4, 128, 4, 512).transpose(0, 2, 1, 3)  8.22 us
    ppermute x1, starting transfers between devices, on_device(): cols4_other = lax.ppermute(cols4, 'dp', CORES)  7.4 us
    ppermute x1, starting transfers between devices, on_device(): pair = mine.astype(F32) + lax.ppermute(other, 'dp', CORES).astype(F32)  7.37 us
  transfers between devices with their start and end apart: 8, of which 5 were waited for; matrix products, arithmetic and copies ran while one was open for 9% of the time, Pallas kernels for 0%

profile of v1, /device:TPU:1, one launch (start us, length us, event | category | flops | bytes accessed | tf_op | source)
XLA Modules:
  0.0 235.6 jit_solution(16958982075264239589)
XLA Ops:
  0.6 0.0 copy-start
  0.7 18.0 %all-gather = bf16[1024,256]{1,0:T(8,128)(2,1)} all-gather(bf16[256,256]{1,0:T(8,128)(2,1)} %param.11), channel_id=2, replica_groups={{0,32,64,96},{16,48,80,112},{128,160,192,224},{144,176,208,240},{256,28..., dimensions={0}, use_global_device_ids=true | all-gather | bytes 655360 | tf_op jit(solution)/shard_map/all_gather | solution.py:82
  18.6 2.1 copy.53
  20.7 7.4 %collective-permute-start = (bf16[4,256,256]{1,2,0:T(8,128)(2,1)}, bf16[4,256,256]{1,2,0:T(8,128)(2,1)}, u32[]{:S(2)}, u32[]{:S(2)}) collective-permute-start(bf16[4,256,256]{1,2,0:T(8,128)(2,1)} %copy.53), channel_id=1, source_target_pairs={{0,16},{16,0},{32,48},{48,32},{64,80},{80,64},{96,112},{112,96},{1... | collective-permute-start | bytes 1572872 | tf_op jit(solution)/shard_map/ppermute | solution.py:83
  28.2 0.2 fusion.4
  28.4 1.6 fusion.17
  30.0 1.2 fusion
  31.1 4.2 %all-to-all-start = ((bf16[16,8,2048]{2,1,0:T(8,128)(2,1)}), bf16[16,8,2048]{2,1,0:T(8,128)(2,1)}, u32[]{:S(2)}, u32[]{:S(2)}) async-start(bf16[16,8,2048]{2,1,0:T(8,128)(2,1)} %fusion), calls=%async_computation | async-start | bytes 1048576 | tf_op jit(solution)/shard_map/all_to_all | solution.py:30
  35.4 23.8 %all-gather.1 = bf16[512,256]{1,0:T(8,128)(2,1)S(1)} all-gather(bf16[128,256]{1,0:T(8,128)(2,1)S(1)} %copy-done.4), channel_id=3, replica_groups={{0,128,256,384},{16,144,272,400},{32,160,288,416},{48,176,304,432},{64,..., dimensions={0}, use_global_device_ids=true | all-gather | bytes 327680 | tf_op jit(solution)/shard_map/all_gather | solution.py:81
  59.2 1.3 select_bitcast_fusion.2
  60.4 2.0 convert_bitcast_fusion
  62.5 4.0 %reshape.187 = bf16[4,128,4,512]{1,0,3,2:T(4,128)(2,1)} reshape(bf16[512,4,2,256]{0,3,2,1:T(8,128)(2,1)} %convert_bitcast_fusion) | data formatting | bytes 4194304 | tf_op jit(solution)/shard_map/reshape | solution.py:88
  66.5 4.3 %copy.56 = bf16[4,128,4,512]{3,1,2,0:T(8,128)(2,1)} copy(bf16[4,128,4,512]{1,0,3,2:T(4,128)(2,1)} %reshape.187) | data formatting | bytes 4194304 | tf_op jit(solution)/shard_map/reshape | solution.py:88
  70.7 6.1 %all-to-all-start.2 = ((bf16[16,128,512]{2,1,0:T(8,128)(2,1)}), bf16[16,128,512]{2,1,0:T(8,128)(2,1)}, u32[]{:S(2)}, u32[]{:S(2)}) async-start(bf16[16,128,512]{2,1,0:T(8,128)(2,1)} %bitcast.69), calls=%async_computation.2 | async-start | bytes 4194304 | tf_op jit(solution)/shard_map/all_to_all | solution.py:30
  76.9 1.1 convert_reduce_fusion.2
  78.0 24.1 %all-to-all-done.2 = bf16[16,128,512]{2,1,0:T(8,128)(2,1)} async-done(((bf16[16,128,512]{2,1,0:T(8,128)(2,1)}), bf16[16,128,512]{2,1,0:T(8,128)(2,1)}, u32[]{:S(2)}, u32[]{:S(2)}) %all-to-all-start.2) | async-done | bytes 2097184 | tf_op jit(solution)/shard_map/all_to_all | solution.py:30
  102.2 0.9 broadcast_in_dim.151
  103.0 6.8 %all-to-all-start.1 = ((bf16[16,8,2048]{2,1,0:T(8,128)(2,1)}), bf16[16,8,2048]{2,1,0:T(8,128)(2,1)}, u32[]{:S(2)}, u32[]{:S(2)}) async-start(bf16[16,8,2048]{2,1,0:T(8,128)(2,1)} %broadcast_in_dim.151), calls=%async_computation.1 | async-start | bytes 1048576 | tf_op jit(solution)/shard_map/all_to_all | solution.py:30
  109.8 2.6 %reduce_sum.87 = bf16[128,512]{1,0:T(8,128)(2,1)} reduce(bf16[16,128,512]{2,1,0:T(8,128)(2,1)} %all-to-all-done.2, bf16[]{:T(256)} %constant.58.clone.1), dimensions={0}, to_apply=%region_3.4 | reduce | flops 983040 | bytes 2228226 | tf_op jit(solution)/shard_map/reduce_sum | solution.py:89
  112.4 2.1 collective-permute-start.1
  114.6 0.6 reduce_sum.85
  115.2 0.6 dynamic_slice.7
  116.5 0.7 compare_select_fusion.1
  117.1 0.0 copy-start.6
  117.1 1.7 all-to-all-done.1
  118.9 1.7 multiply_reduce_fusion
  120.6 0.7 compare_select_fusion
  121.2 0.1 select_reduce_fusion
  121.4 0.1 pad_maximum_fusion.4
  121.4 1.7 fusion.1
  123.2 0.9 pad_maximum_fusion.2
  124.1 20.2 %all-to-all-start.3 = ((bf16[16,8,2176]{2,1,0:T(8,128)(2,1)}), bf16[16,8,2176]{2,1,0:T(8,128)(2,1)}, u32[]{:S(2)}, u32[]{:S(2)}) async-start(bf16[16,8,2176]{2,1,0:T(8,128)(2,1)} %pad_maximum_fusion.2), calls=%async_computation.3 | async-start | bytes 1114112 | tf_op jit(solution)/shard_map/all_to_all | solution.py:30
  144.3 9.2 %all-to-all-done.3 = bf16[16,8,2176]{2,1,0:T(8,128)(2,1)} async-done(((bf16[16,8,2176]{2,1,0:T(8,128)(2,1)}), bf16[16,8,2176]{2,1,0:T(8,128)(2,1)}, u32[]{:S(2)}, u32[]{:S(2)}) %all-to-all-start.3) | async-done | bytes 557088 | tf_op jit(solution)/shard_map/all_to_all | solution.py:30
  153.4 1.1 convert_reduce_fusion.1
  154.6 0.1 fusion.34
  154.7 0.8 broadcast_in_dim.154
  155.5 4.2 %all-to-all-start.4 = ((bf16[16,8,2048]{2,1,0:T(8,128)(2,1)}), bf16[16,8,2048]{2,1,0:T(8,128)(2,1)}, u32[]{:S(2)}, u32[]{:S(2)}) async-start(bf16[16,8,2048]{2,1,0:T(8,128)(2,1)} %broadcast_in_dim.154), calls=%async_computation.4 | async-start | bytes 1048576 | tf_op jit(solution)/shard_map/all_to_all | solution.py:30
  159.7 0.1 add.72
  159.8 0.2 select_reduce_fusion.2
  160.0 0.1 select_select_fusion.2
  160.1 8.6 %all-to-all-done.4 = bf16[16,8,2048]{2,1,0:T(8,128)(2,1)} async-done(((bf16[16,8,2048]{2,1,0:T(8,128)(2,1)}), bf16[16,8,2048]{2,1,0:T(8,128)(2,1)}, u32[]{:S(2)}, u32[]{:S(2)}) %all-to-all-start.4) | async-done | bytes 524320 | tf_op jit(solution)/shard_map/all_to_all | solution.py:30
  168.7 2.9 %convolution_convert_fusion = bf16[2048,176]{0,1:T(8,128)(2,1)} fusion(bf16[2048,176]{0,1:T(8,128)(2,1)S(1)} %copy-done.2, bf16[16,8,2048]{2,1,0:T(8,128)(2,1)} %all-to-all-done.4, bf16[128,2048]{1,0:T(8,128)(2,1)S(1)} %copy-done.1, f32[128]{0:T(128)S(1)} %add_rsqrt_fusion, f32[128,176]{0,1:T(8,128)S(1)} %fusion.17), kind=kOutput, calls=%fused_computation | convolution fusion | flops 185899008 | bytes 2580992 | tf_op jit(solution)/shard_map/dot_general | solution.py:129
  171.6 1.4 copy.57
  173.0 2.0 copy.58
  175.1 1.5 convolution_convert_fusion.3
  176.6 0.6 select_bitcast_fusion
  177.2 0.2 pad_maximum_fusion.1
  177.4 7.4 %collective-permute-start.2 = (bf16[4,4,64,384]{3,2,1,0:T(8,128)(2,1)S(1)}, bf16[4,4,64,384]{3,2,1,0:T(8,128)(2,1)S(1)}, u32[]{:S(2)}, u32[]{:S(2)}) collective-permute-start(bf16[4,4,64,384]{3,2,1,0:T(8,128)(2,1)S(1)} %pad_maximum_fusion.1), channel_id=1, source_target_pairs={{0,16},{16,0},{32,48},{48,32},{64,80},{80,64},{96,112},{112,96},{1... | collective-permute-start | bytes 2359304 | tf_op jit(solution)/shard_map/ppermute | solution.py:142
  184.8 0.6 fusion.10
  185.4 1.3 collective-permute-done.2
  186.7 0.3 convert_add_fusion
  187.0 0.1 slice.124
  187.1 0.2 fusion.25
  187.4 0.1 select_select_fusion
  187.5 0.2 maximum_bitcast_fusion
  187.7 0.1 copy.62
  187.8 25.5 %all_to_all.35 = bf16[4,4,64,384]{3,2,1,0:T(8,128)(2,1)S(1)} all-to-all(bf16[4,4,64,384]{3,2,1,0:T(8,128)(2,1)S(1)} %copy.62), channel_id=1, replica_groups={{0,32,64,96},{16,48,80,112},{128,160,192,224},{144,176,208,240},{256,28..., dimensions={0} | all-to-all | bytes 1572864 | tf_op jit(solution)/shard_map/all_to_all | solution.py:30
  213.3 0.1 convert_reduce_fusion
  213.4 0.2 fusion.32
  213.6 0.1 select_select_fusion.3
  213.7 0.1 pad_maximum_fusion.3
  213.8 18.0 %all_to_all.36 = bf16[4,64,384]{2,1,0:T(8,128)(2,1)S(1)} all-to-all(bf16[4,64,384]{2,1,0:T(8,128)(2,1)S(1)} %pad_maximum_fusion.3), channel_id=1, replica_groups={{0,128,256,384},{16,144,272,400},{32,160,288,416},{48,176,304,432},{64,..., dimensions={0} | all-to-all | bytes 393216 | tf_op jit(solution)/shard_map/all_to_all | solution.py:30
  231.8 0.7 fusion.37
  232.5 0.7 fusion.38
  (28 shorter events, 0.3 us)
Async XLA Ops:
  0.6 118.2 %copy-start = (bf16[2048,512]{1,0:T(8,128)(2,1)S(1)}, bf16[2048,512]{1,0:T(8,128)(2,1)}, u32[]{:S(2)}) copy-start(bf16[2048,512]{1,0:T(8,128)(2,1)} %param.17) | copy-start | bytes 6291460
  0.6 27.5 %copy-start.1 = (bf16[128,2048]{1,0:T(8,128)(2,1)S(1)}, bf16[128,2048]{1,0:T(8,128)(2,1)}, u32[]{:S(2)}) copy-start(bf16[128,2048]{1,0:T(8,128)(2,1)} %param.14) | copy-start | bytes 1572868
  18.6 11.3 %copy-start.2 = (bf16[2048,176]{0,1:T(8,128)(2,1)S(1)}, bf16[2048,176]{0,1:T(8,128)(2,1)}, u32[]{:S(2)}) copy-start(bf16[2048,176]{0,1:T(8,128)(2,1)} %param.16) | copy-start | bytes 2162692
  20.7 38.4 %collective-permute-start = (bf16[4,256,256]{1,2,0:T(8,128)(2,1)}, bf16[4,256,256]{1,2,0:T(8,128)(2,1)}, u32[]{:S(2)}, u32[]{:S(2)}) collective-permute-start(bf16[4,256,256]{1,2,0:T(8,128)(2,1)} %copy.53), channel_id=1, source_target_pairs={{0,16},{16,0},{32,48},{48,32},{64,80},{80,64},{96,112},{112,96},{1... | collective-permute-start | bytes 1572872 | tf_op jit(solution)/shard_map/ppermute | solution.py:83
  28.4 7.0 %copy-start.4 = (bf16[128,256]{1,0:T(8,128)(2,1)S(1)}, bf16[128,256]{1,0:T(8,128)(2,1)}, u32[]{:S(2)}) copy-start(bf16[128,256]{1,0:T(8,128)(2,1)} %param.10) | copy-start | bytes 196612
  31.1 39.6 %all-to-all-start = ((bf16[16,8,2048]{2,1,0:T(8,128)(2,1)}), bf16[16,8,2048]{2,1,0:T(8,128)(2,1)}, u32[]{:S(2)}, u32[]{:S(2)}) async-start(bf16[16,8,2048]{2,1,0:T(8,128)(2,1)} %fusion), calls=%async_computation | async-start | bytes 1048576 | tf_op jit(solution)/shard_map/all_to_all | solution.py:30
  70.7 31.4 %all-to-all-start.2 = ((bf16[16,128,512]{2,1,0:T(8,128)(2,1)}), bf16[16,128,512]{2,1,0:T(8,128)(2,1)}, u32[]{:S(2)}, u32[]{:S(2)}) async-start(bf16[16,128,512]{2,1,0:T(8,128)(2,1)} %bitcast.69), calls=%async_computation.2 | async-start | bytes 4194304 | tf_op jit(solution)/shard_map/all_to_all | solution.py:30
  103.0 11.5 %copy-start.5 = (s32[32]{0:T(128)S(1)}, s32[32]{0:T(128)}, u32[]{:S(2)}) copy-start(s32[32]{0:T(128)} %param.13) | copy-start | bytes 388
  103.0 15.8 %all-to-all-start.1 = ((bf16[16,8,2048]{2,1,0:T(8,128)(2,1)}), bf16[16,8,2048]{2,1,0:T(8,128)(2,1)}, u32[]{:S(2)}, u32[]{:S(2)}) async-start(bf16[16,8,2048]{2,1,0:T(8,128)(2,1)} %broadcast_in_dim.151), calls=%async_computation.1 | async-start | bytes 1048576 | tf_op jit(solution)/shard_map/all_to_all | solution.py:30
  112.4 6.4 %collective-permute-start.1 = (bf16[128,512]{1,0:T(8,128)(2,1)}, bf16[128,512]{1,0:T(8,128)(2,1)}, u32[]{:S(2)}, u32[]{:S(2)}) collective-permute-start(bf16[128,512]{1,0:T(8,128)(2,1)} %reduce_sum.87), channel_id=1, source_target_pairs={{0,0},{1,1},{2,2},{3,3},{4,128},{5,129},{6,130},{7,131},{8,256},{9... | collective-permute-start | bytes 393224 | tf_op jit(solution)/shard_map/ppermute | solution.py:90
  117.1 4.1 %copy-start.6 = (s32[128,1]{0,1:T(1,128)S(1)}, s32[128,1]{0,1:T(1,128)}, u32[]{:S(2)}) copy-start(s32[128,1]{0,1:T(1,128)} %param.12) | copy-start | bytes 1540
  118.8 2.6 %copy-start.3 = (bf16[128,512]{1,0:T(8,128)(2,1)S(1)}, bf16[128,512]{1,0:T(8,128)(2,1)}, u32[]{:S(2)}) copy-start(bf16[128,512]{1,0:T(8,128)(2,1)} %param.9) | copy-start | bytes 393220
  124.1 29.4 %all-to-all-start.3 = ((bf16[16,8,2176]{2,1,0:T(8,128)(2,1)}), bf16[16,8,2176]{2,1,0:T(8,128)(2,1)}, u32[]{:S(2)}, u32[]{:S(2)}) async-start(bf16[16,8,2176]{2,1,0:T(8,128)(2,1)} %pad_maximum_fusion.2), calls=%async_computation.3 | async-start | bytes 1114112 | tf_op jit(solution)/shard_map/all_to_all | solution.py:30
  155.5 13.2 %all-to-all-start.4 = ((bf16[16,8,2048]{2,1,0:T(8,128)(2,1)}), bf16[16,8,2048]{2,1,0:T(8,128)(2,1)}, u32[]{:S(2)}, u32[]{:S(2)}) async-start(bf16[16,8,2048]{2,1,0:T(8,128)(2,1)} %broadcast_in_dim.154), calls=%async_computation.4 | async-start | bytes 1048576 | tf_op jit(solution)/shard_map/all_to_all | solution.py:30
  177.4 9.3 %collective-permute-start.2 = (bf16[4,4,64,384]{3,2,1,0:T(8,128)(2,1)S(1)}, bf16[4,4,64,384]{3,2,1,0:T(8,128)(2,1)S(1)}, u32[]{:S(2)}, u32[]{:S(2)}) collective-permute-start(bf16[4,4,64,384]{3,2,1,0:T(8,128)(2,1)S(1)} %pad_maximum_fusion.1), channel_id=1, source_target_pairs={{0,16},{16,0},{32,48},{48,32},{64,80},{80,64},{96,112},{112,96},{1... | collective-permute-start | bytes 2359304 | tf_op jit(solution)/shard_map/ppermute | solution.py:142

commit v2 on v1

v2 whole, which is shorter than its diff:
```python
import jax
import jax.numpy as jnp
from jax import lax
from jax.experimental import pallas as pl
from jax.experimental.pallas import tpu as pltpu
from jax.sharding import PartitionSpec as P

D = 8192
F32 = jnp.float32
BF16 = jnp.bfloat16

PLACES = [(zh, zl, c) for zh in range(4) for zl in range(4) for c in range(2)]
CORES = [(d, d ^ 1) for d in range(32)]
FAR = [[8 * h + 2 * l + c for h in range(4)] for l in range(4) for c in range(2)]
def index(zh, zl, c):
    return 8 * zh + 2 * zl + c


def near_step(k):
    return [(index(zh, zl, c), index(zh, zl ^ k, c)) for zh, zl, c in PLACES]


def ring_step(k):
    return [(d, (d + (2 - 4 * (d % 2)) * k) % 32) for d in range(32)]


FAR_STEP = [(index(zh, zl, c), index((zh - 1 + 2 * c) % 4, zl, c)) for zh, zl, c in PLACES]


HOME = [
    (index(zh, zl, c) * 16 + 4 * x + y, index(zh, y, c) * 16 + 4 * x + zl)
    for zh, zl, c in PLACES
    for x in range(4)
    for y in range(4)
]


def swap_all(x, axis, groups=None):
    return lax.all_to_all(x, axis, split_axis=0, concat_axis=0, tiled=True, axis_index_groups=groups)


def call(body, name, flops, out_shape, scalars, *arrays):
    vmem = pl.BlockSpec(memory_space=pltpu.VMEM)
    smem = pl.BlockSpec(memory_space=pltpu.SMEM)
    return pl.pallas_call(
        body,
        out_shape=out_shape,
        in_specs=[smem] * len(scalars) + [vmem] * len(arrays),
        out_specs=jax.tree.map(lambda _: vmem, out_shape),
        compiler_params=pltpu.CompilerParams(vmem_limit_bytes=32 << 20),
        cost_estimate=pl.CostEstimate(flops=flops, bytes_accessed=2 << 20, transcendentals=0),
        name=name,
    )(*scalars, *arrays)


def halves(x):
    high = x.astype(BF16).astype(F32)
    return high, x - high


def forward_body(rows, up, down, normed, preact, hidden, pieces):
    x = rows[...].astype(F32)
    mean = jnp.mean(x * x, axis=-1, keepdims=True)
    normed[...] = (x * lax.rsqrt(mean + 1e-05)).astype(BF16)
    pre = lax.dot_general(normed[...], up[...], (((1,), (1,)), ((), ())), preferred_element_type=F32)
    preact[...] = pre
    units = (pre * jax.nn.sigmoid(pre)).astype(BF16)
    hidden[...] = units
    for pair in range(8):
        columns = slice(pair * 256, pair * 256 + 256)
        part = jnp.dot(units, down[:, columns], preferred_element_type=F32).astype(BF16)
        pieces[2 * pair] = part[:, :128]
        pieces[2 * pair + 1] = part[:, 128:]


def head_body(
    place_ref, student, mixed, own, near1, near2, near3, mine, pair, far, half, got, out
):
    zh, zl, core, tensor = place_ref[0], place_ref[1], place_ref[2], place_ref[4]
    mixed_sum = mixed[0].astype(F32)
    for t in range(1, 16):
        mixed_sum += mixed[t].astype(F32)
    block = student[:, pl.ds(pl.multiple_of(tensor * 128, 128), 128)].astype(F32)
    updated = (block + mixed_sum).astype(BF16)
    rows = jnp.concatenate([own[...], near1[...], near2[...], near3[...]], axis=0)

    def in_order(of_core, of_other):
        return jnp.where(core == 0, of_core, of_other), jnp.where(core == 0, of_other, of_core)

    def opposite(column_core):
        held = jnp.where(core == column_core, half[0], half[1])
        other = jnp.where(core == column_core, got[1, 256:], got[0, 256:])
        return jnp.concatenate(in_order(held, other), axis=0)

    side_step = jnp.where(core == 0, 1, 3)
    for step, sides in (
        (0, in_order(mine[...], pair[...])),
        (side_step, in_order(far[0], far[1])),
        (4 - side_step, in_order(got[1, :256], got[0, :256])),
        (2, (opposite(0), opposite(1))),
    ):
        for side, columns in enumerate(sides):
            part = jnp.dot(rows, columns, preferred_element_type=F32).astype(BF16)
            for near in range(4):
                piece = (zh + step) % 4 * 4 + (zl ^ near)
                out[piece, :, side * 256 : side * 256 + 256] = part[near * 128 : near * 128 + 128]
    for t in range(16):
        out[t, :, 512:] = updated


def head_sum_body(got, head, updated):
    total = got[0, :, :512].astype(F32)
    for t in range(1, 16):
        total += got[t, :, :512].astype(F32)
    head[...] = total.astype(BF16)
    for t in range(16):
        updated[:, t * 128 : t * 128 + 128] = got[t, :, 512:]


def project_body(updated, proj, out):
    out[...] = jnp.dot(updated[...], proj[...], preferred_element_type=F32)


def residue_body(scale_ref, length_ref, owners, projected, resid, head, proj, pieces):
    scale, length = scale_ref[0], length_ref[0]
    target = (resid[...].astype(F32) + head[...].astype(F32)).astype(BF16)
    residue = projected[...] - target.astype(F32)
    row = lax.broadcasted_iota(jnp.int32, (128, 1), 0)
    live = (row < length).astype(F32)
    squares = live * jnp.sum(residue * residue, axis=-1, keepdims=True)
    owner = lax.broadcasted_iota(jnp.int32, (128, 128), 1)
    losses = jnp.sum(jnp.where(owners[...] == owner, squares, 0.0), axis=0, keepdims=True)
    high, low = halves(losses)
    side_row = lax.broadcasted_iota(jnp.int32, (16, 128), 0)
    side = jnp.where(side_row == 0, high, jnp.where(side_row == 1, low, 0.0)).astype(BF16)
    cotangent = (2.0 * scale * live * residue).astype(BF16)
    for pair in range(8):
        part = lax.dot_general(
            cotangent,
            proj[pair * 256 : pair * 256 + 256],
            (((1,), (1,)), ((), ())),
            preferred_element_type=F32,
        ).astype(BF16)
        pieces[2 * pair, :128] = part[:, :128]
        pieces[2 * pair + 1, :128] = part[:, 128:]
    for t in range(16):
        pieces[t, 128:] = side


def back_sum_body(got, out, losses):
    total = got[0].astype(F32)
    for t in range(1, 16):
        total += got[t].astype(F32)
    block = total[:128].astype(BF16)
    for t in range(16):
        out[t] = block
    losses[...] = total[128:129] + total[129:130]


def grad_body(place_ref, losses, blocks, hidden, preact, normed, down, mine, other):
    zl, core, source = place_ref[1], place_ref[2], place_ref[3]
    out_grad = jnp.concatenate([blocks[t] for t in range(16)], axis=1)
    hidden_grad = lax.dot_general(
        out_grad, down[...], (((1,), (1,)), ((), ())), preferred_element_type=F32
    )
    pre = preact[...]
    gate_sig = jax.nn.sigmoid(pre)
    pre_grad = hidden_grad * gate_sig * (1.0 + pre * (1.0 - gate_sig))
    up_left = pre_grad.T.astype(BF16)
    down_left = hidden[...].astype(F32).T.astype(BF16)
    lane = lax.broadcasted_iota(jnp.int32, (176, 128), 1)
    loss_lane = lax.broadcasted_iota(jnp.int32, (1, 128), 1)
    side_lane = lax.broadcasted_iota(jnp.int32, (16, 128), 1)
    for pair in range(8):
        columns = slice(pair * 256, pair * 256 + 256)
        up_pair = jnp.dot(up_left, normed[:, columns], preferred_element_type=F32)
        down_pair = jnp.dot(down_left, out_grad[:, columns], preferred_element_type=F32)
        for half in range(2):
            chip = 2 * pair + half
            ahead = (chip % 4 - zl + 4) % 4
            back = (4 - ahead) % 4
            own_piece = jnp.where(core == 0, ahead, back) * 4 + chip // 4
            other_piece = jnp.where(core == 0, back, ahead) * 4 + chip // 4
            up = up_pair[:, half * 128 : half * 128 + 128]
            below = down_pair[:, half * 128 : half * 128 + 128]
            even = jnp.where(lane < 64, up, pltpu.roll(below, 64, 1))
            odd = jnp.where(lane < 64, pltpu.roll(up, 64, 1), below)
            mine[own_piece, :176] = jnp.where(core == 0, even, odd).astype(BF16)
            other[other_piece, :176] = jnp.where(core == 0, odd, even).astype(BF16)
            for out, piece, owner in (
                (mine, own_piece, 2 * chip + core),
                (other, other_piece, 2 * chip + 1 - core),
            ):
                loss = jnp.where(loss_lane == owner, losses[...], 0.0)
                high, low = halves(jnp.sum(loss, axis=1, keepdims=True))
                side = jnp.where(
                    side_lane == 2 * source, high, jnp.where(side_lane == 2 * source + 1, low, 0.0)
                )
                out[piece, 176:] = side.astype(BF16)


def finish_body(scale_ref, got, loss, up, down):
    total = got[0].astype(F32)
    for zh in range(1, 4):
        total += got[zh].astype(F32)
    sums = jnp.sum(total[176:177], axis=1, keepdims=True)
    loss[...] = sums * scale_ref[0]
    grads = total[:176].T
    up[...] = grads[:64]
    down[...] = grads[64:]


def on_device(
    resid,
    context,
    out_weight,
    owners,
    query_lengths,
    student_rows,
    up_weight,
    down_weight,
    proj_weight,
):
    shape = jax.ShapeDtypeStruct
    dp = lax.axis_index("dp")
    place = jnp.stack([dp // 8, dp // 2 % 4, dp % 2, dp, lax.axis_index("tensor")]).astype(jnp.int32)
    loss_scale = 32.0 / (jnp.sum(query_lengths).astype(F32) * D)
    own_length = lax.dynamic_slice_in_dim(query_lengths, dp, 1)

    rows = [context] + [lax.ppermute(context, "dp", near_step(k)) for k in (1, 2, 3)]
    pair = lax.ppermute(out_weight, "dp", CORES)
    far = lax.ppermute(jnp.stack([out_weight, pair]), "dp", FAR_STEP)

    normed, preact, hidden, mixed = call(
        forward_body,
        "forward",
        4 * 128 * 2048 * 176,
        (
            shape((128, 2048), BF16),
            shape((128, 176), F32),
            shape((128, 176), BF16),
            shape((16, 128, 128), BF16),
        ),
        (),
        student_rows,
        up_weight.T,
        down_weight.T,
    )
    rows, far, mixed = lax.optimization_barrier((rows, far, mixed))
    half = lax.dynamic_slice_in_dim(far, dp % 2 * 128, 128, axis=1)
    half = lax.ppermute(half, "dp", FAR_STEP)
    mixed = swap_all(mixed, "tensor")
    half, mixed = lax.optimization_barrier((half, mixed))
    got = lax.ppermute(jnp.concatenate([far, half], axis=1), "dp", CORES)
    parts = call(
        head_body,
        "head_parts",
        2 * 512 * 2048 * 256,
        shape((16, 128, 640), BF16),
        (place,),
        student_rows,
        mixed,
        *rows,
        out_weight,
        pair,
        far,
        half,
        got,
    )
    head, updated = call(
        head_sum_body,
        "head_sum",
        16 * 128 * 512,
        (shape((128, 512), BF16), shape((128, 2048), BF16)),
        (),
        swap_all(parts, "tensor"),
    )
    head = lax.ppermute(head, ("dp", "tensor"), HOME)
    projected = call(
        project_body, "project", 2 * 128 * 2048 * 512, shape((128, 512), F32), (), updated, proj_weight
    )
    pieces = call(
        residue_body,
        "residue",
        2 * 128 * 2048 * 512,
        shape((16, 144, 128), BF16),
        (jnp.reshape(loss_scale, (1,)), own_length),
        owners,
        projected,
        resid,
        head,
        proj_weight,
    )
    blocks, losses = call(
        back_sum_body,
        "back_sum",
        16 * 128 * 128,
        (shape((16, 128, 128), BF16), shape((1, 128), F32)),
        (),
        swap_all(pieces, "tensor"),
    )
    mine, other = call(
        grad_body,
        "grad_terms",
        6 * 128 * 2048 * 176,
        (shape((16, 192, 128), BF16),) * 2,
        (place,),
        losses,
        swap_all(blocks, "tensor"),
        hidden,
        preact,
        normed,
        down_weight.T,
    )
    pair = (mine.astype(F32) + lax.ppermute(other, "dp", CORES).astype(F32)).astype(BF16)
    pair = pair.reshape(4, 4, 192, 128)
    near = pair[0].astype(F32)
    for k, step in ((1, 1), (3, -1), (2, 2)):
        near += lax.ppermute(pair[k], "dp", ring_step(step)).astype(F32)
    near = near.astype(BF16)
    grad = shape((64, 176), F32)
    loss, grad_up, grad_down = call(
        finish_body,
        "finish",
        4 * 192 * 128,
        (shape((1, 1), F32), grad, grad),
        (jnp.reshape(loss_scale, (1,)),),
        swap_all(near, "dp", FAR),
    )
    return (jnp.reshape(loss, (1,)), grad_up, grad_down)


def solution(mesh):
    return jax.shard_map(
        on_device,
        mesh=mesh,
        in_specs=(
            P("dp", "tensor"),
            P("dp", "tensor"),
            P("tensor", "dp"),
            P("dp", None),
            P(),
            P("dp", None),
            P(None, "tensor"),
            P(None, "tensor"),
            P(None, "tensor"),
        ),
        out_specs=(P("dp"), P("dp", "tensor"), P("dp", "tensor")),
        check_vma=False,
    )
```

time: 240 us -> 195 us (0.81)
  waiting for transfers between devices: 44.9 us -> 18.7 us
  local copies, waits for them, and re-layouts: 17.9 us -> 4.13 us
  matrix products: 12.6 us -> 0 us
  blocking collectives: 85.2 us -> 96.4 us
  other arithmetic: 12.4 us -> 1.96 us
  Pallas kernels: 0 us -> 9.84 us
  between operations: 4.17 us -> 1.63 us
    all_to_all x2 -> x4, blocking collectives: 43.5 us -> 96.4 us  [swap_all(): lax.all_to_all(x, axis, split_axis=0, concat_axis=0, tiled=True, axis_ind...]
    all_to_all x5 -> x1, waiting for transfers between devices: 43.6 us -> 0.01 us  [swap_all(): lax.all_to_all(x, axis, split_axis=0, concat_axis=0, tiled=True, axis_ind...]
    all_gather x2 -> x0, blocking collectives: 41.7 us -> none  [the longest x1 23.8 us: on_device(): lax.all_gather(context, 'dp', axis_index_groups=FAR).reshape(512, 256)]
    ppermute x3 -> x12, starting transfers between devices: 16.9 us -> 53.1 us  [the longest x3 10.4 us: on_device(): lax.ppermute(context, 'dp', near_step(k))]
    all_to_all x5 -> x1, starting transfers between devices: 41.6 us -> 5.95 us  [swap_all(): lax.all_to_all(x, axis, split_axis=0, concat_axis=0, tiled=True, axis_ind...]
    ppermute x3 -> x12, waiting for transfers between devices: 1.26 us -> 18.7 us  [the longest x3 6.73 us: on_device(): near += lax.ppermute(pair[k], 'dp', ring_step(step)).astype(F32)]
    dot_general x7 -> x0, matrix products: 12.6 us -> none  [the longest x1 2.87 us: on_device(): lax.dot_general(normed, pre_grad, (((0,), (0,)), ((), ())), preferred_ele...]
    pallas_call x0 -> x8, Pallas kernels: none -> 9.84 us  [call(): pl.pallas_call(body, out_shape=out_shape, in_specs=[smem] * len(scalars)...]
  transfers between devices with their start and end apart: 8 -> 13, of which waited for: 5 -> 7; matrix products, arithmetic and copies ran while one was open for 9% -> 1% of each run, Pallas kernels for 0% -> 1%
where the time goes in v2:
time: 195 us; the launch traced here: 192 us
  blocking collectives  96.4 us (49%)
  starting transfers between devices  59.1 us (30%)
  waiting for transfers between devices  18.7 us (10%)
  Pallas kernels  9.84 us (5%)
  local copies, waits for them, and re-layouts  4.13 us (2%)
  other arithmetic  1.96 us (1%)
    all_to_all x4, blocking collectives, swap_all(): lax.all_to_all(x, axis, split_axis=0, concat_axis=0, tiled=True, axis_ind...  96.4 us
    ppermute x3, starting transfers between devices, on_device(): lax.ppermute(context, 'dp', near_step(k))  10.4 us
    pallas_call x8, Pallas kernels, call(): pl.pallas_call(body, out_shape=out_shape, in_specs=[smem] * len(scalars)...  9.84 us
    ppermute x1, starting transfers between devices, on_device(): pair = lax.ppermute(out_weight, 'dp', CORES)  8.79 us
    ppermute x3, starting transfers between devices, on_device(): near += lax.ppermute(pair[k], 'dp', ring_step(step)).astype(F32)  8.41 us
    ppermute x1, starting transfers between devices, on_device(): half = lax.ppermute(half, 'dp', FAR_STEP)  7.77 us
    ppermute x1, starting transfers between devices, on_device(): got = lax.ppermute(jnp.concatenate([far, half], axis=1), 'dp', CORES)  6.8 us
    ppermute x3, waiting for transfers between devices, on_device(): near += lax.ppermute(pair[k], 'dp', ring_step(step)).astype(F32)  6.73 us
  transfers between devices with their start and end apart: 13, of which 7 were waited for; matrix products, arithmetic and copies ran while one was open for 1% of the time, Pallas kernels for 1%

profile of v2, /device:TPU:1, one launch (start us, length us, event | category | flops | bytes accessed | tf_op | source)
XLA Modules:
  0.0 191.7 jit_solution(16802466233525838572)
XLA Ops:
  0.6 8.8 %collective-permute-start.3 = (bf16[256,256]{1,0:T(8,128)(2,1)}, bf16[256,256]{1,0:T(8,128)(2,1)S(1)}, u32[]{:S(2)}, u32[]{:S(2)}) collective-permute-start(bf16[256,256]{1,0:T(8,128)(2,1)} %mine.1), channel_id=1, source_target_pairs={{0,16},{16,0},{32,48},{48,32},{64,80},{80,64},{96,112},{112,96},{1... | collective-permute-start | bytes 393224 | tf_op jit(solution)/shard_map/ppermute | solution.py:231
  9.4 1.2 collective-permute-done.3.pair
  10.6 0.0 copy-start.4
  10.6 1.0 pad_maximum_fusion.1
  11.6 3.4 %collective-permute-start.4 = (bf16[2,256,256]{2,1,0:T(8,128)(2,1)S(1)}, bf16[2,256,256]{2,1,0:T(8,128)(2,1)S(1)}, u32[]{:S(2)}, u32[]{:S(2)}) collective-permute-start(bf16[2,256,256]{2,1,0:T(8,128)(2,1)S(1)} %pad_maximum_fusion.1), channel_id=1, source_target_pairs={{0,384},{16,144},{32,416},{48,176},{64,448},{80,208},{96,480},{112... | collective-permute-start | bytes 786440 | tf_op jit(solution)/shard_map/ppermute | solution.py:232
  15.0 3.5 %collective-permute-start = (bf16[128,256]{1,0:T(8,128)(2,1)}, bf16[128,256]{1,0:T(8,128)(2,1)S(1)}, u32[]{:S(2)}, u32[]{:S(2)}) collective-permute-start(bf16[128,256]{1,0:T(8,128)(2,1)} %own), channel_id=1, source_target_pairs={{0,32},{16,48},{32,0},{48,16},{64,96},{80,112},{96,64},{112,80},{1... | collective-permute-start | bytes 196616 | tf_op jit(solution)/shard_map/ppermute | solution.py:230
  18.6 4.9 %collective-permute-start.1 = (bf16[128,256]{1,0:T(8,128)(2,1)}, bf16[128,256]{1,0:T(8,128)(2,1)S(1)}, u32[]{:S(2)}, u32[]{:S(2)}) collective-permute-start(bf16[128,256]{1,0:T(8,128)(2,1)} %own), channel_id=1, source_target_pairs={{0,64},{16,80},{32,96},{48,112},{64,0},{80,16},{96,32},{112,48},{1... | collective-permute-start | bytes 196616 | tf_op jit(solution)/shard_map/ppermute | solution.py:230
  23.5 1.9 %collective-permute-start.2 = (bf16[128,256]{1,0:T(8,128)(2,1)}, bf16[128,256]{1,0:T(8,128)(2,1)S(1)}, u32[]{:S(2)}, u32[]{:S(2)}) collective-permute-start(bf16[128,256]{1,0:T(8,128)(2,1)} %own), channel_id=1, source_target_pairs={{0,96},{16,112},{32,64},{48,80},{64,32},{80,48},{96,0},{112,16},{1... | collective-permute-start | bytes 196616 | tf_op jit(solution)/shard_map/ppermute | solution.py:230
  25.4 0.0 copy-start.1
  25.5 1.1 copy-done.1
  26.6 1.0 copy-done.3
  27.6 0.0 copy-start.5
  27.6 1.1 copy-done.5
  28.7 0.0 copy-start.6
  28.7 0.0 copy-start.8
  28.7 1.8 forward.1
  30.5 0.0 collective-permute-done.near1
  30.5 0.0 collective-permute-done.1.near2
  30.5 1.6 collective-permute-done.2.near3
  32.1 0.0 collective-permute-done.4.far
  32.1 6.0 %all-to-all-start = ((bf16[16,128,128]{2,1,0:T(8,128)(2,1)}), bf16[16,128,128]{2,1,0:T(8,128)(2,1)S(1)}, u32[]{:S(2)}, u32[]{:S(2)}) async-start(bf16[16,128,128]{2,1,0:T(8,128)(2,1)} %get-tuple-element.26), calls=%async_computation | async-start | bytes 1048576 | tf_op jit(solution)/shard_map/all_to_all | solution.py:39
  38.1 7.8 %collective-permute-start.5 = (bf16[2,128,256]{2,1,0:T(8,128)(2,1)S(1)}, bf16[2,128,256]{2,1,0:T(8,128)(2,1)S(1)}, u32[]{:S(2)}, u32[]{:S(2)}) collective-permute-start(bf16[2,128,256]{2,1,0:T(8,128)(2,1)S(1)} %constant_dynamic-slice_fusion), channel_id=1, source_target_pairs={{0,384},{16,144},{32,416},{48,176},{64,448},{80,208},{96,480},{112... | collective-permute-start | bytes 393224 | tf_op jit(solution)/shard_map/ppermute | solution.py:251
  45.9 6.1 %collective-permute-done.5.half = bf16[2,128,256]{2,1,0:T(8,128)(2,1)S(1)} collective-permute-done((bf16[2,128,256]{2,1,0:T(8,128)(2,1)S(1)}, bf16[2,128,256]{2,1,0:T(8,128)(2,1)S(1)}, u32[]{:S(2)}, u32[]{:S(2)}) %collective-permute-start.5) | collective-permute-done | bytes 131104 | tf_op jit(solution)/shard_map/ppermute | solution.py:251
  52.0 0.0 all-to-all-done.mixed
  52.0 6.8 %collective-permute-start.6 = (bf16[2,384,256]{2,1,0:T(8,128)(2,1)S(1)}, bf16[2,384,256]{2,1,0:T(8,128)(2,1)S(1)}, u32[]{:S(2)}, u32[]{:S(2)}) collective-permute-start(bf16[2,384,256]{2,1,0:T(8,128)(2,1)S(1)} %pad_maximum_fusion), channel_id=1, source_target_pairs={{0,16},{16,0},{32,48},{48,32},{64,80},{80,64},{96,112},{112,96},{1... | collective-permute-start | bytes 1179656 | tf_op jit(solution)/shard_map/ppermute | solution.py:254
  58.9 0.1 stack.32.place_ref
  59.0 1.2 collective-permute-done.6.got
  60.2 0.0 copy-done.4
  60.2 0.0 copy-done.6
  60.2 0.0 copy-done.8
  60.2 1.4 head_parts.1
  61.6 39.5 %all_to_all.25.got = bf16[16,128,640]{2,1,0:T(8,128)(2,1)S(1)} all-to-all(bf16[16,128,640]{2,1,0:T(8,128)(2,1)S(1)} %head_parts.1), channel_id=1, replica_groups=mesh['dp'=32,'tensor'=16] {'tensor'}, dimensions={0} | all-to-all | bytes 5242880 | tf_op jit(solution)/shard_map/all_to_all | solution.py:39
  101.1 0.0 copy-start.10
  101.1 0.0 copy-start.9
  101.1 1.0 head_sum.1
  102.2 2.3 %collective-permute-start.7 = (bf16[128,512]{1,0:T(8,128)(2,1)}, bf16[128,512]{1,0:T(8,128)(2,1)}, u32[]{:S(2)}, u32[]{:S(2)}) collective-permute-start(bf16[128,512]{1,0:T(8,128)(2,1)} %get-tuple-element.34), channel_id=1, source_target_pairs={{0,0},{1,32},{2,64},{3,96},{4,4},{5,36},{6,68},{7,100},{8,8},{9,40... | collective-permute-start | bytes 393224 | tf_op jit(solution)/shard_map/ppermute | solution.py:278
  104.4 0.0 copy-done.10
  104.4 0.6 reduce_sum.9
  105.1 0.6 dynamic_slice.6.length_ref
  106.3 0.0 copy-done.9
  106.3 0.1 copy.12.owners
  106.5 0.0 copy-done
  106.5 0.4 project.1.projected
  106.9 0.0 collective-permute-done.7.head
  106.9 0.0 copy-done.7
  107.0 2.4 %residue.1 = bf16[16,144,128]{2,1,0:T(8,128)(2,1)S(1)} custom-call(f32[1]{0:T(128)} %bitcast.scale_ref, s32[1]{0:T(128)} %dynamic_slice.6.length_ref, s32[128,1]{1,0:T(8,128)S(1)} %copy.12.owners, f32[128,512]{1,0:T(8,128)S(1)} %project.1.projected, bf16[128,512]{1,0:T(8,128)(2,1)S(1)} %copy-done.7, bf16[128,512]{1,0:T(8,128)(2,1)} %collective-permute-done.7.head, ...), custom_call_target="tpu_custom_call" | custom-call | flops 268435456 | bytes 2097152 | tf_op jit(solution)/shard_map/residue/pallas_call | solution.py:45
  109.4 0.0 copy-start.2
  109.4 22.9 %all_to_all.26.got = bf16[16,144,128]{2,1,0:T(8,128)(2,1)S(1)} all-to-all(bf16[16,144,128]{2,1,0:T(8,128)(2,1)S(1)} %residue.1), channel_id=1, replica_groups=mesh['dp'=32,'tensor'=16] {'tensor'}, dimensions={0} | all-to-all | bytes 1179648 | tf_op jit(solution)/shard_map/all_to_all | solution.py:39
  132.2 0.1 back_sum.1
  132.3 12.6 %all_to_all.27.blocks = bf16[16,128,128]{2,1,0:T(8,128)(2,1)S(1)} all-to-all(bf16[16,128,128]{2,1,0:T(8,128)(2,1)S(1)} %get-tuple-element.36), channel_id=1, replica_groups=mesh['dp'=32,'tensor'=16] {'tensor'}, dimensions={0} | all-to-all | bytes 1048576 | tf_op jit(solution)/shard_map/all_to_all | solution.py:39
  144.9 0.0 copy-done.2
  144.9 1.9 %grad_terms.1 = (bf16[16,192,128]{2,1,0:T(8,128)(2,1)S(1)}, bf16[16,192,128]{2,1,0:T(8,128)(2,1)S(1)}) custom-call(s32[5]{0:T(128)S(1)} %stack.32.place_ref, f32[1,128]{1,0:T(1,128)S(1)} %get-tuple-element.35.losses, bf16[16,128,128]{2,1,0:T(8,128)(2,1)S(1)} %all_to_all.27.blocks, bf16[128,176]{1,0:T(8,128)(2,1)S(1)} %get-tuple-element.37.hidden, ...), custom_call_target="tpu_custom_call" | custom-call | flops 276824064 | bytes 2097152 | tf_op jit(solution)/shard_map/grad_terms/pallas_call | solution.py:45
  146.9 5.3 %collective-permute-start.8 = (bf16[16,192,128]{2,1,0:T(8,128)(2,1)S(1)}, bf16[16,192,128]{2,1,0:T(8,128)(2,1)S(1)}, u32[]{:S(2)}, u32[]{:S(2)}) collective-permute-start(bf16[16,192,128]{2,1,0:T(8,128)(2,1)S(1)} %get-tuple-element.41), channel_id=1, source_target_pairs={{0,16},{16,0},{32,48},{48,32},{64,80},{80,64},{96,112},{112,96},{1... | collective-permute-start | bytes 2359304 | tf_op jit(solution)/shard_map/ppermute | solution.py:315
  152.1 1.9 collective-permute-done.8
  154.0 0.2 add_convert_fusion
  154.3 1.9 %collective-permute-start.10 = (bf16[4,192,128]{2,1,0:T(8,128)(2,1)S(1)}, bf16[4,192,128]{2,1,0:T(8,128)(2,1)S(1)}, u32[]{:S(2)}, u32[]{:S(2)}) collective-permute-start(bf16[4,192,128]{2,1,0:T(8,128)(2,1)S(1)} %get-tuple-element.47), channel_id=1, source_target_pairs={{0,480},{16,48},{32,0},{48,80},{64,32},{80,112},{96,64},{112,144},... | collective-permute-start | bytes 589832 | tf_op jit(solution)/shard_map/ppermute | solution.py:319
  156.2 4.3 %collective-permute-start.11 = (bf16[4,192,128]{2,1,0:T(8,128)(2,1)S(1)}, bf16[4,192,128]{2,1,0:T(8,128)(2,1)S(1)}, u32[]{:S(2)}, u32[]{:S(2)}) collective-permute-start(bf16[4,192,128]{2,1,0:T(8,128)(2,1)S(1)} %get-tuple-element.46), channel_id=1, source_target_pairs={{0,64},{16,464},{32,96},{48,496},{64,128},{80,16},{96,160},{112,48... | collective-permute-start | bytes 589832 | tf_op jit(solution)/shard_map/ppermute | solution.py:319
  160.6 2.1 %collective-permute-start.9 = (bf16[4,192,128]{2,1,0:T(8,128)(2,1)S(1)}, bf16[4,192,128]{2,1,0:T(8,128)(2,1)S(1)}, u32[]{:S(2)}, u32[]{:S(2)}) collective-permute-start(bf16[4,192,128]{2,1,0:T(8,128)(2,1)S(1)} %get-tuple-element.45), channel_id=1, source_target_pairs={{0,32},{16,496},{32,64},{48,16},{64,96},{80,48},{96,128},{112,80},... | collective-permute-start | bytes 589832 | tf_op jit(solution)/shard_map/ppermute | solution.py:319
  162.7 0.0 collective-permute-done.10
  162.7 2.8 %collective-permute-done.11 = bf16[4,192,128]{2,1,0:T(8,128)(2,1)S(1)} collective-permute-done((bf16[4,192,128]{2,1,0:T(8,128)(2,1)S(1)}, bf16[4,192,128]{2,1,0:T(8,128)(2,1)S(1)}, u32[]{:S(2)}, u32[]{:S(2)}) %collective-permute-start.11) | collective-permute-done | bytes 196640 | tf_op jit(solution)/shard_map/ppermute | solution.py:319
  165.6 3.9 %collective-permute-done.9 = bf16[4,192,128]{2,1,0:T(8,128)(2,1)S(1)} collective-permute-done((bf16[4,192,128]{2,1,0:T(8,128)(2,1)S(1)}, bf16[4,192,128]{2,1,0:T(8,128)(2,1)S(1)}, u32[]{:S(2)}, u32[]{:S(2)}) %collective-permute-start.9) | collective-permute-done | bytes 196640 | tf_op jit(solution)/shard_map/ppermute | solution.py:319
  169.5 0.1 add_convert_fusion.1
  169.6 21.4 %all_to_all.28.got = bf16[4,192,128]{2,1,0:T(8,128)(2,1)S(1)} all-to-all(bf16[4,192,128]{2,1,0:T(8,128)(2,1)S(1)} %add_convert_fusion.1), channel_id=1, replica_groups={{0,128,256,384},{16,144,272,400},{32,160,288,416},{48,176,304,432},{64,..., dimensions={0} | all-to-all | bytes 393216 | tf_op jit(solution)/shard_map/all_to_all | solution.py:39
  191.0 0.8 finish.1
  (6 shorter events, 0.1 us)
Async XLA Ops:
  0.6 10.0 %collective-permute-start.3 = (bf16[256,256]{1,0:T(8,128)(2,1)}, bf16[256,256]{1,0:T(8,128)(2,1)S(1)}, u32[]{:S(2)}, u32[]{:S(2)}) collective-permute-start(bf16[256,256]{1,0:T(8,128)(2,1)} %mine.1), channel_id=1, source_target_pairs={{0,16},{16,0},{32,48},{48,32},{64,80},{80,64},{96,112},{112,96},{1... | collective-permute-start | bytes 393224 | tf_op jit(solution)/shard_map/ppermute | solution.py:231
  10.6 49.6 %copy-start.4 = (bf16[128,2048]{1,0:T(8,128)(2,1)S(1)}, bf16[128,2048]{1,0:T(8,128)(2,1)}, u32[]{:S(2)}) copy-start(bf16[128,2048]{1,0:T(8,128)(2,1)} %student.1) | copy-start | bytes 1572868
  11.6 20.5 %collective-permute-start.4 = (bf16[2,256,256]{2,1,0:T(8,128)(2,1)S(1)}, bf16[2,256,256]{2,1,0:T(8,128)(2,1)S(1)}, u32[]{:S(2)}, u32[]{:S(2)}) collective-permute-start(bf16[2,256,256]{2,1,0:T(8,128)(2,1)S(1)} %pad_maximum_fusion.1), channel_id=1, source_target_pairs={{0,384},{16,144},{32,416},{48,176},{64,448},{80,208},{96,480},{112... | collective-permute-start | bytes 786440 | tf_op jit(solution)/shard_map/ppermute | solution.py:232
  15.0 15.4 %collective-permute-start = (bf16[128,256]{1,0:T(8,128)(2,1)}, bf16[128,256]{1,0:T(8,128)(2,1)S(1)}, u32[]{:S(2)}, u32[]{:S(2)}) collective-permute-start(bf16[128,256]{1,0:T(8,128)(2,1)} %own), channel_id=1, source_target_pairs={{0,32},{16,48},{32,0},{48,16},{64,96},{80,112},{96,64},{112,80},{1... | collective-permute-start | bytes 196616 | tf_op jit(solution)/shard_map/ppermute | solution.py:230
  18.6 11.9 %collective-permute-start.1 = (bf16[128,256]{1,0:T(8,128)(2,1)}, bf16[128,256]{1,0:T(8,128)(2,1)S(1)}, u32[]{:S(2)}, u32[]{:S(2)}) collective-permute-start(bf16[128,256]{1,0:T(8,128)(2,1)} %own), channel_id=1, source_target_pairs={{0,64},{16,80},{32,96},{48,112},{64,0},{80,16},{96,32},{112,48},{1... | collective-permute-start | bytes 196616 | tf_op jit(solution)/shard_map/ppermute | solution.py:230
  23.5 8.6 %collective-permute-start.2 = (bf16[128,256]{1,0:T(8,128)(2,1)}, bf16[128,256]{1,0:T(8,128)(2,1)S(1)}, u32[]{:S(2)}, u32[]{:S(2)}) collective-permute-start(bf16[128,256]{1,0:T(8,128)(2,1)} %own), channel_id=1, source_target_pairs={{0,96},{16,112},{32,64},{48,80},{64,32},{80,48},{96,0},{112,16},{1... | collective-permute-start | bytes 196616 | tf_op jit(solution)/shard_map/ppermute | solution.py:230
  25.4 1.1 copy-start.1
  26.6 1.0 copy-start.3
  27.6 1.1 copy-start.5
  28.7 31.5 %copy-start.6 = (bf16[256,256]{1,0:T(8,128)(2,1)S(1)}, bf16[256,256]{1,0:T(8,128)(2,1)}, u32[]{:S(2)}) copy-start(bf16[256,256]{1,0:T(8,128)(2,1)} %mine.1) | copy-start | bytes 393220
  28.7 31.5 %copy-start.8 = (bf16[128,256]{1,0:T(8,128)(2,1)S(1)}, bf16[128,256]{1,0:T(8,128)(2,1)}, u32[]{:S(2)}) copy-start(bf16[128,256]{1,0:T(8,128)(2,1)} %own) | copy-start | bytes 196612
  32.1 19.9 %all-to-all-start = ((bf16[16,128,128]{2,1,0:T(8,128)(2,1)}), bf16[16,128,128]{2,1,0:T(8,128)(2,1)S(1)}, u32[]{:S(2)}, u32[]{:S(2)}) async-start(bf16[16,128,128]{2,1,0:T(8,128)(2,1)} %get-tuple-element.26), calls=%async_computation | async-start | bytes 1048576 | tf_op jit(solution)/shard_map/all_to_all | solution.py:39
  38.1 13.9 %collective-permute-start.5 = (bf16[2,128,256]{2,1,0:T(8,128)(2,1)S(1)}, bf16[2,128,256]{2,1,0:T(8,128)(2,1)S(1)}, u32[]{:S(2)}, u32[]{:S(2)}) collective-permute-start(bf16[2,128,256]{2,1,0:T(8,128)(2,1)S(1)} %constant_dynamic-slice_fusion), channel_id=1, source_target_pairs={{0,384},{16,144},{32,416},{48,176},{64,448},{80,208},{96,480},{112... | collective-permute-start | bytes 393224 | tf_op jit(solution)/shard_map/ppermute | solution.py:251
  52.0 8.1 %collective-permute-start.6 = (bf16[2,384,256]{2,1,0:T(8,128)(2,1)S(1)}, bf16[2,384,256]{2,1,0:T(8,128)(2,1)S(1)}, u32[]{:S(2)}, u32[]{:S(2)}) collective-permute-start(bf16[2,384,256]{2,1,0:T(8,128)(2,1)S(1)} %pad_maximum_fusion), channel_id=1, source_target_pairs={{0,16},{16,0},{32,48},{48,32},{64,80},{80,64},{96,112},{112,96},{1... | collective-permute-start | bytes 1179656 | tf_op jit(solution)/shard_map/ppermute | solution.py:254
  101.1 3.3 %copy-start.10 = (s32[32]{0:T(128)S(1)}, s32[32]{0:T(128)}, u32[]{:S(2)}) copy-start(s32[32]{0:T(128)} %param.13) | copy-start | bytes 388
  101.1 5.2 %copy-start.9 = (s32[128,1]{0,1:T(1,128)S(1)}, s32[128,1]{0,1:T(1,128)}, u32[]{:S(2)}) copy-start(s32[128,1]{0,1:T(1,128)} %param.12) | copy-start | bytes 1540
  101.1 5.3 %copy-start = (bf16[2048,512]{1,0:T(8,128)(2,1)S(1)}, bf16[2048,512]{1,0:T(8,128)(2,1)}, u32[]{:S(2)}) copy-start(bf16[2048,512]{1,0:T(8,128)(2,1)} %proj.3) | copy-start | bytes 6291460
  102.2 4.8 %copy-start.7 = (bf16[128,512]{1,0:T(8,128)(2,1)S(1)}, bf16[128,512]{1,0:T(8,128)(2,1)}, u32[]{:S(2)}) copy-start(bf16[128,512]{1,0:T(8,128)(2,1)} %resid.1) | copy-start | bytes 393220
  102.2 4.8 %collective-permute-start.7 = (bf16[128,512]{1,0:T(8,128)(2,1)}, bf16[128,512]{1,0:T(8,128)(2,1)}, u32[]{:S(2)}, u32[]{:S(2)}) collective-permute-start(bf16[128,512]{1,0:T(8,128)(2,1)} %get-tuple-element.34), channel_id=1, source_target_pairs={{0,0},{1,32},{2,64},{3,96},{4,4},{5,36},{6,68},{7,100},{8,8},{9,40... | collective-permute-start | bytes 393224 | tf_op jit(solution)/shard_map/ppermute | solution.py:278
  109.4 35.6 %copy-start.2 = (bf16[2048,176]{0,1:T(8,128)(2,1)S(1)}, bf16[2048,176]{0,1:T(8,128)(2,1)}, u32[]{:S(2)}) copy-start(bf16[2048,176]{0,1:T(8,128)(2,1)} %param.16) | copy-start | bytes 2162692
  146.9 7.2 %collective-permute-start.8 = (bf16[16,192,128]{2,1,0:T(8,128)(2,1)S(1)}, bf16[16,192,128]{2,1,0:T(8,128)(2,1)S(1)}, u32[]{:S(2)}, u32[]{:S(2)}) collective-permute-start(bf16[16,192,128]{2,1,0:T(8,128)(2,1)S(1)} %get-tuple-element.41), channel_id=1, source_target_pairs={{0,16},{16,0},{32,48},{48,32},{64,80},{80,64},{96,112},{112,96},{1... | collective-permute-start | bytes 2359304 | tf_op jit(solution)/shard_map/ppermute | solution.py:315
  154.3 8.4 %collective-permute-start.10 = (bf16[4,192,128]{2,1,0:T(8,128)(2,1)S(1)}, bf16[4,192,128]{2,1,0:T(8,128)(2,1)S(1)}, u32[]{:S(2)}, u32[]{:S(2)}) collective-permute-start(bf16[4,192,128]{2,1,0:T(8,128)(2,1)S(1)} %get-tuple-element.47), channel_id=1, source_target_pairs={{0,480},{16,48},{32,0},{48,80},{64,32},{80,112},{96,64},{112,144},... | collective-permute-start | bytes 589832 | tf_op jit(solution)/shard_map/ppermute | solution.py:319
  156.2 9.4 %collective-permute-start.11 = (bf16[4,192,128]{2,1,0:T(8,128)(2,1)S(1)}, bf16[4,192,128]{2,1,0:T(8,128)(2,1)S(1)}, u32[]{:S(2)}, u32[]{:S(2)}) collective-permute-start(bf16[4,192,128]{2,1,0:T(8,128)(2,1)S(1)} %get-tuple-element.46), channel_id=1, source_target_pairs={{0,64},{16,464},{32,96},{48,496},{64,128},{80,16},{96,160},{112,48... | collective-permute-start | bytes 589832 | tf_op jit(solution)/shard_map/ppermute | solution.py:319
  160.6 8.9 %collective-permute-start.9 = (bf16[4,192,128]{2,1,0:T(8,128)(2,1)S(1)}, bf16[4,192,128]{2,1,0:T(8,128)(2,1)S(1)}, u32[]{:S(2)}, u32[]{:S(2)}) collective-permute-start(bf16[4,192,128]{2,1,0:T(8,128)(2,1)S(1)} %get-tuple-element.45), channel_id=1, source_target_pairs={{0,32},{16,496},{32,64},{48,16},{64,96},{80,48},{96,128},{112,80},... | collective-permute-start | bytes 589832 | tf_op jit(solution)/shard_map/ppermute | solution.py:319

commit v3 on v2

--- a/solution.py
+++ b/solution.py
@@ -249,9 +249,9 @@
     rows, far, mixed = lax.optimization_barrier((rows, far, mixed))
     half = lax.dynamic_slice_in_dim(far, dp % 2 * 128, 128, axis=1)
     half = lax.ppermute(half, "dp", FAR_STEP)
+    got = lax.ppermute(jnp.concatenate([far, half], axis=1), "dp", CORES)
     mixed = swap_all(mixed, "tensor")
-    half, mixed = lax.optimization_barrier((half, mixed))
-    got = lax.ppermute(jnp.concatenate([far, half], axis=1), "dp", CORES)
+    got, mixed = lax.optimization_barrier((got, mixed))
     parts = call(
         head_body,
         "head_parts",

time: 195 us -> 189 us (0.969)
  the two profiles are of different devices: /device:TPU:1 before, /device:TPU:65 now
where the time goes in v3:
time: 189 us; the launch traced here: 188 us
  blocking collectives  84.8 us (45%)
  starting transfers between devices  58.8 us (31%)
  waiting for transfers between devices  26.6 us (14%)
  Pallas kernels  9.84 us (5%)
  local copies, waits for them, and re-layouts  4.12 us (2%)
  other arithmetic  1.97 us (1%)
    all_to_all x4, blocking collectives, swap_all(): lax.all_to_all(x, axis, split_axis=0, concat_axis=0, tiled=True, axis_ind...  84.8 us
    ppermute x1, starting transfers between devices, on_device(): lax.ppermute(other, 'dp', CORES).astype(F32)  9.96 us
    pallas_call x8, Pallas kernels, call(): pl.pallas_call(body, out_shape=out_shape, in_specs=[smem] * len(scalars)...  9.84 us
    ppermute x3, starting transfers between devices, on_device(): near += lax.ppermute(pair[k], 'dp', ring_step(step)).astype(F32)  8.85 us
    ppermute x1, starting transfers between devices, on_device(): far = lax.ppermute(jnp.stack([out_weight, pair]), 'dp', FAR_STEP)  8.82 us
    ppermute x3, starting transfers between devices, on_device(): lax.ppermute(context, 'dp', near_step(k))  8.56 us
    ppermute x1, starting transfers between devices, on_device(): half = lax.ppermute(half, 'dp', FAR_STEP)  8.28 us
    ppermute x3, waiting for transfers between devices, on_device(): near += lax.ppermute(pair[k], 'dp', ring_step(step)).astype(F32)  7.62 us
  transfers between devices with their start and end apart: 13, of which 8 were waited for; matrix products, arithmetic and copies ran while one was open for 1% of the time, Pallas kernels for 1%

profile of v3, /device:TPU:65, one launch (start us, length us, event | category | flops | bytes accessed | tf_op | source)
XLA Modules:
  0.0 187.8 jit_solution(17004793241897722891)
XLA Ops:
  0.6 2.6 %collective-permute-start.3 = (bf16[256,256]{1,0:T(8,128)(2,1)}, bf16[256,256]{1,0:T(8,128)(2,1)S(1)}, u32[]{:S(2)}, u32[]{:S(2)}) collective-permute-start(bf16[256,256]{1,0:T(8,128)(2,1)} %mine.1), channel_id=1, source_target_pairs={{0,16},{16,0},{32,48},{48,32},{64,80},{80,64},{96,112},{112,96},{1... | collective-permute-start | bytes 393224 | tf_op jit(solution)/shard_map/ppermute | solution.py:231
  3.2 1.2 collective-permute-done.3.pair
  4.4 0.0 copy-start.4
  4.4 1.0 pad_maximum_fusion.1
  5.4 8.8 %collective-permute-start.4 = (bf16[2,256,256]{2,1,0:T(8,128)(2,1)S(1)}, bf16[2,256,256]{2,1,0:T(8,128)(2,1)S(1)}, u32[]{:S(2)}, u32[]{:S(2)}) collective-permute-start(bf16[2,256,256]{2,1,0:T(8,128)(2,1)S(1)} %pad_maximum_fusion.1), channel_id=1, source_target_pairs={{0,384},{16,144},{32,416},{48,176},{64,448},{80,208},{96,480},{112... | collective-permute-start | bytes 786440 | tf_op jit(solution)/shard_map/ppermute | solution.py:232
  14.2 3.5 %collective-permute-start = (bf16[128,256]{1,0:T(8,128)(2,1)}, bf16[128,256]{1,0:T(8,128)(2,1)S(1)}, u32[]{:S(2)}, u32[]{:S(2)}) collective-permute-start(bf16[128,256]{1,0:T(8,128)(2,1)} %own), channel_id=1, source_target_pairs={{0,32},{16,48},{32,0},{48,16},{64,96},{80,112},{96,64},{112,80},{1... | collective-permute-start | bytes 196616 | tf_op jit(solution)/shard_map/ppermute | solution.py:230
  17.8 1.9 %collective-permute-start.1 = (bf16[128,256]{1,0:T(8,128)(2,1)}, bf16[128,256]{1,0:T(8,128)(2,1)S(1)}, u32[]{:S(2)}, u32[]{:S(2)}) collective-permute-start(bf16[128,256]{1,0:T(8,128)(2,1)} %own), channel_id=1, source_target_pairs={{0,64},{16,80},{32,96},{48,112},{64,0},{80,16},{96,32},{112,48},{1... | collective-permute-start | bytes 196616 | tf_op jit(solution)/shard_map/ppermute | solution.py:230
  19.7 3.1 %collective-permute-start.2 = (bf16[128,256]{1,0:T(8,128)(2,1)}, bf16[128,256]{1,0:T(8,128)(2,1)S(1)}, u32[]{:S(2)}, u32[]{:S(2)}) collective-permute-start(bf16[128,256]{1,0:T(8,128)(2,1)} %own), channel_id=1, source_target_pairs={{0,96},{16,112},{32,64},{48,80},{64,32},{80,48},{96,0},{112,16},{1... | collective-permute-start | bytes 196616 | tf_op jit(solution)/shard_map/ppermute | solution.py:230
  22.8 0.0 copy-start.1
  22.8 1.1 copy-done.1
  23.9 0.0 copy-start.3
  23.9 1.0 copy-done.3
  25.0 0.0 copy-start.5
  25.0 1.1 copy-done.5
  26.1 0.0 copy-start.6
  26.1 0.0 copy-start.8
  26.1 1.8 forward.1
  27.9 0.0 collective-permute-done.near1
  27.9 1.0 collective-permute-done.1.near2
  28.9 2.7 %collective-permute-done.2.near3 = bf16[128,256]{1,0:T(8,128)(2,1)S(1)} collective-permute-done((bf16[128,256]{1,0:T(8,128)(2,1)}, bf16[128,256]{1,0:T(8,128)(2,1)S(1)}, u32[]{:S(2)}, u32[]{:S(2)}) %collective-permute-start.2) | collective-permute-done | bytes 65568 | tf_op jit(solution)/shard_map/ppermute | solution.py:230
  31.6 0.0 collective-permute-done.4.far
  31.6 8.3 %collective-permute-start.5 = (bf16[2,128,256]{2,1,0:T(8,128)(2,1)S(1)}, bf16[2,128,256]{2,1,0:T(8,128)(2,1)S(1)}, u32[]{:S(2)}, u32[]{:S(2)}) collective-permute-start(bf16[2,128,256]{2,1,0:T(8,128)(2,1)S(1)} %constant_dynamic-slice_fusion), channel_id=1, source_target_pairs={{0,384},{16,144},{32,416},{48,176},{64,448},{80,208},{96,480},{112... | collective-permute-start | bytes 393224 | tf_op jit(solution)/shard_map/ppermute | solution.py:251
  39.9 6.6 %all-to-all-start = ((bf16[16,128,128]{2,1,0:T(8,128)(2,1)}), bf16[16,128,128]{2,1,0:T(8,128)(2,1)S(1)}, u32[]{:S(2)}, u32[]{:S(2)}) async-start(bf16[16,128,128]{2,1,0:T(8,128)(2,1)} %get-tuple-element.26), calls=%async_computation | async-start | bytes 1048576 | tf_op jit(solution)/shard_map/all_to_all | solution.py:39
  46.5 0.0 collective-permute-done.5.half
  46.5 3.1 %collective-permute-start.6 = (bf16[2,384,256]{2,1,0:T(8,128)(2,1)S(1)}, bf16[2,384,256]{2,1,0:T(8,128)(2,1)S(1)}, u32[]{:S(2)}, u32[]{:S(2)}) collective-permute-start(bf16[2,384,256]{2,1,0:T(8,128)(2,1)S(1)} %pad_maximum_fusion), channel_id=1, source_target_pairs={{0,16},{16,0},{32,48},{48,32},{64,80},{80,64},{96,112},{112,96},{1... | collective-permute-start | bytes 1179656 | tf_op jit(solution)/shard_map/ppermute | solution.py:252
  49.7 0.1 stack.32.place_ref
  49.8 7.0 %all-to-all-done.mixed = bf16[16,128,128]{2,1,0:T(8,128)(2,1)S(1)} async-done(((bf16[16,128,128]{2,1,0:T(8,128)(2,1)}), bf16[16,128,128]{2,1,0:T(8,128)(2,1)S(1)}, u32[]{:S(2)}, u32[]{:S(2)}) %all-to-all-start) | async-done | bytes 524320 | tf_op jit(solution)/shard_map/all_to_all | solution.py:39
  56.8 0.0 collective-permute-done.6.got
  56.8 0.0 copy-done.4
  56.8 0.0 copy-done.6
  56.8 0.0 copy-done.8
  56.8 1.4 head_parts.1
  58.3 35.2 %all_to_all.25.got = bf16[16,128,640]{2,1,0:T(8,128)(2,1)S(1)} all-to-all(bf16[16,128,640]{2,1,0:T(8,128)(2,1)S(1)} %head_parts.1), channel_id=1, replica_groups=mesh['dp'=32,'tensor'=16] {'tensor'}, dimensions={0} | all-to-all | bytes 5242880 | tf_op jit(solution)/shard_map/all_to_all | solution.py:39
  93.5 0.0 copy-start.9
  93.5 1.0 head_sum.1
  94.5 2.0 %collective-permute-start.7 = (bf16[128,512]{1,0:T(8,128)(2,1)}, bf16[128,512]{1,0:T(8,128)(2,1)}, u32[]{:S(2)}, u32[]{:S(2)}) collective-permute-start(bf16[128,512]{1,0:T(8,128)(2,1)} %get-tuple-element.34), channel_id=1, source_target_pairs={{0,0},{1,32},{2,64},{3,96},{4,4},{5,36},{6,68},{7,100},{8,8},{9,40... | collective-permute-start | bytes 393224 | tf_op jit(solution)/shard_map/ppermute | solution.py:278
  96.6 0.0 copy-done.10
  96.6 0.6 reduce_sum.9
  97.2 0.6 dynamic_slice.6.length_ref
  98.4 0.0 copy-done.9
  98.5 0.1 copy.12.owners
  98.6 0.0 copy-done
  98.6 0.4 project.1.projected
  99.1 5.2 %collective-permute-done.7.head = bf16[128,512]{1,0:T(8,128)(2,1)} collective-permute-done((bf16[128,512]{1,0:T(8,128)(2,1)}, bf16[128,512]{1,0:T(8,128)(2,1)}, u32[]{:S(2)}, u32[]{:S(2)}) %collective-permute-start.7) | collective-permute-done | bytes 131104 | tf_op jit(solution)/shard_map/ppermute | solution.py:278
  104.2 0.0 copy-done.7
  104.2 2.4 %residue.1 = bf16[16,144,128]{2,1,0:T(8,128)(2,1)S(1)} custom-call(f32[1]{0:T(128)} %bitcast.scale_ref, s32[1]{0:T(128)} %dynamic_slice.6.length_ref, s32[128,1]{1,0:T(8,128)S(1)} %copy.12.owners, f32[128,512]{1,0:T(8,128)S(1)} %project.1.projected, bf16[128,512]{1,0:T(8,128)(2,1)S(1)} %copy-done.7, bf16[128,512]{1,0:T(8,128)(2,1)} %collective-permute-done.7.head, ...), custom_call_target="tpu_custom_call" | custom-call | flops 268435456 | bytes 2097152 | tf_op jit(solution)/shard_map/residue/pallas_call | solution.py:45
  106.6 0.0 copy-start.2
  106.6 12.0 %all_to_all.26.got = bf16[16,144,128]{2,1,0:T(8,128)(2,1)S(1)} all-to-all(bf16[16,144,128]{2,1,0:T(8,128)(2,1)S(1)} %residue.1), channel_id=1, replica_groups=mesh['dp'=32,'tensor'=16] {'tensor'}, dimensions={0} | all-to-all | bytes 1179648 | tf_op jit(solution)/shard_map/all_to_all | solution.py:39
  118.6 0.1 back_sum.1
  118.7 11.9 %all_to_all.27.blocks = bf16[16,128,128]{2,1,0:T(8,128)(2,1)S(1)} all-to-all(bf16[16,128,128]{2,1,0:T(8,128)(2,1)S(1)} %get-tuple-element.36), channel_id=1, replica_groups=mesh['dp'=32,'tensor'=16] {'tensor'}, dimensions={0} | all-to-all | bytes 1048576 | tf_op jit(solution)/shard_map/all_to_all | solution.py:39
  130.7 0.0 copy-done.2
  130.7 1.9 %grad_terms.1 = (bf16[16,192,128]{2,1,0:T(8,128)(2,1)S(1)}, bf16[16,192,128]{2,1,0:T(8,128)(2,1)S(1)}) custom-call(s32[5]{0:T(128)S(1)} %stack.32.place_ref, f32[1,128]{1,0:T(1,128)S(1)} %get-tuple-element.35.losses, bf16[16,128,128]{2,1,0:T(8,128)(2,1)S(1)} %all_to_all.27.blocks, bf16[128,176]{1,0:T(8,128)(2,1)S(1)} %get-tuple-element.37.hidden, ...), custom_call_target="tpu_custom_call" | custom-call | flops 276824064 | bytes 2097152 | tf_op jit(solution)/shard_map/grad_terms/pallas_call | solution.py:45
  132.6 10.0 %collective-permute-start.8 = (bf16[16,192,128]{2,1,0:T(8,128)(2,1)S(1)}, bf16[16,192,128]{2,1,0:T(8,128)(2,1)S(1)}, u32[]{:S(2)}, u32[]{:S(2)}) collective-permute-start(bf16[16,192,128]{2,1,0:T(8,128)(2,1)S(1)} %get-tuple-element.41), channel_id=1, source_target_pairs={{0,16},{16,0},{32,48},{48,32},{64,80},{80,64},{96,112},{112,96},{1... | collective-permute-start | bytes 2359304 | tf_op jit(solution)/shard_map/ppermute | solution.py:315
  142.6 1.9 %collective-permute-done.8 = bf16[16,192,128]{2,1,0:T(8,128)(2,1)S(1)} collective-permute-done((bf16[16,192,128]{2,1,0:T(8,128)(2,1)S(1)}, bf16[16,192,128]{2,1,0:T(8,128)(2,1)S(1)}, u32[]{:S(2)}, u32[]{:S(2)}) %collective-permute-start.8) | collective-permute-done | bytes 786464 | tf_op jit(solution)/shard_map/ppermute | solution.py:315
  144.5 0.2 add_convert_fusion
  144.7 5.0 %collective-permute-start.10 = (bf16[4,192,128]{2,1,0:T(8,128)(2,1)S(1)}, bf16[4,192,128]{2,1,0:T(8,128)(2,1)S(1)}, u32[]{:S(2)}, u32[]{:S(2)}) collective-permute-start(bf16[4,192,128]{2,1,0:T(8,128)(2,1)S(1)} %get-tuple-element.47), channel_id=1, source_target_pairs={{0,480},{16,48},{32,0},{48,80},{64,32},{80,112},{96,64},{112,144},... | collective-permute-start | bytes 589832 | tf_op jit(solution)/shard_map/ppermute | solution.py:319
  149.8 1.9 %collective-permute-start.11 = (bf16[4,192,128]{2,1,0:T(8,128)(2,1)S(1)}, bf16[4,192,128]{2,1,0:T(8,128)(2,1)S(1)}, u32[]{:S(2)}, u32[]{:S(2)}) collective-permute-start(bf16[4,192,128]{2,1,0:T(8,128)(2,1)S(1)} %get-tuple-element.46), channel_id=1, source_target_pairs={{0,64},{16,464},{32,96},{48,496},{64,128},{80,16},{96,160},{112,48... | collective-permute-start | bytes 589832 | tf_op jit(solution)/shard_map/ppermute | solution.py:319
  151.7 1.9 %collective-permute-start.9 = (bf16[4,192,128]{2,1,0:T(8,128)(2,1)S(1)}, bf16[4,192,128]{2,1,0:T(8,128)(2,1)S(1)}, u32[]{:S(2)}, u32[]{:S(2)}) collective-permute-start(bf16[4,192,128]{2,1,0:T(8,128)(2,1)S(1)} %get-tuple-element.45), channel_id=1, source_target_pairs={{0,32},{16,496},{32,64},{48,16},{64,96},{80,48},{96,128},{112,80},... | collective-permute-start | bytes 589832 | tf_op jit(solution)/shard_map/ppermute | solution.py:319
  153.6 0.0 collective-permute-done.10
  153.6 4.8 %collective-permute-done.11 = bf16[4,192,128]{2,1,0:T(8,128)(2,1)S(1)} collective-permute-done((bf16[4,192,128]{2,1,0:T(8,128)(2,1)S(1)}, bf16[4,192,128]{2,1,0:T(8,128)(2,1)S(1)}, u32[]{:S(2)}, u32[]{:S(2)}) %collective-permute-start.11) | collective-permute-done | bytes 196640 | tf_op jit(solution)/shard_map/ppermute | solution.py:319
  158.4 2.9 %collective-permute-done.9 = bf16[4,192,128]{2,1,0:T(8,128)(2,1)S(1)} collective-permute-done((bf16[4,192,128]{2,1,0:T(8,128)(2,1)S(1)}, bf16[4,192,128]{2,1,0:T(8,128)(2,1)S(1)}, u32[]{:S(2)}, u32[]{:S(2)}) %collective-permute-start.9) | collective-permute-done | bytes 196640 | tf_op jit(solution)/shard_map/ppermute | solution.py:319
  161.2 0.1 add_convert_fusion.1
  161.4 25.7 %all_to_all.28.got = bf16[4,192,128]{2,1,0:T(8,128)(2,1)S(1)} all-to-all(bf16[4,192,128]{2,1,0:T(8,128)(2,1)S(1)} %add_convert_fusion.1), channel_id=1, replica_groups={{0,128,256,384},{16,144,272,400},{32,160,288,416},{48,176,304,432},{64,..., dimensions={0} | all-to-all | bytes 393216 | tf_op jit(solution)/shard_map/all_to_all | solution.py:39
  187.0 0.8 finish.1
  (6 shorter events, 0.1 us)
Async XLA Ops:
  0.6 3.8 %collective-permute-start.3 = (bf16[256,256]{1,0:T(8,128)(2,1)}, bf16[256,256]{1,0:T(8,128)(2,1)S(1)}, u32[]{:S(2)}, u32[]{:S(2)}) collective-permute-start(bf16[256,256]{1,0:T(8,128)(2,1)} %mine.1), channel_id=1, source_target_pairs={{0,16},{16,0},{32,48},{48,32},{64,80},{80,64},{96,112},{112,96},{1... | collective-permute-start | bytes 393224 | tf_op jit(solution)/shard_map/ppermute | solution.py:231
  4.4 52.4 %copy-start.4 = (bf16[128,2048]{1,0:T(8,128)(2,1)S(1)}, bf16[128,2048]{1,0:T(8,128)(2,1)}, u32[]{:S(2)}) copy-start(bf16[128,2048]{1,0:T(8,128)(2,1)} %student.1) | copy-start | bytes 1572868
  5.4 26.2 %collective-permute-start.4 = (bf16[2,256,256]{2,1,0:T(8,128)(2,1)S(1)}, bf16[2,256,256]{2,1,0:T(8,128)(2,1)S(1)}, u32[]{:S(2)}, u32[]{:S(2)}) collective-permute-start(bf16[2,256,256]{2,1,0:T(8,128)(2,1)S(1)} %pad_maximum_fusion.1), channel_id=1, source_target_pairs={{0,384},{16,144},{32,416},{48,176},{64,448},{80,208},{96,480},{112... | collective-permute-start | bytes 786440 | tf_op jit(solution)/shard_map/ppermute | solution.py:232
  14.2 13.7 %collective-permute-start = (bf16[128,256]{1,0:T(8,128)(2,1)}, bf16[128,256]{1,0:T(8,128)(2,1)S(1)}, u32[]{:S(2)}, u32[]{:S(2)}) collective-permute-start(bf16[128,256]{1,0:T(8,128)(2,1)} %own), channel_id=1, source_target_pairs={{0,32},{16,48},{32,0},{48,16},{64,96},{80,112},{96,64},{112,80},{1... | collective-permute-start | bytes 196616 | tf_op jit(solution)/shard_map/ppermute | solution.py:230
  17.8 11.1 %collective-permute-start.1 = (bf16[128,256]{1,0:T(8,128)(2,1)}, bf16[128,256]{1,0:T(8,128)(2,1)S(1)}, u32[]{:S(2)}, u32[]{:S(2)}) collective-permute-start(bf16[128,256]{1,0:T(8,128)(2,1)} %own), channel_id=1, source_target_pairs={{0,64},{16,80},{32,96},{48,112},{64,0},{80,16},{96,32},{112,48},{1... | collective-permute-start | bytes 196616 | tf_op jit(solution)/shard_map/ppermute | solution.py:230
  19.7 11.9 %collective-permute-start.2 = (bf16[128,256]{1,0:T(8,128)(2,1)}, bf16[128,256]{1,0:T(8,128)(2,1)S(1)}, u32[]{:S(2)}, u32[]{:S(2)}) collective-permute-start(bf16[128,256]{1,0:T(8,128)(2,1)} %own), channel_id=1, source_target_pairs={{0,96},{16,112},{32,64},{48,80},{64,32},{80,48},{96,0},{112,16},{1... | collective-permute-start | bytes 196616 | tf_op jit(solution)/shard_map/ppermute | solution.py:230
  22.8 1.1 copy-start.1
  23.9 1.0 copy-start.3
  25.0 1.1 copy-start.5
  26.1 30.7 %copy-start.6 = (bf16[256,256]{1,0:T(8,128)(2,1)S(1)}, bf16[256,256]{1,0:T(8,128)(2,1)}, u32[]{:S(2)}) copy-start(bf16[256,256]{1,0:T(8,128)(2,1)} %mine.1) | copy-start | bytes 393220
  26.1 30.7 %copy-start.8 = (bf16[128,256]{1,0:T(8,128)(2,1)S(1)}, bf16[128,256]{1,0:T(8,128)(2,1)}, u32[]{:S(2)}) copy-start(bf16[128,256]{1,0:T(8,128)(2,1)} %own) | copy-start | bytes 196612
  31.6 14.9 %collective-permute-start.5 = (bf16[2,128,256]{2,1,0:T(8,128)(2,1)S(1)}, bf16[2,128,256]{2,1,0:T(8,128)(2,1)S(1)}, u32[]{:S(2)}, u32[]{:S(2)}) collective-permute-start(bf16[2,128,256]{2,1,0:T(8,128)(2,1)S(1)} %constant_dynamic-slice_fusion), channel_id=1, source_target_pairs={{0,384},{16,144},{32,416},{48,176},{64,448},{80,208},{96,480},{112... | collective-permute-start | bytes 393224 | tf_op jit(solution)/shard_map/ppermute | solution.py:251
  39.9 16.9 %all-to-all-start = ((bf16[16,128,128]{2,1,0:T(8,128)(2,1)}), bf16[16,128,128]{2,1,0:T(8,128)(2,1)S(1)}, u32[]{:S(2)}, u32[]{:S(2)}) async-start(bf16[16,128,128]{2,1,0:T(8,128)(2,1)} %get-tuple-element.26), calls=%async_computation | async-start | bytes 1048576 | tf_op jit(solution)/shard_map/all_to_all | solution.py:39
  46.5 10.3 %collective-permute-start.6 = (bf16[2,384,256]{2,1,0:T(8,128)(2,1)S(1)}, bf16[2,384,256]{2,1,0:T(8,128)(2,1)S(1)}, u32[]{:S(2)}, u32[]{:S(2)}) collective-permute-start(bf16[2,384,256]{2,1,0:T(8,128)(2,1)S(1)} %pad_maximum_fusion), channel_id=1, source_target_pairs={{0,16},{16,0},{32,48},{48,32},{64,80},{80,64},{96,112},{112,96},{1... | collective-permute-start | bytes 1179656 | tf_op jit(solution)/shard_map/ppermute | solution.py:252
  93.5 3.1 %copy-start.10 = (s32[32]{0:T(128)S(1)}, s32[32]{0:T(128)}, u32[]{:S(2)}) copy-start(s32[32]{0:T(128)} %param.13) | copy-start | bytes 388
  93.5 5.0 %copy-start.9 = (s32[128,1]{0,1:T(1,128)S(1)}, s32[128,1]{0,1:T(1,128)}, u32[]{:S(2)}) copy-start(s32[128,1]{0,1:T(1,128)} %param.12) | copy-start | bytes 1540
  93.5 5.1 %copy-start = (bf16[2048,512]{1,0:T(8,128)(2,1)S(1)}, bf16[2048,512]{1,0:T(8,128)(2,1)}, u32[]{:S(2)}) copy-start(bf16[2048,512]{1,0:T(8,128)(2,1)} %proj.3) | copy-start | bytes 6291460
  94.5 9.7 %copy-start.7 = (bf16[128,512]{1,0:T(8,128)(2,1)S(1)}, bf16[128,512]{1,0:T(8,128)(2,1)}, u32[]{:S(2)}) copy-start(bf16[128,512]{1,0:T(8,128)(2,1)} %resid.1) | copy-start | bytes 393220
  94.5 9.7 %collective-permute-start.7 = (bf16[128,512]{1,0:T(8,128)(2,1)}, bf16[128,512]{1,0:T(8,128)(2,1)}, u32[]{:S(2)}, u32[]{:S(2)}) collective-permute-start(bf16[128,512]{1,0:T(8,128)(2,1)} %get-tuple-element.34), channel_id=1, source_target_pairs={{0,0},{1,32},{2,64},{3,96},{4,4},{5,36},{6,68},{7,100},{8,8},{9,40... | collective-permute-start | bytes 393224 | tf_op jit(solution)/shard_map/ppermute | solution.py:278
  106.6 24.1 %copy-start.2 = (bf16[2048,176]{0,1:T(8,128)(2,1)S(1)}, bf16[2048,176]{0,1:T(8,128)(2,1)}, u32[]{:S(2)}) copy-start(bf16[2048,176]{0,1:T(8,128)(2,1)} %param.16) | copy-start | bytes 2162692
  132.6 11.9 %collective-permute-start.8 = (bf16[16,192,128]{2,1,0:T(8,128)(2,1)S(1)}, bf16[16,192,128]{2,1,0:T(8,128)(2,1)S(1)}, u32[]{:S(2)}, u32[]{:S(2)}) collective-permute-start(bf16[16,192,128]{2,1,0:T(8,128)(2,1)S(1)} %get-tuple-element.41), channel_id=1, source_target_pairs={{0,16},{16,0},{32,48},{48,32},{64,80},{80,64},{96,112},{112,96},{1... | collective-permute-start | bytes 2359304 | tf_op jit(solution)/shard_map/ppermute | solution.py:315
  144.7 8.9 %collective-permute-start.10 = (bf16[4,192,128]{2,1,0:T(8,128)(2,1)S(1)}, bf16[4,192,128]{2,1,0:T(8,128)(2,1)S(1)}, u32[]{:S(2)}, u32[]{:S(2)}) collective-permute-start(bf16[4,192,128]{2,1,0:T(8,128)(2,1)S(1)} %get-tuple-element.47), channel_id=1, source_target_pairs={{0,480},{16,48},{32,0},{48,80},{64,32},{80,112},{96,64},{112,144},... | collective-permute-start | bytes 589832 | tf_op jit(solution)/shard_map/ppermute | solution.py:319
  149.8 8.6 %collective-permute-start.11 = (bf16[4,192,128]{2,1,0:T(8,128)(2,1)S(1)}, bf16[4,192,128]{2,1,0:T(8,128)(2,1)S(1)}, u32[]{:S(2)}, u32[]{:S(2)}) collective-permute-start(bf16[4,192,128]{2,1,0:T(8,128)(2,1)S(1)} %get-tuple-element.46), channel_id=1, source_target_pairs={{0,64},{16,464},{32,96},{48,496},{64,128},{80,16},{96,160},{112,48... | collective-permute-start | bytes 589832 | tf_op jit(solution)/shard_map/ppermute | solution.py:319
  151.7 9.6 %collective-permute-start.9 = (bf16[4,192,128]{2,1,0:T(8,128)(2,1)S(1)}, bf16[4,192,128]{2,1,0:T(8,128)(2,1)S(1)}, u32[]{:S(2)}, u32[]{:S(2)}) collective-permute-start(bf16[4,192,128]{2,1,0:T(8,128)(2,1)S(1)} %get-tuple-element.45), channel_id=1, source_target_pairs={{0,32},{16,496},{32,64},{48,16},{64,96},{80,48},{96,128},{112,80},... | collective-permute-start | bytes 589832 | tf_op jit(solution)/shard_map/ppermute | solution.py:319

commit v4 on v3

--- a/solution.py
+++ b/solution.py
@@ -16,10 +16,6 @@
     return 8 * zh + 2 * zl + c
 
 
-def near_step(k):
-    return [(index(zh, zl, c), index(zh, zl ^ k, c)) for zh, zl, c in PLACES]
-
-
 def ring_step(k):
     return [(d, (d + (2 - 4 * (d % 2)) * k) % 32) for d in range(32)]
 
@@ -27,8 +23,16 @@
 FAR_STEP = [(index(zh, zl, c), index((zh - 1 + 2 * c) % 4, zl, c)) for zh, zl, c in PLACES]
 
 
+NEAR = (0, 1, -1, 2)
+
+
+def home_of(zh, zl, c, x, y):
+    chip = (4 * zh + zl + NEAR[y] * (1 - 2 * c)) % 16
+    return (2 * chip + c) * 16 + 4 * x + zl
+
+
 HOME = [
-    (index(zh, zl, c) * 16 + 4 * x + y, index(zh, y, c) * 16 + 4 * x + zl)
+    (index(zh, zl, c) * 16 + 4 * x + y, home_of(zh, zl, c, x, y))
     for zh, zl, c in PLACES
     for x in range(4)
     for y in range(4)
@@ -76,7 +80,7 @@
 def head_body(
     place_ref, student, mixed, own, near1, near2, near3, mine, pair, far, half, got, out
 ):
-    zh, zl, core, tensor = place_ref[0], place_ref[1], place_ref[2], place_ref[4]
+    zh, core, tensor = place_ref[0], place_ref[2], place_ref[4]
     mixed_sum = mixed[0].astype(F32)
     for t in range(1, 16):
         mixed_sum += mixed[t].astype(F32)
@@ -102,7 +106,7 @@
         for side, columns in enumerate(sides):
             part = jnp.dot(rows, columns, preferred_element_type=F32).astype(BF16)
             for near in range(4):
-                piece = (zh + step) % 4 * 4 + (zl ^ near)
+                piece = (zh + step) % 4 * 4 + near
                 out[piece, :, side * 256 : side * 256 + 256] = part[near * 128 : near * 128 + 128]
     for t in range(16):
         out[t, :, 512:] = updated
@@ -227,7 +231,7 @@
     loss_scale = 32.0 / (jnp.sum(query_lengths).astype(F32) * D)
     own_length = lax.dynamic_slice_in_dim(query_lengths, dp, 1)
 
-    rows = [context] + [lax.ppermute(context, "dp", near_step(k)) for k in (1, 2, 3)]
+    rows = [context] + [lax.ppermute(context, "dp", ring_step(-k)) for k in NEAR[1:]]
     pair = lax.ppermute(out_weight, "dp", CORES)
     far = lax.ppermute(jnp.stack([out_weight, pair]), "dp", FAR_STEP)
 
@@ -315,7 +319,7 @@
     pair = (mine.astype(F32) + lax.ppermute(other, "dp", CORES).astype(F32)).astype(BF16)
     pair = pair.reshape(4, 4, 192, 128)
     near = pair[0].astype(F32)
-    for k, step in ((1, 1), (3, -1), (2, 2)):
+    for k, step in ((2, 2), (1, 1), (3, -1)):
         near += lax.ppermute(pair[k], "dp", ring_step(step)).astype(F32)
     near = near.astype(BF16)
     grad = shape((64, 176), F32)

time: 189 us -> 188 us (level)
  the two profiles are of different devices: /device:TPU:65 before, /device:TPU:1 now
where the time goes in v4:
time: 188 us; the launch traced here: 184 us
  blocking collectives  92.4 us (49%)
  starting transfers between devices  61.3 us (33%)
  waiting for transfers between devices  13 us (7%)
  Pallas kernels  9.76 us (5%)
  local copies, waits for them, and re-layouts  4.12 us (2%)
  other arithmetic  1.97 us (1%)
    all_to_all x4, blocking collectives, swap_all(): lax.all_to_all(x, axis, split_axis=0, concat_axis=0, tiled=True, axis_ind...  92.4 us
    ppermute x3, starting transfers between devices, on_device(): lax.ppermute(context, 'dp', ring_step(-k))  10.4 us
    pallas_call x8, Pallas kernels, call(): pl.pallas_call(body, out_shape=out_shape, in_specs=[smem] * len(scalars)...  9.76 us
    ppermute x3, starting transfers between devices, on_device(): near += lax.ppermute(pair[k], 'dp', ring_step(step)).astype(F32)  9.43 us
    ppermute x1, starting transfers between devices, on_device(): pair = lax.ppermute(out_weight, 'dp', CORES)  8.79 us
    ppermute x1, starting transfers between devices, on_device(): lax.ppermute(other, 'dp', CORES).astype(F32)  8.44 us
    all_to_all x1, starting transfers between devices, swap_all(): lax.all_to_all(x, axis, split_axis=0, concat_axis=0, tiled=True, axis_ind...  6.77 us
    ppermute x1, starting transfers between devices, on_device(): half = lax.ppermute(half, 'dp', FAR_STEP)  6 us
  transfers between devices with their start and end apart: 13, of which 7 were waited for; matrix products, arithmetic and copies ran while one was open for 1% of the time, Pallas kernels for 1%

profile of v4, /device:TPU:1, one launch (start us, length us, event | category | flops | bytes accessed | tf_op | source)
XLA Modules:
  0.0 184.1 jit_solution(8403600861047299199)
XLA Ops:
  0.6 8.8 %collective-permute-start.3 = (bf16[256,256]{1,0:T(8,128)(2,1)}, bf16[256,256]{1,0:T(8,128)(2,1)S(1)}, u32[]{:S(2)}, u32[]{:S(2)}) collective-permute-start(bf16[256,256]{1,0:T(8,128)(2,1)} %mine.1), channel_id=1, source_target_pairs={{0,16},{16,0},{32,48},{48,32},{64,80},{80,64},{96,112},{112,96},{1... | collective-permute-start | bytes 393224 | tf_op jit(solution)/shard_map/ppermute | solution.py:235
  9.4 1.2 collective-permute-done.3.pair
  10.6 0.0 copy-start.4
  10.6 1.0 pad_maximum_fusion.1
  11.6 3.4 %collective-permute-start.4 = (bf16[2,256,256]{2,1,0:T(8,128)(2,1)S(1)}, bf16[2,256,256]{2,1,0:T(8,128)(2,1)S(1)}, u32[]{:S(2)}, u32[]{:S(2)}) collective-permute-start(bf16[2,256,256]{2,1,0:T(8,128)(2,1)S(1)} %pad_maximum_fusion.1), channel_id=1, source_target_pairs={{0,384},{16,144},{32,416},{48,176},{64,448},{80,208},{96,480},{112... | collective-permute-start | bytes 786440 | tf_op jit(solution)/shard_map/ppermute | solution.py:236
  15.0 3.5 %collective-permute-start = (bf16[128,256]{1,0:T(8,128)(2,1)}, bf16[128,256]{1,0:T(8,128)(2,1)S(1)}, u32[]{:S(2)}, u32[]{:S(2)}) collective-permute-start(bf16[128,256]{1,0:T(8,128)(2,1)} %own), channel_id=1, source_target_pairs={{0,480},{16,48},{32,0},{48,80},{64,32},{80,112},{96,64},{112,144},... | collective-permute-start | bytes 196616 | tf_op jit(solution)/shard_map/ppermute | solution.py:234
  18.6 2.9 %collective-permute-start.1 = (bf16[128,256]{1,0:T(8,128)(2,1)}, bf16[128,256]{1,0:T(8,128)(2,1)S(1)}, u32[]{:S(2)}, u32[]{:S(2)}) collective-permute-start(bf16[128,256]{1,0:T(8,128)(2,1)} %own), channel_id=1, source_target_pairs={{0,32},{16,496},{32,64},{48,16},{64,96},{80,48},{96,128},{112,80},... | collective-permute-start | bytes 196616 | tf_op jit(solution)/shard_map/ppermute | solution.py:234
  21.6 3.9 %collective-permute-start.2 = (bf16[128,256]{1,0:T(8,128)(2,1)}, bf16[128,256]{1,0:T(8,128)(2,1)S(1)}, u32[]{:S(2)}, u32[]{:S(2)}) collective-permute-start(bf16[128,256]{1,0:T(8,128)(2,1)} %own), channel_id=1, source_target_pairs={{0,448},{16,80},{32,480},{48,112},{64,0},{80,144},{96,32},{112,176... | collective-permute-start | bytes 196616 | tf_op jit(solution)/shard_map/ppermute | solution.py:234
  25.5 0.0 copy-start.1
  25.5 1.1 copy-done.1
  26.6 1.0 copy-done.3
  27.6 0.0 copy-start.5
  27.6 1.1 copy-done.5
  28.7 0.0 copy-start.6
  28.7 0.0 copy-start.8
  28.7 1.8 forward.1
  30.5 0.4 collective-permute-done.near1
  30.9 0.0 collective-permute-done.1.near2
  30.9 1.4 collective-permute-done.2.near3
  32.3 0.0 collective-permute-done.4.far
  32.3 6.0 %collective-permute-start.5 = (bf16[2,128,256]{2,1,0:T(8,128)(2,1)S(1)}, bf16[2,128,256]{2,1,0:T(8,128)(2,1)S(1)}, u32[]{:S(2)}, u32[]{:S(2)}) collective-permute-start(bf16[2,128,256]{2,1,0:T(8,128)(2,1)S(1)} %constant_dynamic-slice_fusion), channel_id=1, source_target_pairs={{0,384},{16,144},{32,416},{48,176},{64,448},{80,208},{96,480},{112... | collective-permute-start | bytes 393224 | tf_op jit(solution)/shard_map/ppermute | solution.py:255
  38.3 6.8 %all-to-all-start = ((bf16[16,128,128]{2,1,0:T(8,128)(2,1)}), bf16[16,128,128]{2,1,0:T(8,128)(2,1)S(1)}, u32[]{:S(2)}, u32[]{:S(2)}) async-start(bf16[16,128,128]{2,1,0:T(8,128)(2,1)} %get-tuple-element.26), calls=%async_computation | async-start | bytes 1048576 | tf_op jit(solution)/shard_map/all_to_all | solution.py:43
  45.1 0.0 collective-permute-done.5.half
  45.2 5.8 %collective-permute-start.6 = (bf16[2,384,256]{2,1,0:T(8,128)(2,1)S(1)}, bf16[2,384,256]{2,1,0:T(8,128)(2,1)S(1)}, u32[]{:S(2)}, u32[]{:S(2)}) collective-permute-start(bf16[2,384,256]{2,1,0:T(8,128)(2,1)S(1)} %pad_maximum_fusion), channel_id=1, source_target_pairs={{0,16},{16,0},{32,48},{48,32},{64,80},{80,64},{96,112},{112,96},{1... | collective-permute-start | bytes 1179656 | tf_op jit(solution)/shard_map/ppermute | solution.py:256
  51.0 0.1 stack.32.place_ref
  51.1 3.1 %all-to-all-done.mixed = bf16[16,128,128]{2,1,0:T(8,128)(2,1)S(1)} async-done(((bf16[16,128,128]{2,1,0:T(8,128)(2,1)}), bf16[16,128,128]{2,1,0:T(8,128)(2,1)S(1)}, u32[]{:S(2)}, u32[]{:S(2)}) %all-to-all-start) | async-done | bytes 524320 | tf_op jit(solution)/shard_map/all_to_all | solution.py:43
  54.2 0.0 collective-permute-done.6.got
  54.2 0.0 copy-done.4
  54.2 0.0 copy-done.6
  54.2 0.0 copy-done.8
  54.2 1.3 head_parts.1
  55.5 34.9 %all_to_all.25.got = bf16[16,128,640]{2,1,0:T(8,128)(2,1)S(1)} all-to-all(bf16[16,128,640]{2,1,0:T(8,128)(2,1)S(1)} %head_parts.1), channel_id=1, replica_groups=mesh['dp'=32,'tensor'=16] {'tensor'}, dimensions={0} | all-to-all | bytes 5242880 | tf_op jit(solution)/shard_map/all_to_all | solution.py:43
  90.5 0.0 copy-start.9
  90.5 0.0 copy-start
  90.5 1.0 head_sum.1
  91.5 2.3 %collective-permute-start.7 = (bf16[128,512]{1,0:T(8,128)(2,1)}, bf16[128,512]{1,0:T(8,128)(2,1)}, u32[]{:S(2)}, u32[]{:S(2)}) collective-permute-start(bf16[128,512]{1,0:T(8,128)(2,1)} %get-tuple-element.34), channel_id=1, source_target_pairs={{0,0},{1,32},{2,480},{3,64},{4,4},{5,36},{6,484},{7,68},{8,8},{9,4... | collective-permute-start | bytes 393224 | tf_op jit(solution)/shard_map/ppermute | solution.py:282
  93.8 0.0 copy-done.10
  93.8 0.6 reduce_sum.9
  94.4 0.6 dynamic_slice.6.length_ref
  95.6 0.0 copy-done.9
  95.6 0.1 copy.12.owners
  95.8 0.0 copy-done
  95.8 0.4 project.1.projected
  96.3 0.0 collective-permute-done.7.head
  96.3 0.0 copy-done.7
  96.3 2.4 %residue.1 = bf16[16,144,128]{2,1,0:T(8,128)(2,1)S(1)} custom-call(f32[1]{0:T(128)} %bitcast.scale_ref, s32[1]{0:T(128)} %dynamic_slice.6.length_ref, s32[128,1]{1,0:T(8,128)S(1)} %copy.12.owners, f32[128,512]{1,0:T(8,128)S(1)} %project.1.projected, bf16[128,512]{1,0:T(8,128)(2,1)S(1)} %copy-done.7, bf16[128,512]{1,0:T(8,128)(2,1)} %collective-permute-done.7.head, ...), custom_call_target="tpu_custom_call" | custom-call | flops 268435456 | bytes 2097152 | tf_op jit(solution)/shard_map/residue/pallas_call | solution.py:49
  98.7 0.0 copy-start.2
  98.7 20.8 %all_to_all.26.got = bf16[16,144,128]{2,1,0:T(8,128)(2,1)S(1)} all-to-all(bf16[16,144,128]{2,1,0:T(8,128)(2,1)S(1)} %residue.1), channel_id=1, replica_groups=mesh['dp'=32,'tensor'=16] {'tensor'}, dimensions={0} | all-to-all | bytes 1179648 | tf_op jit(solution)/shard_map/all_to_all | solution.py:43
  119.5 0.1 back_sum.1
  119.6 12.0 %all_to_all.27.blocks = bf16[16,128,128]{2,1,0:T(8,128)(2,1)S(1)} all-to-all(bf16[16,128,128]{2,1,0:T(8,128)(2,1)S(1)} %get-tuple-element.36), channel_id=1, replica_groups=mesh['dp'=32,'tensor'=16] {'tensor'}, dimensions={0} | all-to-all | bytes 1048576 | tf_op jit(solution)/shard_map/all_to_all | solution.py:43
  131.6 0.0 copy-done.2
  131.6 1.9 %grad_terms.1 = (bf16[16,192,128]{2,1,0:T(8,128)(2,1)S(1)}, bf16[16,192,128]{2,1,0:T(8,128)(2,1)S(1)}) custom-call(s32[5]{0:T(128)S(1)} %stack.32.place_ref, f32[1,128]{1,0:T(1,128)S(1)} %get-tuple-element.35.losses, bf16[16,128,128]{2,1,0:T(8,128)(2,1)S(1)} %all_to_all.27.blocks, bf16[128,176]{1,0:T(8,128)(2,1)S(1)} %get-tuple-element.37.hidden, ...), custom_call_target="tpu_custom_call" | custom-call | flops 276824064 | bytes 2097152 | tf_op jit(solution)/shard_map/grad_terms/pallas_call | solution.py:49
  133.6 8.4 %collective-permute-start.8 = (bf16[16,192,128]{2,1,0:T(8,128)(2,1)S(1)}, bf16[16,192,128]{2,1,0:T(8,128)(2,1)S(1)}, u32[]{:S(2)}, u32[]{:S(2)}) collective-permute-start(bf16[16,192,128]{2,1,0:T(8,128)(2,1)S(1)} %get-tuple-element.41), channel_id=1, source_target_pairs={{0,16},{16,0},{32,48},{48,32},{64,80},{80,64},{96,112},{112,96},{1... | collective-permute-start | bytes 2359304 | tf_op jit(solution)/shard_map/ppermute | solution.py:319
  142.0 1.9 %collective-permute-done.8 = bf16[16,192,128]{2,1,0:T(8,128)(2,1)S(1)} collective-permute-done((bf16[16,192,128]{2,1,0:T(8,128)(2,1)S(1)}, bf16[16,192,128]{2,1,0:T(8,128)(2,1)S(1)}, u32[]{:S(2)}, u32[]{:S(2)}) %collective-permute-start.8) | collective-permute-done | bytes 786464 | tf_op jit(solution)/shard_map/ppermute | solution.py:319
  143.9 0.2 add_convert_fusion
  144.2 2.3 %collective-permute-start.10 = (bf16[4,192,128]{2,1,0:T(8,128)(2,1)S(1)}, bf16[4,192,128]{2,1,0:T(8,128)(2,1)S(1)}, u32[]{:S(2)}, u32[]{:S(2)}) collective-permute-start(bf16[4,192,128]{2,1,0:T(8,128)(2,1)S(1)} %get-tuple-element.47), channel_id=1, source_target_pairs={{0,32},{16,496},{32,64},{48,16},{64,96},{80,48},{96,128},{112,80},... | collective-permute-start | bytes 589832 | tf_op jit(solution)/shard_map/ppermute | solution.py:323
  146.5 3.0 %collective-permute-start.11 = (bf16[4,192,128]{2,1,0:T(8,128)(2,1)S(1)}, bf16[4,192,128]{2,1,0:T(8,128)(2,1)S(1)}, u32[]{:S(2)}, u32[]{:S(2)}) collective-permute-start(bf16[4,192,128]{2,1,0:T(8,128)(2,1)S(1)} %get-tuple-element.46), channel_id=1, source_target_pairs={{0,480},{16,48},{32,0},{48,80},{64,32},{80,112},{96,64},{112,144},... | collective-permute-start | bytes 589832 | tf_op jit(solution)/shard_map/ppermute | solution.py:323
  149.5 4.1 %collective-permute-start.9 = (bf16[4,192,128]{2,1,0:T(8,128)(2,1)S(1)}, bf16[4,192,128]{2,1,0:T(8,128)(2,1)S(1)}, u32[]{:S(2)}, u32[]{:S(2)}) collective-permute-start(bf16[4,192,128]{2,1,0:T(8,128)(2,1)S(1)} %get-tuple-element.45), channel_id=1, source_target_pairs={{0,64},{16,464},{32,96},{48,496},{64,128},{80,16},{96,160},{112,48... | collective-permute-start | bytes 589832 | tf_op jit(solution)/shard_map/ppermute | solution.py:323
  153.6 0.0 collective-permute-done.10
  153.7 1.1 collective-permute-done.11
  154.8 3.9 %collective-permute-done.9 = bf16[4,192,128]{2,1,0:T(8,128)(2,1)S(1)} collective-permute-done((bf16[4,192,128]{2,1,0:T(8,128)(2,1)S(1)}, bf16[4,192,128]{2,1,0:T(8,128)(2,1)S(1)}, u32[]{:S(2)}, u32[]{:S(2)}) %collective-permute-start.9) | collective-permute-done | bytes 196640 | tf_op jit(solution)/shard_map/ppermute | solution.py:323
  158.6 0.1 add_convert_fusion.1
  158.7 24.6 %all_to_all.28.got = bf16[4,192,128]{2,1,0:T(8,128)(2,1)S(1)} all-to-all(bf16[4,192,128]{2,1,0:T(8,128)(2,1)S(1)} %add_convert_fusion.1), channel_id=1, replica_groups={{0,128,256,384},{16,144,272,400},{32,160,288,416},{48,176,304,432},{64,..., dimensions={0} | all-to-all | bytes 393216 | tf_op jit(solution)/shard_map/all_to_all | solution.py:43
  183.3 0.8 finish.1
  (6 shorter events, 0.1 us)
Async XLA Ops:
  0.6 10.0 %collective-permute-start.3 = (bf16[256,256]{1,0:T(8,128)(2,1)}, bf16[256,256]{1,0:T(8,128)(2,1)S(1)}, u32[]{:S(2)}, u32[]{:S(2)}) collective-permute-start(bf16[256,256]{1,0:T(8,128)(2,1)} %mine.1), channel_id=1, source_target_pairs={{0,16},{16,0},{32,48},{48,32},{64,80},{80,64},{96,112},{112,96},{1... | collective-permute-start | bytes 393224 | tf_op jit(solution)/shard_map/ppermute | solution.py:235
  10.6 43.6 %copy-start.4 = (bf16[128,2048]{1,0:T(8,128)(2,1)S(1)}, bf16[128,2048]{1,0:T(8,128)(2,1)}, u32[]{:S(2)}) copy-start(bf16[128,2048]{1,0:T(8,128)(2,1)} %student.1) | copy-start | bytes 1572868
  11.6 20.7 %collective-permute-start.4 = (bf16[2,256,256]{2,1,0:T(8,128)(2,1)S(1)}, bf16[2,256,256]{2,1,0:T(8,128)(2,1)S(1)}, u32[]{:S(2)}, u32[]{:S(2)}) collective-permute-start(bf16[2,256,256]{2,1,0:T(8,128)(2,1)S(1)} %pad_maximum_fusion.1), channel_id=1, source_target_pairs={{0,384},{16,144},{32,416},{48,176},{64,448},{80,208},{96,480},{112... | collective-permute-start | bytes 786440 | tf_op jit(solution)/shard_map/ppermute | solution.py:236
  15.0 15.8 %collective-permute-start = (bf16[128,256]{1,0:T(8,128)(2,1)}, bf16[128,256]{1,0:T(8,128)(2,1)S(1)}, u32[]{:S(2)}, u32[]{:S(2)}) collective-permute-start(bf16[128,256]{1,0:T(8,128)(2,1)} %own), channel_id=1, source_target_pairs={{0,480},{16,48},{32,0},{48,80},{64,32},{80,112},{96,64},{112,144},... | collective-permute-start | bytes 196616 | tf_op jit(solution)/shard_map/ppermute | solution.py:234
  18.6 12.3 %collective-permute-start.1 = (bf16[128,256]{1,0:T(8,128)(2,1)}, bf16[128,256]{1,0:T(8,128)(2,1)S(1)}, u32[]{:S(2)}, u32[]{:S(2)}) collective-permute-start(bf16[128,256]{1,0:T(8,128)(2,1)} %own), channel_id=1, source_target_pairs={{0,32},{16,496},{32,64},{48,16},{64,96},{80,48},{96,128},{112,80},... | collective-permute-start | bytes 196616 | tf_op jit(solution)/shard_map/ppermute | solution.py:234
  21.6 10.8 %collective-permute-start.2 = (bf16[128,256]{1,0:T(8,128)(2,1)}, bf16[128,256]{1,0:T(8,128)(2,1)S(1)}, u32[]{:S(2)}, u32[]{:S(2)}) collective-permute-start(bf16[128,256]{1,0:T(8,128)(2,1)} %own), channel_id=1, source_target_pairs={{0,448},{16,80},{32,480},{48,112},{64,0},{80,144},{96,32},{112,176... | collective-permute-start | bytes 196616 | tf_op jit(solution)/shard_map/ppermute | solution.py:234
  25.5 1.1 copy-start.1
  26.6 1.0 copy-start.3
  27.6 1.1 copy-start.5
  28.7 25.5 %copy-start.6 = (bf16[256,256]{1,0:T(8,128)(2,1)S(1)}, bf16[256,256]{1,0:T(8,128)(2,1)}, u32[]{:S(2)}) copy-start(bf16[256,256]{1,0:T(8,128)(2,1)} %mine.1) | copy-start | bytes 393220
  28.7 25.5 %copy-start.8 = (bf16[128,256]{1,0:T(8,128)(2,1)S(1)}, bf16[128,256]{1,0:T(8,128)(2,1)}, u32[]{:S(2)}) copy-start(bf16[128,256]{1,0:T(8,128)(2,1)} %own) | copy-start | bytes 196612
  32.3 12.8 %collective-permute-start.5 = (bf16[2,128,256]{2,1,0:T(8,128)(2,1)S(1)}, bf16[2,128,256]{2,1,0:T(8,128)(2,1)S(1)}, u32[]{:S(2)}, u32[]{:S(2)}) collective-permute-start(bf16[2,128,256]{2,1,0:T(8,128)(2,1)S(1)} %constant_dynamic-slice_fusion), channel_id=1, source_target_pairs={{0,384},{16,144},{32,416},{48,176},{64,448},{80,208},{96,480},{112... | collective-permute-start | bytes 393224 | tf_op jit(solution)/shard_map/ppermute | solution.py:255
  38.3 15.8 %all-to-all-start = ((bf16[16,128,128]{2,1,0:T(8,128)(2,1)}), bf16[16,128,128]{2,1,0:T(8,128)(2,1)S(1)}, u32[]{:S(2)}, u32[]{:S(2)}) async-start(bf16[16,128,128]{2,1,0:T(8,128)(2,1)} %get-tuple-element.26), calls=%async_computation | async-start | bytes 1048576 | tf_op jit(solution)/shard_map/all_to_all | solution.py:43
  45.2 9.0 %collective-permute-start.6 = (bf16[2,384,256]{2,1,0:T(8,128)(2,1)S(1)}, bf16[2,384,256]{2,1,0:T(8,128)(2,1)S(1)}, u32[]{:S(2)}, u32[]{:S(2)}) collective-permute-start(bf16[2,384,256]{2,1,0:T(8,128)(2,1)S(1)} %pad_maximum_fusion), channel_id=1, source_target_pairs={{0,16},{16,0},{32,48},{48,32},{64,80},{80,64},{96,112},{112,96},{1... | collective-permute-start | bytes 1179656 | tf_op jit(solution)/shard_map/ppermute | solution.py:256
  90.5 3.3 %copy-start.10 = (s32[32]{0:T(128)S(1)}, s32[32]{0:T(128)}, u32[]{:S(2)}) copy-start(s32[32]{0:T(128)} %param.13) | copy-start | bytes 388
  90.5 5.2 %copy-start.9 = (s32[128,1]{0,1:T(1,128)S(1)}, s32[128,1]{0,1:T(1,128)}, u32[]{:S(2)}) copy-start(s32[128,1]{0,1:T(1,128)} %param.12) | copy-start | bytes 1540
  90.5 5.3 %copy-start = (bf16[2048,512]{1,0:T(8,128)(2,1)S(1)}, bf16[2048,512]{1,0:T(8,128)(2,1)}, u32[]{:S(2)}) copy-start(bf16[2048,512]{1,0:T(8,128)(2,1)} %proj.3) | copy-start | bytes 6291460
  91.5 4.8 %copy-start.7 = (bf16[128,512]{1,0:T(8,128)(2,1)S(1)}, bf16[128,512]{1,0:T(8,128)(2,1)}, u32[]{:S(2)}) copy-start(bf16[128,512]{1,0:T(8,128)(2,1)} %resid.1) | copy-start | bytes 393220
  91.5 4.8 %collective-permute-start.7 = (bf16[128,512]{1,0:T(8,128)(2,1)}, bf16[128,512]{1,0:T(8,128)(2,1)}, u32[]{:S(2)}, u32[]{:S(2)}) collective-permute-start(bf16[128,512]{1,0:T(8,128)(2,1)} %get-tuple-element.34), channel_id=1, source_target_pairs={{0,0},{1,32},{2,480},{3,64},{4,4},{5,36},{6,484},{7,68},{8,8},{9,4... | collective-permute-start | bytes 393224 | tf_op jit(solution)/shard_map/ppermute | solution.py:282
  98.7 33.0 %copy-start.2 = (bf16[2048,176]{0,1:T(8,128)(2,1)S(1)}, bf16[2048,176]{0,1:T(8,128)(2,1)}, u32[]{:S(2)}) copy-start(bf16[2048,176]{0,1:T(8,128)(2,1)} %param.16) | copy-start | bytes 2162692
  133.6 10.3 %collective-permute-start.8 = (bf16[16,192,128]{2,1,0:T(8,128)(2,1)S(1)}, bf16[16,192,128]{2,1,0:T(8,128)(2,1)S(1)}, u32[]{:S(2)}, u32[]{:S(2)}) collective-permute-start(bf16[16,192,128]{2,1,0:T(8,128)(2,1)S(1)} %get-tuple-element.41), channel_id=1, source_target_pairs={{0,16},{16,0},{32,48},{48,32},{64,80},{80,64},{96,112},{112,96},{1... | collective-permute-start | bytes 2359304 | tf_op jit(solution)/shard_map/ppermute | solution.py:319
  144.2 9.5 %collective-permute-start.10 = (bf16[4,192,128]{2,1,0:T(8,128)(2,1)S(1)}, bf16[4,192,128]{2,1,0:T(8,128)(2,1)S(1)}, u32[]{:S(2)}, u32[]{:S(2)}) collective-permute-start(bf16[4,192,128]{2,1,0:T(8,128)(2,1)S(1)} %get-tuple-element.47), channel_id=1, source_target_pairs={{0,32},{16,496},{32,64},{48,16},{64,96},{80,48},{96,128},{112,80},... | collective-permute-start | bytes 589832 | tf_op jit(solution)/shard_map/ppermute | solution.py:323
  146.5 8.3 %collective-permute-start.11 = (bf16[4,192,128]{2,1,0:T(8,128)(2,1)S(1)}, bf16[4,192,128]{2,1,0:T(8,128)(2,1)S(1)}, u32[]{:S(2)}, u32[]{:S(2)}) collective-permute-start(bf16[4,192,128]{2,1,0:T(8,128)(2,1)S(1)} %get-tuple-element.46), channel_id=1, source_target_pairs={{0,480},{16,48},{32,0},{48,80},{64,32},{80,112},{96,64},{112,144},... | collective-permute-start | bytes 589832 | tf_op jit(solution)/shard_map/ppermute | solution.py:323
  149.5 9.1 %collective-permute-start.9 = (bf16[4,192,128]{2,1,0:T(8,128)(2,1)S(1)}, bf16[4,192,128]{2,1,0:T(8,128)(2,1)S(1)}, u32[]{:S(2)}, u32[]{:S(2)}) collective-permute-start(bf16[4,192,128]{2,1,0:T(8,128)(2,1)S(1)} %get-tuple-element.45), channel_id=1, source_target_pairs={{0,64},{16,464},{32,96},{48,496},{64,128},{80,16},{96,160},{112,48... | collective-permute-start | bytes 589832 | tf_op jit(solution)/shard_map/ppermute | solution.py:323

commit v5 on v4

--- a/solution.py
+++ b/solution.py
@@ -60,6 +60,11 @@
 def halves(x):
     high = x.astype(BF16).astype(F32)
     return high, x - high
+
+
+def both_body(own, other, out):
+    out[0] = own[...]
+    out[1] = other[...]
 
 
 def forward_body(rows, up, down, normed, preact, hidden, pieces):
@@ -233,7 +238,8 @@
 
     rows = [context] + [lax.ppermute(context, "dp", ring_step(-k)) for k in NEAR[1:]]
     pair = lax.ppermute(out_weight, "dp", CORES)
-    far = lax.ppermute(jnp.stack([out_weight, pair]), "dp", FAR_STEP)
+    both = call(both_body, "both_cores", 0, shape((2, 256, 256), BF16), (), out_weight, pair)
+    far = lax.ppermute(both, "dp", FAR_STEP)
 
     normed, preact, hidden, mixed = call(
         forward_body,
@@ -319,7 +325,7 @@
     pair = (mine.astype(F32) + lax.ppermute(other, "dp", CORES).astype(F32)).astype(BF16)
     pair = pair.reshape(4, 4, 192, 128)
     near = pair[0].astype(F32)
-    for k, step in ((2, 2), (1, 1), (3, -1)):
+    for k, step in ((1, 1), (2, 2), (3, -1)):
         near += lax.ppermute(pair[k], "dp", ring_step(step)).astype(F32)
     near = near.astype(BF16)
     grad = shape((64, 176), F32)

time: 188 us -> 186 us (0.989)
    unnamed x23 -> x25, local copies, waits for them, and re-layouts: 3.4 us -> 4.3 us
    pallas_call x8 -> x9, Pallas kernels: 9.76 us -> 9.75 us  [call(): pl.pallas_call(body, out_shape=out_shape, in_specs=[smem] * len(scalars)...]
  transfers between devices with their start and end apart: 13 -> 13, of which waited for: 7 -> 6; matrix products, arithmetic and copies ran while one was open for 1% -> 1% of each run, Pallas kernels for 1% -> 1%
where the time goes in v5:
time: 186 us; the launch traced here: 183 us
  blocking collectives  91.3 us (49%)
  starting transfers between devices  62.6 us (34%)
  waiting for transfers between devices  11.3 us (6%)
  Pallas kernels  9.75 us (5%)
  local copies, waits for them, and re-layouts  5.02 us (3%)
    all_to_all x4, blocking collectives, swap_all(): lax.all_to_all(x, axis, split_axis=0, concat_axis=0, tiled=True, axis_ind...  91.3 us
    ppermute x3, starting transfers between devices, on_device(): near += lax.ppermute(pair[k], 'dp', ring_step(step)).astype(F32)  10.6 us
    ppermute x3, starting transfers between devices, on_device(): lax.ppermute(context, 'dp', ring_step(-k))  10.4 us
    pallas_call x9, Pallas kernels, call(): pl.pallas_call(body, out_shape=out_shape, in_specs=[smem] * len(scalars)...  9.75 us
    ppermute x1, starting transfers between devices, on_device(): pair = lax.ppermute(out_weight, 'dp', CORES)  8.79 us
    ppermute x1, starting transfers between devices, on_device(): lax.ppermute(other, 'dp', CORES).astype(F32)  8.44 us
    all_to_all x1, starting transfers between devices, swap_all(): lax.all_to_all(x, axis, split_axis=0, concat_axis=0, tiled=True, axis_ind...  6.77 us
    ppermute x1, starting transfers between devices, on_device(): half = lax.ppermute(half, 'dp', FAR_STEP)  6 us
  transfers between devices with their start and end apart: 13, of which 6 were waited for; matrix products, arithmetic and copies ran while one was open for 1% of the time, Pallas kernels for 1%

profile of v5, /device:TPU:1, one launch (start us, length us, event | category | flops | bytes accessed | tf_op | source)
XLA Modules:
  0.0 182.6 jit_solution(13774763142139106500)
XLA Ops:
  0.6 8.8 %collective-permute-start.3 = (bf16[256,256]{1,0:T(8,128)(2,1)}, bf16[256,256]{1,0:T(8,128)(2,1)S(1)}, u32[]{:S(2)}, u32[]{:S(2)}) collective-permute-start(bf16[256,256]{1,0:T(8,128)(2,1)} %mine.1), channel_id=1, source_target_pairs={{0,16},{16,0},{32,48},{48,32},{64,80},{80,64},{96,112},{112,96},{1... | collective-permute-start | bytes 393224 | tf_op jit(solution)/shard_map/ppermute | solution.py:240
  9.4 1.2 collective-permute-done.3.other.pair
  10.6 0.0 copy-start.6
  10.6 0.9 copy-done.6
  11.5 0.0 copy-start.4
  11.5 3.6 %collective-permute-start.4 = (bf16[2,256,256]{2,1,0:T(8,128)(2,1)S(1)}, bf16[2,256,256]{2,1,0:T(8,128)(2,1)S(1)}, u32[]{:S(2)}, u32[]{:S(2)}) collective-permute-start(bf16[2,256,256]{2,1,0:T(8,128)(2,1)S(1)} %both_cores.1), channel_id=1, source_target_pairs={{0,384},{16,144},{32,416},{48,176},{64,448},{80,208},{96,480},{112... | collective-permute-start | bytes 786440 | tf_op jit(solution)/shard_map/ppermute | solution.py:242
  15.1 3.5 %collective-permute-start = (bf16[128,256]{1,0:T(8,128)(2,1)}, bf16[128,256]{1,0:T(8,128)(2,1)S(1)}, u32[]{:S(2)}, u32[]{:S(2)}) collective-permute-start(bf16[128,256]{1,0:T(8,128)(2,1)} %own.2), channel_id=1, source_target_pairs={{0,480},{16,48},{32,0},{48,80},{64,32},{80,112},{96,64},{112,144},... | collective-permute-start | bytes 196616 | tf_op jit(solution)/shard_map/ppermute | solution.py:239
  18.7 2.9 %collective-permute-start.1 = (bf16[128,256]{1,0:T(8,128)(2,1)}, bf16[128,256]{1,0:T(8,128)(2,1)S(1)}, u32[]{:S(2)}, u32[]{:S(2)}) collective-permute-start(bf16[128,256]{1,0:T(8,128)(2,1)} %own.2), channel_id=1, source_target_pairs={{0,32},{16,496},{32,64},{48,16},{64,96},{80,48},{96,128},{112,80},... | collective-permute-start | bytes 196616 | tf_op jit(solution)/shard_map/ppermute | solution.py:239
  21.6 3.9 %collective-permute-start.2 = (bf16[128,256]{1,0:T(8,128)(2,1)}, bf16[128,256]{1,0:T(8,128)(2,1)S(1)}, u32[]{:S(2)}, u32[]{:S(2)}) collective-permute-start(bf16[128,256]{1,0:T(8,128)(2,1)} %own.2), channel_id=1, source_target_pairs={{0,448},{16,80},{32,480},{48,112},{64,0},{80,144},{96,32},{112,176... | collective-permute-start | bytes 196616 | tf_op jit(solution)/shard_map/ppermute | solution.py:239
  25.5 0.0 copy-start.1
  25.5 1.1 copy-done.1
  26.6 0.0 copy-start.3
  26.6 1.0 copy-done.3
  27.7 0.0 copy-start.5
  27.7 1.1 copy-done.5
  28.8 0.0 copy-start.7
  28.8 0.0 copy-start.9
  28.8 1.8 forward.1
  30.6 0.4 collective-permute-done.near1
  30.9 0.0 collective-permute-done.1.near2
  30.9 1.4 collective-permute-done.2.near3
  32.4 0.0 collective-permute-done.4.far
  32.4 6.0 %collective-permute-start.5 = (bf16[2,128,256]{2,1,0:T(8,128)(2,1)S(1)}, bf16[2,128,256]{2,1,0:T(8,128)(2,1)S(1)}, u32[]{:S(2)}, u32[]{:S(2)}) collective-permute-start(bf16[2,128,256]{2,1,0:T(8,128)(2,1)S(1)} %constant_dynamic-slice_fusion), channel_id=1, source_target_pairs={{0,384},{16,144},{32,416},{48,176},{64,448},{80,208},{96,480},{112... | collective-permute-start | bytes 393224 | tf_op jit(solution)/shard_map/ppermute | solution.py:261
  38.4 6.8 %all-to-all-start = ((bf16[16,128,128]{2,1,0:T(8,128)(2,1)}), bf16[16,128,128]{2,1,0:T(8,128)(2,1)S(1)}, u32[]{:S(2)}, u32[]{:S(2)}) async-start(bf16[16,128,128]{2,1,0:T(8,128)(2,1)} %get-tuple-element.26), calls=%async_computation | async-start | bytes 1048576 | tf_op jit(solution)/shard_map/all_to_all | solution.py:43
  45.2 0.0 collective-permute-done.5.half
  45.2 5.8 %collective-permute-start.6 = (bf16[2,384,256]{2,1,0:T(8,128)(2,1)S(1)}, bf16[2,384,256]{2,1,0:T(8,128)(2,1)S(1)}, u32[]{:S(2)}, u32[]{:S(2)}) collective-permute-start(bf16[2,384,256]{2,1,0:T(8,128)(2,1)S(1)} %pad_maximum_fusion), channel_id=1, source_target_pairs={{0,16},{16,0},{32,48},{48,32},{64,80},{80,64},{96,112},{112,96},{1... | collective-permute-start | bytes 1179656 | tf_op jit(solution)/shard_map/ppermute | solution.py:262
  51.1 0.1 stack.23.place_ref
  51.1 3.1 %all-to-all-done.mixed = bf16[16,128,128]{2,1,0:T(8,128)(2,1)S(1)} async-done(((bf16[16,128,128]{2,1,0:T(8,128)(2,1)}), bf16[16,128,128]{2,1,0:T(8,128)(2,1)S(1)}, u32[]{:S(2)}, u32[]{:S(2)}) %all-to-all-start) | async-done | bytes 524320 | tf_op jit(solution)/shard_map/all_to_all | solution.py:43
  54.2 0.0 collective-permute-done.6.got
  54.2 0.0 copy-done.4
  54.2 0.0 copy-done.7
  54.3 0.0 copy-done.9
  54.3 1.3 head_parts.1
  55.6 34.9 %all_to_all.25.got = bf16[16,128,640]{2,1,0:T(8,128)(2,1)S(1)} all-to-all(bf16[16,128,640]{2,1,0:T(8,128)(2,1)S(1)} %head_parts.1), channel_id=1, replica_groups=mesh['dp'=32,'tensor'=16] {'tensor'}, dimensions={0} | all-to-all | bytes 5242880 | tf_op jit(solution)/shard_map/all_to_all | solution.py:43
  90.5 1.0 head_sum.1
  91.5 2.3 %collective-permute-start.7 = (bf16[128,512]{1,0:T(8,128)(2,1)}, bf16[128,512]{1,0:T(8,128)(2,1)}, u32[]{:S(2)}, u32[]{:S(2)}) collective-permute-start(bf16[128,512]{1,0:T(8,128)(2,1)} %get-tuple-element.34), channel_id=1, source_target_pairs={{0,0},{1,32},{2,480},{3,64},{4,4},{5,36},{6,484},{7,68},{8,8},{9,4... | collective-permute-start | bytes 393224 | tf_op jit(solution)/shard_map/ppermute | solution.py:288
  93.8 0.0 copy-done.11
  93.8 0.6 reduce_sum.9
  94.5 0.6 dynamic_slice.6.length_ref
  95.7 0.0 copy-done.10
  95.7 0.1 copy.12.owners
  95.9 0.0 copy-done
  95.9 0.4 project.1.projected
  96.3 0.0 collective-permute-done.7.head
  96.3 0.0 copy-done.8
  96.3 2.4 %residue.1 = bf16[16,144,128]{2,1,0:T(8,128)(2,1)S(1)} custom-call(f32[1]{0:T(128)} %bitcast.scale_ref, s32[1]{0:T(128)} %dynamic_slice.6.length_ref, s32[128,1]{1,0:T(8,128)S(1)} %copy.12.owners, f32[128,512]{1,0:T(8,128)S(1)} %project.1.projected, bf16[128,512]{1,0:T(8,128)(2,1)S(1)} %copy-done.8, bf16[128,512]{1,0:T(8,128)(2,1)} %collective-permute-done.7.head, ...), custom_call_target="tpu_custom_call" | custom-call | flops 268435456 | bytes 2097152 | tf_op jit(solution)/shard_map/residue/pallas_call | solution.py:49
  98.7 0.0 copy-start.2
  98.7 20.8 %all_to_all.26.got = bf16[16,144,128]{2,1,0:T(8,128)(2,1)S(1)} all-to-all(bf16[16,144,128]{2,1,0:T(8,128)(2,1)S(1)} %residue.1), channel_id=1, replica_groups=mesh['dp'=32,'tensor'=16] {'tensor'}, dimensions={0} | all-to-all | bytes 1179648 | tf_op jit(solution)/shard_map/all_to_all | solution.py:43
  119.6 0.1 back_sum.1
  119.7 12.0 %all_to_all.27.blocks = bf16[16,128,128]{2,1,0:T(8,128)(2,1)S(1)} all-to-all(bf16[16,128,128]{2,1,0:T(8,128)(2,1)S(1)} %get-tuple-element.36), channel_id=1, replica_groups=mesh['dp'=32,'tensor'=16] {'tensor'}, dimensions={0} | all-to-all | bytes 1048576 | tf_op jit(solution)/shard_map/all_to_all | solution.py:43
  131.7 0.0 copy-done.2
  131.7 1.9 %grad_terms.1 = (bf16[16,192,128]{2,1,0:T(8,128)(2,1)S(1)}, bf16[16,192,128]{2,1,0:T(8,128)(2,1)S(1)}) custom-call(s32[5]{0:T(128)S(1)} %stack.23.place_ref, f32[1,128]{1,0:T(1,128)S(1)} %get-tuple-element.35.losses, bf16[16,128,128]{2,1,0:T(8,128)(2,1)S(1)} %all_to_all.27.blocks, bf16[128,176]{1,0:T(8,128)(2,1)S(1)} %get-tuple-element.37.hidden, ...), custom_call_target="tpu_custom_call" | custom-call | flops 276824064 | bytes 2097152 | tf_op jit(solution)/shard_map/grad_terms/pallas_call | solution.py:49
  133.6 8.4 %collective-permute-start.8 = (bf16[16,192,128]{2,1,0:T(8,128)(2,1)S(1)}, bf16[16,192,128]{2,1,0:T(8,128)(2,1)S(1)}, u32[]{:S(2)}, u32[]{:S(2)}) collective-permute-start(bf16[16,192,128]{2,1,0:T(8,128)(2,1)S(1)} %get-tuple-element.41), channel_id=1, source_target_pairs={{0,16},{16,0},{32,48},{48,32},{64,80},{80,64},{96,112},{112,96},{1... | collective-permute-start | bytes 2359304 | tf_op jit(solution)/shard_map/ppermute | solution.py:325
  142.1 1.9 %collective-permute-done.8 = bf16[16,192,128]{2,1,0:T(8,128)(2,1)S(1)} collective-permute-done((bf16[16,192,128]{2,1,0:T(8,128)(2,1)S(1)}, bf16[16,192,128]{2,1,0:T(8,128)(2,1)S(1)}, u32[]{:S(2)}, u32[]{:S(2)}) %collective-permute-start.8) | collective-permute-done | bytes 786464 | tf_op jit(solution)/shard_map/ppermute | solution.py:325
  144.0 0.2 add_convert_fusion
  144.2 4.1 %collective-permute-start.10 = (bf16[4,192,128]{2,1,0:T(8,128)(2,1)S(1)}, bf16[4,192,128]{2,1,0:T(8,128)(2,1)S(1)}, u32[]{:S(2)}, u32[]{:S(2)}) collective-permute-start(bf16[4,192,128]{2,1,0:T(8,128)(2,1)S(1)} %get-tuple-element.47), channel_id=1, source_target_pairs={{0,64},{16,464},{32,96},{48,496},{64,128},{80,16},{96,160},{112,48... | collective-permute-start | bytes 589832 | tf_op jit(solution)/shard_map/ppermute | solution.py:329
  148.4 1.9 %collective-permute-start.11 = (bf16[4,192,128]{2,1,0:T(8,128)(2,1)S(1)}, bf16[4,192,128]{2,1,0:T(8,128)(2,1)S(1)}, u32[]{:S(2)}, u32[]{:S(2)}) collective-permute-start(bf16[4,192,128]{2,1,0:T(8,128)(2,1)S(1)} %get-tuple-element.46), channel_id=1, source_target_pairs={{0,480},{16,48},{32,0},{48,80},{64,32},{80,112},{96,64},{112,144},... | collective-permute-start | bytes 589832 | tf_op jit(solution)/shard_map/ppermute | solution.py:329
  150.3 4.6 %collective-permute-start.9 = (bf16[4,192,128]{2,1,0:T(8,128)(2,1)S(1)}, bf16[4,192,128]{2,1,0:T(8,128)(2,1)S(1)}, u32[]{:S(2)}, u32[]{:S(2)}) collective-permute-start(bf16[4,192,128]{2,1,0:T(8,128)(2,1)S(1)} %get-tuple-element.45), channel_id=1, source_target_pairs={{0,32},{16,496},{32,64},{48,16},{64,96},{80,48},{96,128},{112,80},... | collective-permute-start | bytes 589832 | tf_op jit(solution)/shard_map/ppermute | solution.py:329
  154.9 0.0 collective-permute-done.10
  154.9 3.3 %collective-permute-done.11 = bf16[4,192,128]{2,1,0:T(8,128)(2,1)S(1)} collective-permute-done((bf16[4,192,128]{2,1,0:T(8,128)(2,1)S(1)}, bf16[4,192,128]{2,1,0:T(8,128)(2,1)S(1)}, u32[]{:S(2)}, u32[]{:S(2)}) %collective-permute-start.11) | collective-permute-done | bytes 196640 | tf_op jit(solution)/shard_map/ppermute | solution.py:329
  158.2 0.0 collective-permute-done.9
  158.2 0.1 add_convert_fusion.1
  158.3 23.5 %all_to_all.28.got = bf16[4,192,128]{2,1,0:T(8,128)(2,1)S(1)} all-to-all(bf16[4,192,128]{2,1,0:T(8,128)(2,1)S(1)} %add_convert_fusion.1), channel_id=1, replica_groups={{0,128,256,384},{16,144,272,400},{32,160,288,416},{48,176,304,432},{64,..., dimensions={0} | all-to-all | bytes 393216 | tf_op jit(solution)/shard_map/all_to_all | solution.py:43
  181.8 0.8 finish.1
  (8 shorter events, 0.1 us)
Async XLA Ops:
  0.6 10.0 %collective-permute-start.3 = (bf16[256,256]{1,0:T(8,128)(2,1)}, bf16[256,256]{1,0:T(8,128)(2,1)S(1)}, u32[]{:S(2)}, u32[]{:S(2)}) collective-permute-start(bf16[256,256]{1,0:T(8,128)(2,1)} %mine.1), channel_id=1, source_target_pairs={{0,16},{16,0},{32,48},{48,32},{64,80},{80,64},{96,112},{112,96},{1... | collective-permute-start | bytes 393224 | tf_op jit(solution)/shard_map/ppermute | solution.py:240
  10.6 0.9 copy-start.6
  11.5 42.7 %copy-start.4 = (bf16[128,2048]{1,0:T(8,128)(2,1)S(1)}, bf16[128,2048]{1,0:T(8,128)(2,1)}, u32[]{:S(2)}) copy-start(bf16[128,2048]{1,0:T(8,128)(2,1)} %student.1) | copy-start | bytes 1572868
  11.5 20.9 %collective-permute-start.4 = (bf16[2,256,256]{2,1,0:T(8,128)(2,1)S(1)}, bf16[2,256,256]{2,1,0:T(8,128)(2,1)S(1)}, u32[]{:S(2)}, u32[]{:S(2)}) collective-permute-start(bf16[2,256,256]{2,1,0:T(8,128)(2,1)S(1)} %both_cores.1), channel_id=1, source_target_pairs={{0,384},{16,144},{32,416},{48,176},{64,448},{80,208},{96,480},{112... | collective-permute-start | bytes 786440 | tf_op jit(solution)/shard_map/ppermute | solution.py:242
  15.1 15.8 %collective-permute-start = (bf16[128,256]{1,0:T(8,128)(2,1)}, bf16[128,256]{1,0:T(8,128)(2,1)S(1)}, u32[]{:S(2)}, u32[]{:S(2)}) collective-permute-start(bf16[128,256]{1,0:T(8,128)(2,1)} %own.2), channel_id=1, source_target_pairs={{0,480},{16,48},{32,0},{48,80},{64,32},{80,112},{96,64},{112,144},... | collective-permute-start | bytes 196616 | tf_op jit(solution)/shard_map/ppermute | solution.py:239
  18.7 12.3 %collective-permute-start.1 = (bf16[128,256]{1,0:T(8,128)(2,1)}, bf16[128,256]{1,0:T(8,128)(2,1)S(1)}, u32[]{:S(2)}, u32[]{:S(2)}) collective-permute-start(bf16[128,256]{1,0:T(8,128)(2,1)} %own.2), channel_id=1, source_target_pairs={{0,32},{16,496},{32,64},{48,16},{64,96},{80,48},{96,128},{112,80},... | collective-permute-start | bytes 196616 | tf_op jit(solution)/shard_map/ppermute | solution.py:239
  21.6 10.8 %collective-permute-start.2 = (bf16[128,256]{1,0:T(8,128)(2,1)}, bf16[128,256]{1,0:T(8,128)(2,1)S(1)}, u32[]{:S(2)}, u32[]{:S(2)}) collective-permute-start(bf16[128,256]{1,0:T(8,128)(2,1)} %own.2), channel_id=1, source_target_pairs={{0,448},{16,80},{32,480},{48,112},{64,0},{80,144},{96,32},{112,176... | collective-permute-start | bytes 196616 | tf_op jit(solution)/shard_map/ppermute | solution.py:239
  25.5 1.1 copy-start.1
  26.6 1.0 copy-start.3
  27.7 1.1 copy-start.5
  28.8 25.5 %copy-start.7 = (bf16[256,256]{1,0:T(8,128)(2,1)S(1)}, bf16[256,256]{1,0:T(8,128)(2,1)}, u32[]{:S(2)}) copy-start(bf16[256,256]{1,0:T(8,128)(2,1)} %mine.1) | copy-start | bytes 393220
  28.8 25.5 %copy-start.9 = (bf16[128,256]{1,0:T(8,128)(2,1)S(1)}, bf16[128,256]{1,0:T(8,128)(2,1)}, u32[]{:S(2)}) copy-start(bf16[128,256]{1,0:T(8,128)(2,1)} %own.2) | copy-start | bytes 196612
  32.4 12.8 %collective-permute-start.5 = (bf16[2,128,256]{2,1,0:T(8,128)(2,1)S(1)}, bf16[2,128,256]{2,1,0:T(8,128)(2,1)S(1)}, u32[]{:S(2)}, u32[]{:S(2)}) collective-permute-start(bf16[2,128,256]{2,1,0:T(8,128)(2,1)S(1)} %constant_dynamic-slice_fusion), channel_id=1, source_target_pairs={{0,384},{16,144},{32,416},{48,176},{64,448},{80,208},{96,480},{112... | collective-permute-start | bytes 393224 | tf_op jit(solution)/shard_map/ppermute | solution.py:261
  38.4 15.8 %all-to-all-start = ((bf16[16,128,128]{2,1,0:T(8,128)(2,1)}), bf16[16,128,128]{2,1,0:T(8,128)(2,1)S(1)}, u32[]{:S(2)}, u32[]{:S(2)}) async-start(bf16[16,128,128]{2,1,0:T(8,128)(2,1)} %get-tuple-element.26), calls=%async_computation | async-start | bytes 1048576 | tf_op jit(solution)/shard_map/all_to_all | solution.py:43
  45.2 9.0 %collective-permute-start.6 = (bf16[2,384,256]{2,1,0:T(8,128)(2,1)S(1)}, bf16[2,384,256]{2,1,0:T(8,128)(2,1)S(1)}, u32[]{:S(2)}, u32[]{:S(2)}) collective-permute-start(bf16[2,384,256]{2,1,0:T(8,128)(2,1)S(1)} %pad_maximum_fusion), channel_id=1, source_target_pairs={{0,16},{16,0},{32,48},{48,32},{64,80},{80,64},{96,112},{112,96},{1... | collective-permute-start | bytes 1179656 | tf_op jit(solution)/shard_map/ppermute | solution.py:262
  90.5 3.3 %copy-start.11 = (s32[32]{0:T(128)S(1)}, s32[32]{0:T(128)}, u32[]{:S(2)}) copy-start(s32[32]{0:T(128)} %param.13) | copy-start | bytes 388
  90.5 5.2 %copy-start.10 = (s32[128,1]{0,1:T(1,128)S(1)}, s32[128,1]{0,1:T(1,128)}, u32[]{:S(2)}) copy-start(s32[128,1]{0,1:T(1,128)} %param.12) | copy-start | bytes 1540
  90.5 5.3 %copy-start = (bf16[2048,512]{1,0:T(8,128)(2,1)S(1)}, bf16[2048,512]{1,0:T(8,128)(2,1)}, u32[]{:S(2)}) copy-start(bf16[2048,512]{1,0:T(8,128)(2,1)} %proj.3) | copy-start | bytes 6291460
  91.5 4.8 %copy-start.8 = (bf16[128,512]{1,0:T(8,128)(2,1)S(1)}, bf16[128,512]{1,0:T(8,128)(2,1)}, u32[]{:S(2)}) copy-start(bf16[128,512]{1,0:T(8,128)(2,1)} %resid.1) | copy-start | bytes 393220
  91.5 4.8 %collective-permute-start.7 = (bf16[128,512]{1,0:T(8,128)(2,1)}, bf16[128,512]{1,0:T(8,128)(2,1)}, u32[]{:S(2)}, u32[]{:S(2)}) collective-permute-start(bf16[128,512]{1,0:T(8,128)(2,1)} %get-tuple-element.34), channel_id=1, source_target_pairs={{0,0},{1,32},{2,480},{3,64},{4,4},{5,36},{6,484},{7,68},{8,8},{9,4... | collective-permute-start | bytes 393224 | tf_op jit(solution)/shard_map/ppermute | solution.py:288
  98.7 33.0 %copy-start.2 = (bf16[2048,176]{0,1:T(8,128)(2,1)S(1)}, bf16[2048,176]{0,1:T(8,128)(2,1)}, u32[]{:S(2)}) copy-start(bf16[2048,176]{0,1:T(8,128)(2,1)} %param.16) | copy-start | bytes 2162692
  133.6 10.3 %collective-permute-start.8 = (bf16[16,192,128]{2,1,0:T(8,128)(2,1)S(1)}, bf16[16,192,128]{2,1,0:T(8,128)(2,1)S(1)}, u32[]{:S(2)}, u32[]{:S(2)}) collective-permute-start(bf16[16,192,128]{2,1,0:T(8,128)(2,1)S(1)} %get-tuple-element.41), channel_id=1, source_target_pairs={{0,16},{16,0},{32,48},{48,32},{64,80},{80,64},{96,112},{112,96},{1... | collective-permute-start | bytes 2359304 | tf_op jit(solution)/shard_map/ppermute | solution.py:325
  144.2 10.7 %collective-permute-start.10 = (bf16[4,192,128]{2,1,0:T(8,128)(2,1)S(1)}, bf16[4,192,128]{2,1,0:T(8,128)(2,1)S(1)}, u32[]{:S(2)}, u32[]{:S(2)}) collective-permute-start(bf16[4,192,128]{2,1,0:T(8,128)(2,1)S(1)} %get-tuple-element.47), channel_id=1, source_target_pairs={{0,64},{16,464},{32,96},{48,496},{64,128},{80,16},{96,160},{112,48... | collective-permute-start | bytes 589832 | tf_op jit(solution)/shard_map/ppermute | solution.py:329
  148.4 9.8 %collective-permute-start.11 = (bf16[4,192,128]{2,1,0:T(8,128)(2,1)S(1)}, bf16[4,192,128]{2,1,0:T(8,128)(2,1)S(1)}, u32[]{:S(2)}, u32[]{:S(2)}) collective-permute-start(bf16[4,192,128]{2,1,0:T(8,128)(2,1)S(1)} %get-tuple-element.46), channel_id=1, source_target_pairs={{0,480},{16,48},{32,0},{48,80},{64,32},{80,112},{96,64},{112,144},... | collective-permute-start | bytes 589832 | tf_op jit(solution)/shard_map/ppermute | solution.py:329
  150.3 7.9 %collective-permute-start.9 = (bf16[4,192,128]{2,1,0:T(8,128)(2,1)S(1)}, bf16[4,192,128]{2,1,0:T(8,128)(2,1)S(1)}, u32[]{:S(2)}, u32[]{:S(2)}) collective-permute-start(bf16[4,192,128]{2,1,0:T(8,128)(2,1)S(1)} %get-tuple-element.45), channel_id=1, source_target_pairs={{0,32},{16,496},{32,64},{48,16},{64,96},{80,48},{96,128},{112,80},... | collective-permute-start | bytes 589832 | tf_op jit(solution)/shard_map/ppermute | solution.py:329

commit v6 on v5

--- a/solution.py
+++ b/solution.py
@@ -11,7 +11,11 @@
 
 PLACES = [(zh, zl, c) for zh in range(4) for zl in range(4) for c in range(2)]
 CORES = [(d, d ^ 1) for d in range(32)]
-FAR = [[8 * h + 2 * l + c for h in range(4)] for l in range(4) for c in range(2)]
+FAR = [
+    [8 * (3 * c + (1 - 2 * c) * h) + 2 * l + c for h in range(4)] for l in range(4) for c in range(2)
+]
+
+
 def index(zh, zl, c):
     return 8 * zh + 2 * zl + c
 
@@ -188,8 +192,9 @@
             chip = 2 * pair + half
             ahead = (chip % 4 - zl + 4) % 4
             back = (4 - ahead) % 4
-            own_piece = jnp.where(core == 0, ahead, back) * 4 + chip // 4
-            other_piece = jnp.where(core == 0, back, ahead) * 4 + chip // 4
+            first, second = ahead * 4 + chip // 4, back * 4 + 3 - chip // 4
+            own_piece = jnp.where(core == 0, first, second)
+            other_piece = jnp.where(core == 0, second, first)
             up = up_pair[:, half * 128 : half * 128 + 128]
             below = down_pair[:, half * 128 : half * 128 + 128]
             even = jnp.where(lane < 64, up, pltpu.roll(below, 64, 1))

time: 186 us -> 185 us (level)
  the two profiles are of different devices: /device:TPU:1 before, /device:TPU:32 now
where the time goes in v6:
time: 185 us; the launch traced here: 184 us
  blocking collectives  92.3 us (50%)
  starting transfers between devices  55.6 us (30%)
  waiting for transfers between devices  18.5 us (10%)
  Pallas kernels  9.75 us (5%)
  local copies, waits for them, and re-layouts  5.03 us (3%)
    all_to_all x4, blocking collectives, swap_all(): lax.all_to_all(x, axis, split_axis=0, concat_axis=0, tiled=True, axis_ind...  92.3 us
    ppermute x1, starting transfers between devices, on_device(): far = lax.ppermute(both, 'dp', FAR_STEP)  12 us
    ppermute x3, starting transfers between devices, on_device(): near += lax.ppermute(pair[k], 'dp', ring_step(step)).astype(F32)  11.7 us
    ppermute x3, starting transfers between devices, on_device(): lax.ppermute(context, 'dp', ring_step(-k))  11.6 us
    pallas_call x9, Pallas kernels, call(): pl.pallas_call(body, out_shape=out_shape, in_specs=[smem] * len(scalars)...  9.75 us
    all_to_all x1, waiting for transfers between devices, swap_all(): lax.all_to_all(x, axis, split_axis=0, concat_axis=0, tiled=True, axis_ind...  6.63 us
    all_to_all x1, starting transfers between devices, swap_all(): lax.all_to_all(x, axis, split_axis=0, concat_axis=0, tiled=True, axis_ind...  6.35 us
    ppermute x1, starting transfers between devices, on_device(): half = lax.ppermute(half, 'dp', FAR_STEP)  5.83 us
  transfers between devices with their start and end apart: 13, of which 6 were waited for; matrix products, arithmetic and copies ran while one was open for 1% of the time, Pallas kernels for 1%

profile of v6, /device:TPU:32, one launch (start us, length us, event | category | flops | bytes accessed | tf_op | source)
XLA Modules:
  0.0 183.8 jit_solution(11448482610956505270)
XLA Ops:
  0.6 1.9 %collective-permute-start.3 = (bf16[256,256]{1,0:T(8,128)(2,1)}, bf16[256,256]{1,0:T(8,128)(2,1)S(1)}, u32[]{:S(2)}, u32[]{:S(2)}) collective-permute-start(bf16[256,256]{1,0:T(8,128)(2,1)} %mine.1), channel_id=1, source_target_pairs={{0,16},{16,0},{32,48},{48,32},{64,80},{80,64},{96,112},{112,96},{1... | collective-permute-start | bytes 393224 | tf_op jit(solution)/shard_map/ppermute | solution.py:245
  2.6 1.5 collective-permute-done.3.other.pair
  4.1 0.9 copy-done.6
  5.0 0.0 copy-start.4
  5.0 12.0 %collective-permute-start.4 = (bf16[2,256,256]{2,1,0:T(8,128)(2,1)S(1)}, bf16[2,256,256]{2,1,0:T(8,128)(2,1)S(1)}, u32[]{:S(2)}, u32[]{:S(2)}) collective-permute-start(bf16[2,256,256]{2,1,0:T(8,128)(2,1)S(1)} %both_cores.1), channel_id=1, source_target_pairs={{0,384},{16,144},{32,416},{48,176},{64,448},{80,208},{96,480},{112... | collective-permute-start | bytes 786440 | tf_op jit(solution)/shard_map/ppermute | solution.py:247
  17.0 2.9 %collective-permute-start = (bf16[128,256]{1,0:T(8,128)(2,1)}, bf16[128,256]{1,0:T(8,128)(2,1)S(1)}, u32[]{:S(2)}, u32[]{:S(2)}) collective-permute-start(bf16[128,256]{1,0:T(8,128)(2,1)} %own.2), channel_id=1, source_target_pairs={{0,480},{16,48},{32,0},{48,80},{64,32},{80,112},{96,64},{112,144},... | collective-permute-start | bytes 196616 | tf_op jit(solution)/shard_map/ppermute | solution.py:244
  19.9 2.9 %collective-permute-start.1 = (bf16[128,256]{1,0:T(8,128)(2,1)}, bf16[128,256]{1,0:T(8,128)(2,1)S(1)}, u32[]{:S(2)}, u32[]{:S(2)}) collective-permute-start(bf16[128,256]{1,0:T(8,128)(2,1)} %own.2), channel_id=1, source_target_pairs={{0,32},{16,496},{32,64},{48,16},{64,96},{80,48},{96,128},{112,80},... | collective-permute-start | bytes 196616 | tf_op jit(solution)/shard_map/ppermute | solution.py:244
  22.9 5.8 %collective-permute-start.2 = (bf16[128,256]{1,0:T(8,128)(2,1)}, bf16[128,256]{1,0:T(8,128)(2,1)S(1)}, u32[]{:S(2)}, u32[]{:S(2)}) collective-permute-start(bf16[128,256]{1,0:T(8,128)(2,1)} %own.2), channel_id=1, source_target_pairs={{0,448},{16,80},{32,480},{48,112},{64,0},{80,144},{96,32},{112,176... | collective-permute-start | bytes 196616 | tf_op jit(solution)/shard_map/ppermute | solution.py:244
  28.7 0.0 copy-start.1
  28.7 1.1 copy-done.1
  29.8 0.0 copy-start.3
  29.8 1.0 copy-done.3
  30.8 0.0 copy-start.5
  30.8 1.1 copy-done.5
  31.9 0.0 copy-start.7
  31.9 0.0 copy-start.9
  31.9 1.8 forward.1
  33.7 0.0 collective-permute-done.near1
  33.7 0.0 collective-permute-done.1.near2
  33.7 0.0 collective-permute-done.2.near3
  33.7 0.0 collective-permute-done.4.far
  33.8 5.8 %collective-permute-start.5 = (bf16[2,128,256]{2,1,0:T(8,128)(2,1)S(1)}, bf16[2,128,256]{2,1,0:T(8,128)(2,1)S(1)}, u32[]{:S(2)}, u32[]{:S(2)}) collective-permute-start(bf16[2,128,256]{2,1,0:T(8,128)(2,1)S(1)} %constant_dynamic-slice_fusion), channel_id=1, source_target_pairs={{0,384},{16,144},{32,416},{48,176},{64,448},{80,208},{96,480},{112... | collective-permute-start | bytes 393224 | tf_op jit(solution)/shard_map/ppermute | solution.py:266
  39.6 6.3 %all-to-all-start = ((bf16[16,128,128]{2,1,0:T(8,128)(2,1)}), bf16[16,128,128]{2,1,0:T(8,128)(2,1)S(1)}, u32[]{:S(2)}, u32[]{:S(2)}) async-start(bf16[16,128,128]{2,1,0:T(8,128)(2,1)} %get-tuple-element.26), calls=%async_computation | async-start | bytes 1048576 | tf_op jit(solution)/shard_map/all_to_all | solution.py:47
  45.9 1.4 collective-permute-done.5.half
  47.4 1.9 %collective-permute-start.6 = (bf16[2,384,256]{2,1,0:T(8,128)(2,1)S(1)}, bf16[2,384,256]{2,1,0:T(8,128)(2,1)S(1)}, u32[]{:S(2)}, u32[]{:S(2)}) collective-permute-start(bf16[2,384,256]{2,1,0:T(8,128)(2,1)S(1)} %pad_maximum_fusion), channel_id=1, source_target_pairs={{0,16},{16,0},{32,48},{48,32},{64,80},{80,64},{96,112},{112,96},{1... | collective-permute-start | bytes 1179656 | tf_op jit(solution)/shard_map/ppermute | solution.py:267
  49.3 0.1 stack.23.place_ref
  49.4 6.6 %all-to-all-done.mixed = bf16[16,128,128]{2,1,0:T(8,128)(2,1)S(1)} async-done(((bf16[16,128,128]{2,1,0:T(8,128)(2,1)}), bf16[16,128,128]{2,1,0:T(8,128)(2,1)S(1)}, u32[]{:S(2)}, u32[]{:S(2)}) %all-to-all-start) | async-done | bytes 524320 | tf_op jit(solution)/shard_map/all_to_all | solution.py:47
  56.0 0.0 collective-permute-done.6.got
  56.0 0.0 copy-done.4
  56.0 0.0 copy-done.7
  56.1 0.0 copy-done.9
  56.1 1.3 head_parts.1
  57.4 35.8 %all_to_all.25.got = bf16[16,128,640]{2,1,0:T(8,128)(2,1)S(1)} all-to-all(bf16[16,128,640]{2,1,0:T(8,128)(2,1)S(1)} %head_parts.1), channel_id=1, replica_groups=mesh['dp'=32,'tensor'=16] {'tensor'}, dimensions={0} | all-to-all | bytes 5242880 | tf_op jit(solution)/shard_map/all_to_all | solution.py:47
  93.2 0.0 copy-start.11
  93.2 1.0 head_sum.1
  94.2 2.4 %collective-permute-start.7 = (bf16[128,512]{1,0:T(8,128)(2,1)}, bf16[128,512]{1,0:T(8,128)(2,1)}, u32[]{:S(2)}, u32[]{:S(2)}) collective-permute-start(bf16[128,512]{1,0:T(8,128)(2,1)} %get-tuple-element.34), channel_id=1, source_target_pairs={{0,0},{1,32},{2,480},{3,64},{4,4},{5,36},{6,484},{7,68},{8,8},{9,4... | collective-permute-start | bytes 393224 | tf_op jit(solution)/shard_map/ppermute | solution.py:293
  96.6 0.0 copy-done.11
  96.6 0.6 reduce_sum.9
  97.2 0.6 dynamic_slice.6.length_ref
  98.5 0.0 copy-done.10
  98.5 0.1 copy.12.owners
  98.6 0.0 copy-done
  98.6 0.4 project.1.projected
  99.1 3.3 %collective-permute-done.7.head = bf16[128,512]{1,0:T(8,128)(2,1)} collective-permute-done((bf16[128,512]{1,0:T(8,128)(2,1)}, bf16[128,512]{1,0:T(8,128)(2,1)}, u32[]{:S(2)}, u32[]{:S(2)}) %collective-permute-start.7) | collective-permute-done | bytes 131104 | tf_op jit(solution)/shard_map/ppermute | solution.py:293
  102.4 0.0 copy-done.8
  102.4 2.4 %residue.1 = bf16[16,144,128]{2,1,0:T(8,128)(2,1)S(1)} custom-call(f32[1]{0:T(128)} %bitcast.scale_ref, s32[1]{0:T(128)} %dynamic_slice.6.length_ref, s32[128,1]{1,0:T(8,128)S(1)} %copy.12.owners, f32[128,512]{1,0:T(8,128)S(1)} %project.1.projected, bf16[128,512]{1,0:T(8,128)(2,1)S(1)} %copy-done.8, bf16[128,512]{1,0:T(8,128)(2,1)} %collective-permute-done.7.head, ...), custom_call_target="tpu_custom_call" | custom-call | flops 268435456 | bytes 2097152 | tf_op jit(solution)/shard_map/residue/pallas_call | solution.py:53
  104.8 0.0 copy-start.2
  104.8 16.2 %all_to_all.26.got = bf16[16,144,128]{2,1,0:T(8,128)(2,1)S(1)} all-to-all(bf16[16,144,128]{2,1,0:T(8,128)(2,1)S(1)} %residue.1), channel_id=1, replica_groups=mesh['dp'=32,'tensor'=16] {'tensor'}, dimensions={0} | all-to-all | bytes 1179648 | tf_op jit(solution)/shard_map/all_to_all | solution.py:47
  121.0 0.1 back_sum.1
  121.1 13.3 %all_to_all.27.blocks = bf16[16,128,128]{2,1,0:T(8,128)(2,1)S(1)} all-to-all(bf16[16,128,128]{2,1,0:T(8,128)(2,1)S(1)} %get-tuple-element.36), channel_id=1, replica_groups=mesh['dp'=32,'tensor'=16] {'tensor'}, dimensions={0} | all-to-all | bytes 1048576 | tf_op jit(solution)/shard_map/all_to_all | solution.py:47
  134.4 0.0 copy-done.2
  134.4 1.9 %grad_terms.1 = (bf16[16,192,128]{2,1,0:T(8,128)(2,1)S(1)}, bf16[16,192,128]{2,1,0:T(8,128)(2,1)S(1)}) custom-call(s32[5]{0:T(128)S(1)} %stack.23.place_ref, f32[1,128]{1,0:T(1,128)S(1)} %get-tuple-element.35.losses, bf16[16,128,128]{2,1,0:T(8,128)(2,1)S(1)} %all_to_all.27.blocks, bf16[128,176]{1,0:T(8,128)(2,1)S(1)} %get-tuple-element.37.hidden, ...), custom_call_target="tpu_custom_call" | custom-call | flops 276824064 | bytes 2097152 | tf_op jit(solution)/shard_map/grad_terms/pallas_call | solution.py:53
  136.3 1.9 %collective-permute-start.8 = (bf16[16,192,128]{2,1,0:T(8,128)(2,1)S(1)}, bf16[16,192,128]{2,1,0:T(8,128)(2,1)S(1)}, u32[]{:S(2)}, u32[]{:S(2)}) collective-permute-start(bf16[16,192,128]{2,1,0:T(8,128)(2,1)S(1)} %get-tuple-element.41), channel_id=1, source_target_pairs={{0,16},{16,0},{32,48},{48,32},{64,80},{80,64},{96,112},{112,96},{1... | collective-permute-start | bytes 2359304 | tf_op jit(solution)/shard_map/ppermute | solution.py:330
  138.3 2.3 %collective-permute-done.8 = bf16[16,192,128]{2,1,0:T(8,128)(2,1)S(1)} collective-permute-done((bf16[16,192,128]{2,1,0:T(8,128)(2,1)S(1)}, bf16[16,192,128]{2,1,0:T(8,128)(2,1)S(1)}, u32[]{:S(2)}, u32[]{:S(2)}) %collective-permute-start.8) | collective-permute-done | bytes 786464 | tf_op jit(solution)/shard_map/ppermute | solution.py:330
  140.5 0.2 add_convert_fusion
  140.8 2.9 %collective-permute-start.10 = (bf16[4,192,128]{2,1,0:T(8,128)(2,1)S(1)}, bf16[4,192,128]{2,1,0:T(8,128)(2,1)S(1)}, u32[]{:S(2)}, u32[]{:S(2)}) collective-permute-start(bf16[4,192,128]{2,1,0:T(8,128)(2,1)S(1)} %get-tuple-element.47), channel_id=1, source_target_pairs={{0,64},{16,464},{32,96},{48,496},{64,128},{80,16},{96,160},{112,48... | collective-permute-start | bytes 589832 | tf_op jit(solution)/shard_map/ppermute | solution.py:334
  143.7 3.4 %collective-permute-start.11 = (bf16[4,192,128]{2,1,0:T(8,128)(2,1)S(1)}, bf16[4,192,128]{2,1,0:T(8,128)(2,1)S(1)}, u32[]{:S(2)}, u32[]{:S(2)}) collective-permute-start(bf16[4,192,128]{2,1,0:T(8,128)(2,1)S(1)} %get-tuple-element.46), channel_id=1, source_target_pairs={{0,480},{16,48},{32,0},{48,80},{64,32},{80,112},{96,64},{112,144},... | collective-permute-start | bytes 589832 | tf_op jit(solution)/shard_map/ppermute | solution.py:334
  147.1 5.4 %collective-permute-start.9 = (bf16[4,192,128]{2,1,0:T(8,128)(2,1)S(1)}, bf16[4,192,128]{2,1,0:T(8,128)(2,1)S(1)}, u32[]{:S(2)}, u32[]{:S(2)}) collective-permute-start(bf16[4,192,128]{2,1,0:T(8,128)(2,1)S(1)} %get-tuple-element.45), channel_id=1, source_target_pairs={{0,32},{16,496},{32,64},{48,16},{64,96},{80,48},{96,128},{112,80},... | collective-permute-start | bytes 589832 | tf_op jit(solution)/shard_map/ppermute | solution.py:334
  152.5 0.0 collective-permute-done.10
  152.5 3.4 %collective-permute-done.11 = bf16[4,192,128]{2,1,0:T(8,128)(2,1)S(1)} collective-permute-done((bf16[4,192,128]{2,1,0:T(8,128)(2,1)S(1)}, bf16[4,192,128]{2,1,0:T(8,128)(2,1)S(1)}, u32[]{:S(2)}, u32[]{:S(2)}) %collective-permute-start.11) | collective-permute-done | bytes 196640 | tf_op jit(solution)/shard_map/ppermute | solution.py:334
  155.9 0.0 collective-permute-done.9
  155.9 0.1 add_convert_fusion.1
  156.0 27.0 %all_to_all.28.got = bf16[4,192,128]{2,1,0:T(8,128)(2,1)S(1)} all-to-all(bf16[4,192,128]{2,1,0:T(8,128)(2,1)S(1)} %add_convert_fusion.1), channel_id=1, replica_groups={{0,128,256,384},{400,272,144,16},{32,160,288,416},{432,304,176,48},{64,..., dimensions={0} | all-to-all | bytes 393216 | tf_op jit(solution)/shard_map/all_to_all | solution.py:47
  183.0 0.8 finish.1
  (8 shorter events, 0.1 us)
Async XLA Ops:
  0.6 3.5 %collective-permute-start.3 = (bf16[256,256]{1,0:T(8,128)(2,1)}, bf16[256,256]{1,0:T(8,128)(2,1)S(1)}, u32[]{:S(2)}, u32[]{:S(2)}) collective-permute-start(bf16[256,256]{1,0:T(8,128)(2,1)} %mine.1), channel_id=1, source_target_pairs={{0,16},{16,0},{32,48},{48,32},{64,80},{80,64},{96,112},{112,96},{1... | collective-permute-start | bytes 393224 | tf_op jit(solution)/shard_map/ppermute | solution.py:245
  4.1 0.9 copy-start.6
  5.0 51.1 %copy-start.4 = (bf16[128,2048]{1,0:T(8,128)(2,1)S(1)}, bf16[128,2048]{1,0:T(8,128)(2,1)}, u32[]{:S(2)}) copy-start(bf16[128,2048]{1,0:T(8,128)(2,1)} %student.1) | copy-start | bytes 1572868
  5.0 28.7 %collective-permute-start.4 = (bf16[2,256,256]{2,1,0:T(8,128)(2,1)S(1)}, bf16[2,256,256]{2,1,0:T(8,128)(2,1)S(1)}, u32[]{:S(2)}, u32[]{:S(2)}) collective-permute-start(bf16[2,256,256]{2,1,0:T(8,128)(2,1)S(1)} %both_cores.1), channel_id=1, source_target_pairs={{0,384},{16,144},{32,416},{48,176},{64,448},{80,208},{96,480},{112... | collective-permute-start | bytes 786440 | tf_op jit(solution)/shard_map/ppermute | solution.py:247
  17.0 16.7 %collective-permute-start = (bf16[128,256]{1,0:T(8,128)(2,1)}, bf16[128,256]{1,0:T(8,128)(2,1)S(1)}, u32[]{:S(2)}, u32[]{:S(2)}) collective-permute-start(bf16[128,256]{1,0:T(8,128)(2,1)} %own.2), channel_id=1, source_target_pairs={{0,480},{16,48},{32,0},{48,80},{64,32},{80,112},{96,64},{112,144},... | collective-permute-start | bytes 196616 | tf_op jit(solution)/shard_map/ppermute | solution.py:244
  19.9 13.8 %collective-permute-start.1 = (bf16[128,256]{1,0:T(8,128)(2,1)}, bf16[128,256]{1,0:T(8,128)(2,1)S(1)}, u32[]{:S(2)}, u32[]{:S(2)}) collective-permute-start(bf16[128,256]{1,0:T(8,128)(2,1)} %own.2), channel_id=1, source_target_pairs={{0,32},{16,496},{32,64},{48,16},{64,96},{80,48},{96,128},{112,80},... | collective-permute-start | bytes 196616 | tf_op jit(solution)/shard_map/ppermute | solution.py:244
  22.9 10.9 %collective-permute-start.2 = (bf16[128,256]{1,0:T(8,128)(2,1)}, bf16[128,256]{1,0:T(8,128)(2,1)S(1)}, u32[]{:S(2)}, u32[]{:S(2)}) collective-permute-start(bf16[128,256]{1,0:T(8,128)(2,1)} %own.2), channel_id=1, source_target_pairs={{0,448},{16,80},{32,480},{48,112},{64,0},{80,144},{96,32},{112,176... | collective-permute-start | bytes 196616 | tf_op jit(solution)/shard_map/ppermute | solution.py:244
  28.7 1.1 copy-start.1
  29.8 1.0 copy-start.3
  30.8 1.1 copy-start.5
  31.9 24.1 %copy-start.7 = (bf16[256,256]{1,0:T(8,128)(2,1)S(1)}, bf16[256,256]{1,0:T(8,128)(2,1)}, u32[]{:S(2)}) copy-start(bf16[256,256]{1,0:T(8,128)(2,1)} %mine.1) | copy-start | bytes 393220
  31.9 24.1 %copy-start.9 = (bf16[128,256]{1,0:T(8,128)(2,1)S(1)}, bf16[128,256]{1,0:T(8,128)(2,1)}, u32[]{:S(2)}) copy-start(bf16[128,256]{1,0:T(8,128)(2,1)} %own.2) | copy-start | bytes 196612
  33.8 13.6 %collective-permute-start.5 = (bf16[2,128,256]{2,1,0:T(8,128)(2,1)S(1)}, bf16[2,128,256]{2,1,0:T(8,128)(2,1)S(1)}, u32[]{:S(2)}, u32[]{:S(2)}) collective-permute-start(bf16[2,128,256]{2,1,0:T(8,128)(2,1)S(1)} %constant_dynamic-slice_fusion), channel_id=1, source_target_pairs={{0,384},{16,144},{32,416},{48,176},{64,448},{80,208},{96,480},{112... | collective-permute-start | bytes 393224 | tf_op jit(solution)/shard_map/ppermute | solution.py:266
  39.6 16.4 %all-to-all-start = ((bf16[16,128,128]{2,1,0:T(8,128)(2,1)}), bf16[16,128,128]{2,1,0:T(8,128)(2,1)S(1)}, u32[]{:S(2)}, u32[]{:S(2)}) async-start(bf16[16,128,128]{2,1,0:T(8,128)(2,1)} %get-tuple-element.26), calls=%async_computation | async-start | bytes 1048576 | tf_op jit(solution)/shard_map/all_to_all | solution.py:47
  47.4 8.7 %collective-permute-start.6 = (bf16[2,384,256]{2,1,0:T(8,128)(2,1)S(1)}, bf16[2,384,256]{2,1,0:T(8,128)(2,1)S(1)}, u32[]{:S(2)}, u32[]{:S(2)}) collective-permute-start(bf16[2,384,256]{2,1,0:T(8,128)(2,1)S(1)} %pad_maximum_fusion), channel_id=1, source_target_pairs={{0,16},{16,0},{32,48},{48,32},{64,80},{80,64},{96,112},{112,96},{1... | collective-permute-start | bytes 1179656 | tf_op jit(solution)/shard_map/ppermute | solution.py:267
  93.2 3.4 %copy-start.11 = (s32[32]{0:T(128)S(1)}, s32[32]{0:T(128)}, u32[]{:S(2)}) copy-start(s32[32]{0:T(128)} %param.13) | copy-start | bytes 388
  93.2 5.3 %copy-start.10 = (s32[128,1]{0,1:T(1,128)S(1)}, s32[128,1]{0,1:T(1,128)}, u32[]{:S(2)}) copy-start(s32[128,1]{0,1:T(1,128)} %param.12) | copy-start | bytes 1540
  93.2 5.5 %copy-start = (bf16[2048,512]{1,0:T(8,128)(2,1)S(1)}, bf16[2048,512]{1,0:T(8,128)(2,1)}, u32[]{:S(2)}) copy-start(bf16[2048,512]{1,0:T(8,128)(2,1)} %proj.3) | copy-start | bytes 6291460
  94.2 8.2 %copy-start.8 = (bf16[128,512]{1,0:T(8,128)(2,1)S(1)}, bf16[128,512]{1,0:T(8,128)(2,1)}, u32[]{:S(2)}) copy-start(bf16[128,512]{1,0:T(8,128)(2,1)} %resid.1) | copy-start | bytes 393220
  94.2 8.2 %collective-permute-start.7 = (bf16[128,512]{1,0:T(8,128)(2,1)}, bf16[128,512]{1,0:T(8,128)(2,1)}, u32[]{:S(2)}, u32[]{:S(2)}) collective-permute-start(bf16[128,512]{1,0:T(8,128)(2,1)} %get-tuple-element.34), channel_id=1, source_target_pairs={{0,0},{1,32},{2,480},{3,64},{4,4},{5,36},{6,484},{7,68},{8,8},{9,4... | collective-permute-start | bytes 393224 | tf_op jit(solution)/shard_map/ppermute | solution.py:293
  104.8 29.6 %copy-start.2 = (bf16[2048,176]{0,1:T(8,128)(2,1)S(1)}, bf16[2048,176]{0,1:T(8,128)(2,1)}, u32[]{:S(2)}) copy-start(bf16[2048,176]{0,1:T(8,128)(2,1)} %param.16) | copy-start | bytes 2162692
  136.3 4.2 %collective-permute-start.8 = (bf16[16,192,128]{2,1,0:T(8,128)(2,1)S(1)}, bf16[16,192,128]{2,1,0:T(8,128)(2,1)S(1)}, u32[]{:S(2)}, u32[]{:S(2)}) collective-permute-start(bf16[16,192,128]{2,1,0:T(8,128)(2,1)S(1)} %get-tuple-element.41), channel_id=1, source_target_pairs={{0,16},{16,0},{32,48},{48,32},{64,80},{80,64},{96,112},{112,96},{1... | collective-permute-start | bytes 2359304 | tf_op jit(solution)/shard_map/ppermute | solution.py:330
  140.8 11.7 %collective-permute-start.10 = (bf16[4,192,128]{2,1,0:T(8,128)(2,1)S(1)}, bf16[4,192,128]{2,1,0:T(8,128)(2,1)S(1)}, u32[]{:S(2)}, u32[]{:S(2)}) collective-permute-start(bf16[4,192,128]{2,1,0:T(8,128)(2,1)S(1)} %get-tuple-element.47), channel_id=1, source_target_pairs={{0,64},{16,464},{32,96},{48,496},{64,128},{80,16},{96,160},{112,48... | collective-permute-start | bytes 589832 | tf_op jit(solution)/shard_map/ppermute | solution.py:334
  143.7 12.2 %collective-permute-start.11 = (bf16[4,192,128]{2,1,0:T(8,128)(2,1)S(1)}, bf16[4,192,128]{2,1,0:T(8,128)(2,1)S(1)}, u32[]{:S(2)}, u32[]{:S(2)}) collective-permute-start(bf16[4,192,128]{2,1,0:T(8,128)(2,1)S(1)} %get-tuple-element.46), channel_id=1, source_target_pairs={{0,480},{16,48},{32,0},{48,80},{64,32},{80,112},{96,64},{112,144},... | collective-permute-start | bytes 589832 | tf_op jit(solution)/shard_map/ppermute | solution.py:334
  147.1 8.8 %collective-permute-start.9 = (bf16[4,192,128]{2,1,0:T(8,128)(2,1)S(1)}, bf16[4,192,128]{2,1,0:T(8,128)(2,1)S(1)}, u32[]{:S(2)}, u32[]{:S(2)}) collective-permute-start(bf16[4,192,128]{2,1,0:T(8,128)(2,1)S(1)} %get-tuple-element.45), channel_id=1, source_target_pairs={{0,32},{16,496},{32,64},{48,16},{64,96},{80,48},{96,128},{112,80},... | collective-permute-start | bytes 589832 | tf_op jit(solution)/shard_map/ppermute | solution.py:334

commit v7 on v6

--- a/solution.py
+++ b/solution.py
@@ -41,6 +41,19 @@
     for x in range(4)
     for y in range(4)
 ]
+
+
+ACROSS = [
+    [d * 16 + (15 - t if d % 2 else t) for t in range(16)] for d in range(32)
+]
+
+
+def spot(core, t):
+    return jnp.where(core == 0, t, 15 - t)
+
+
+def across(x):
+    return swap_all(x, ("dp", "tensor"), ACROSS)
 
 
 def swap_all(x, axis, groups=None):
@@ -71,7 +84,7 @@
     out[1] = other[...]
 
 
-def forward_body(rows, up, down, normed, preact, hidden, pieces):
+def forward_body(place_ref, rows, up, down, normed, preact, hidden, pieces):
     x = rows[...].astype(F32)
     mean = jnp.mean(x * x, axis=-1, keepdims=True)
     normed[...] = (x * lax.rsqrt(mean + 1e-05)).astype(BF16)
@@ -82,8 +95,8 @@
     for pair in range(8):
         columns = slice(pair * 256, pair * 256 + 256)
         part = jnp.dot(units, down[:, columns], preferred_element_type=F32).astype(BF16)
-        pieces[2 * pair] = part[:, :128]
-        pieces[2 * pair + 1] = part[:, 128:]
+        pieces[spot(place_ref[2], 2 * pair)] = part[:, :128]
+        pieces[spot(place_ref[2], 2 * pair + 1)] = part[:, 128:]
 
 
 def head_body(
@@ -115,26 +128,26 @@
         for side, columns in enumerate(sides):
             part = jnp.dot(rows, columns, preferred_element_type=F32).astype(BF16)
             for near in range(4):
-                piece = (zh + step) % 4 * 4 + near
+                piece = spot(core, (zh + step) % 4 * 4 + near)
                 out[piece, :, side * 256 : side * 256 + 256] = part[near * 128 : near * 128 + 128]
     for t in range(16):
         out[t, :, 512:] = updated
 
 
-def head_sum_body(got, head, updated):
+def head_sum_body(place_ref, got, head, updated):
     total = got[0, :, :512].astype(F32)
     for t in range(1, 16):
         total += got[t, :, :512].astype(F32)
     head[...] = total.astype(BF16)
     for t in range(16):
-        updated[:, t * 128 : t * 128 + 128] = got[t, :, 512:]
+        updated[:, t * 128 : t * 128 + 128] = got[spot(place_ref[2], t), :, 512:]
 
 
 def project_body(updated, proj, out):
     out[...] = jnp.dot(updated[...], proj[...], preferred_element_type=F32)
 
 
-def residue_body(scale_ref, length_ref, owners, projected, resid, head, proj, pieces):
+def residue_body(place_ref, scale_ref, length_ref, owners, projected, resid, head, proj, pieces):
     scale, length = scale_ref[0], length_ref[0]
     target = (resid[...].astype(F32) + head[...].astype(F32)).astype(BF16)
     residue = projected[...] - target.astype(F32)
@@ -154,8 +167,8 @@
             (((1,), (1,)), ((), ())),
             preferred_element_type=F32,
         ).astype(BF16)
-        pieces[2 * pair, :128] = part[:, :128]
-        pieces[2 * pair + 1, :128] = part[:, 128:]
+        pieces[spot(place_ref[2], 2 * pair), :128] = part[:, :128]
+        pieces[spot(place_ref[2], 2 * pair + 1), :128] = part[:, 128:]
     for t in range(16):
         pieces[t, 128:] = side
 
@@ -172,7 +185,7 @@
 
 def grad_body(place_ref, losses, blocks, hidden, preact, normed, down, mine, other):
     zl, core, source = place_ref[1], place_ref[2], place_ref[3]
-    out_grad = jnp.concatenate([blocks[t] for t in range(16)], axis=1)
+    out_grad = jnp.concatenate([blocks[spot(core, t)] for t in range(16)], axis=1)
     hidden_grad = lax.dot_general(
         out_grad, down[...], (((1,), (1,)), ((), ())), preferred_element_type=F32
     )
@@ -256,7 +269,7 @@
             shape((128, 176), BF16),
             shape((16, 128, 128), BF16),
         ),
-        (),
+        (place,),
         student_rows,
         up_weight.T,
         down_weight.T,
@@ -265,7 +278,7 @@
     half = lax.dynamic_slice_in_dim(far, dp % 2 * 128, 128, axis=1)
     half = lax.ppermute(half, "dp", FAR_STEP)
     got = lax.ppermute(jnp.concatenate([far, half], axis=1), "dp", CORES)
-    mixed = swap_all(mixed, "tensor")
+    mixed = across(mixed)
     got, mixed = lax.optimization_barrier((got, mixed))
     parts = call(
         head_body,
@@ -287,8 +300,8 @@
         "head_sum",
         16 * 128 * 512,
         (shape((128, 512), BF16), shape((128, 2048), BF16)),
-        (),
-        swap_all(parts, "tensor"),
+        (place,),
+        across(parts),
     )
     head = lax.ppermute(head, ("dp", "tensor"), HOME)
     projected = call(
@@ -299,7 +312,7 @@
         "residue",
         2 * 128 * 2048 * 512,
         shape((16, 144, 128), BF16),
-        (jnp.reshape(loss_scale, (1,)), own_length),
+        (place, jnp.reshape(loss_scale, (1,)), own_length),
         owners,
         projected,
         resid,
@@ -312,7 +325,7 @@
         16 * 128 * 128,
         (shape((16, 128, 128), BF16), shape((1, 128), F32)),
         (),
-        swap_all(pieces, "tensor"),
+        across(pieces),
     )
     mine, other = call(
         grad_body,
@@ -321,7 +334,7 @@
         (shape((16, 192, 128), BF16),) * 2,
         (place,),
         losses,
-        swap_all(blocks, "tensor"),
+        across(blocks),
         hidden,
         preact,
         normed,

time: 185 us -> 185 us (level)
  the two profiles are of different devices: /device:TPU:32 before, /device:TPU:1 now
where the time goes in v7:
time: 185 us; the launch traced here: 184 us
  blocking collectives  89.9 us (49%)
  starting transfers between devices  65.8 us (36%)
  Pallas kernels  10.9 us (6%)
  waiting for transfers between devices  9.43 us (5%)
  local copies, waits for them, and re-layouts  5.03 us (3%)
    all_to_all x4, blocking collectives, swap_all(): lax.all_to_all(x, axis, split_axis=0, concat_axis=0, tiled=True, axis_ind...  89.9 us
    ppermute x1, starting transfers between devices, on_device(): lax.ppermute(other, 'dp', CORES).astype(F32)  11.3 us
    pallas_call x9, Pallas kernels, call(): pl.pallas_call(body, out_shape=out_shape, in_specs=[smem] * len(scalars)...  10.9 us
    ppermute x3, starting transfers between devices, on_device(): near += lax.ppermute(pair[k], 'dp', ring_step(step)).astype(F32)  10.4 us
    ppermute x3, starting transfers between devices, on_device(): lax.ppermute(context, 'dp', ring_step(-k))  10.4 us
    ppermute x1, starting transfers between devices, on_device(): pair = lax.ppermute(out_weight, 'dp', CORES)  8.79 us
    all_to_all x1, starting transfers between devices, swap_all(): lax.all_to_all(x, axis, split_axis=0, concat_axis=0, tiled=True, axis_ind...  8.4 us
    ppermute x1, starting transfers between devices, on_device(): half = lax.ppermute(half, 'dp', FAR_STEP)  6 us
  transfers between devices with their start and end apart: 13, of which 7 were waited for; matrix products, arithmetic and copies ran while one was open for 1% of the time, Pallas kernels for 2%

profile of v7, /device:TPU:1, one launch (start us, length us, event | category | flops | bytes accessed | tf_op | source)
XLA Modules:
  0.0 183.7 jit_solution(12118769429327948203)
XLA Ops:
  0.6 8.8 %collective-permute-start.3 = (bf16[256,256]{1,0:T(8,128)(2,1)}, bf16[256,256]{1,0:T(8,128)(2,1)S(1)}, u32[]{:S(2)}, u32[]{:S(2)}) collective-permute-start(bf16[256,256]{1,0:T(8,128)(2,1)} %mine.1), channel_id=1, source_target_pairs={{0,16},{16,0},{32,48},{48,32},{64,80},{80,64},{96,112},{112,96},{1... | collective-permute-start | bytes 393224 | tf_op jit(solution)/shard_map/ppermute | solution.py:258
  9.4 1.2 collective-permute-done.3.other.pair
  10.6 0.0 copy-start.6
  10.6 0.9 copy-done.6
  11.5 0.0 copy-start.4
  11.5 0.0 copy-start.9
  11.5 3.6 %collective-permute-start.4 = (bf16[2,256,256]{2,1,0:T(8,128)(2,1)S(1)}, bf16[2,256,256]{2,1,0:T(8,128)(2,1)S(1)}, u32[]{:S(2)}, u32[]{:S(2)}) collective-permute-start(bf16[2,256,256]{2,1,0:T(8,128)(2,1)S(1)} %both_cores.1), channel_id=1, source_target_pairs={{0,384},{16,144},{32,416},{48,176},{64,448},{80,208},{96,480},{112... | collective-permute-start | bytes 786440 | tf_op jit(solution)/shard_map/ppermute | solution.py:260
  15.1 3.5 %collective-permute-start = (bf16[128,256]{1,0:T(8,128)(2,1)}, bf16[128,256]{1,0:T(8,128)(2,1)S(1)}, u32[]{:S(2)}, u32[]{:S(2)}) collective-permute-start(bf16[128,256]{1,0:T(8,128)(2,1)} %own.2), channel_id=1, source_target_pairs={{0,480},{16,48},{32,0},{48,80},{64,32},{80,112},{96,64},{112,144},... | collective-permute-start | bytes 196616 | tf_op jit(solution)/shard_map/ppermute | solution.py:257
  18.7 2.9 %collective-permute-start.1 = (bf16[128,256]{1,0:T(8,128)(2,1)}, bf16[128,256]{1,0:T(8,128)(2,1)S(1)}, u32[]{:S(2)}, u32[]{:S(2)}) collective-permute-start(bf16[128,256]{1,0:T(8,128)(2,1)} %own.2), channel_id=1, source_target_pairs={{0,32},{16,496},{32,64},{48,16},{64,96},{80,48},{96,128},{112,80},... | collective-permute-start | bytes 196616 | tf_op jit(solution)/shard_map/ppermute | solution.py:257
  21.6 3.9 %collective-permute-start.2 = (bf16[128,256]{1,0:T(8,128)(2,1)}, bf16[128,256]{1,0:T(8,128)(2,1)S(1)}, u32[]{:S(2)}, u32[]{:S(2)}) collective-permute-start(bf16[128,256]{1,0:T(8,128)(2,1)} %own.2), channel_id=1, source_target_pairs={{0,448},{16,80},{32,480},{48,112},{64,0},{80,144},{96,32},{112,176... | collective-permute-start | bytes 196616 | tf_op jit(solution)/shard_map/ppermute | solution.py:257
  25.6 0.1 stack.23.place_ref
  25.7 0.0 copy-start.1
  25.7 1.1 copy-done.1
  26.8 0.0 copy-start.3
  26.8 1.0 copy-done.3
  27.8 0.0 copy-start.5
  27.8 1.1 copy-done.5
  28.9 0.0 copy-start.7
  28.9 2.3 %forward.1 = (bf16[128,2048]{1,0:T(8,128)(2,1)S(1)}, f32[128,176]{1,0:T(8,128)S(1)}, bf16[128,176]{1,0:T(8,128)(2,1)S(1)}, bf16[16,128,128]{2,1,0:T(8,128)(2,1)}) custom-call(s32[5]{0:T(128)S(1)} %stack.23.place_ref, bf16[128,2048]{1,0:T(8,128)(2,1)S(1)} %copy-done.3, bf16[176,2048]{1,0:T(8,128)(2,1)S(1)} %bitcast.11, bf16[176,2048]{1,0:T(8,128)(2,1)S(1)} %bitcast.9), custom_call_target="tpu_custom_call" | custom-call | flops 184549376 | bytes 2097152 | tf_op jit(solution)/shard_map/forward/pallas_call | solution.py:66
  31.2 0.0 collective-permute-done.near1
  31.2 0.0 collective-permute-done.1.near2
  31.2 1.2 collective-permute-done.2.near3
  32.4 0.0 collective-permute-done.4.far
  32.4 6.0 %collective-permute-start.5 = (bf16[2,128,256]{2,1,0:T(8,128)(2,1)S(1)}, bf16[2,128,256]{2,1,0:T(8,128)(2,1)S(1)}, u32[]{:S(2)}, u32[]{:S(2)}) collective-permute-start(bf16[2,128,256]{2,1,0:T(8,128)(2,1)S(1)} %constant_dynamic-slice_fusion), channel_id=1, source_target_pairs={{0,384},{16,144},{32,416},{48,176},{64,448},{80,208},{96,480},{112... | collective-permute-start | bytes 393224 | tf_op jit(solution)/shard_map/ppermute | solution.py:279
  38.4 8.4 %all-to-all-start = ((bf16[16,128,128]{2,1,0:T(8,128)(2,1)}), bf16[16,128,128]{2,1,0:T(8,128)(2,1)S(1)}, u32[]{:S(2)}, u32[]{:S(2)}) async-start(bf16[16,128,128]{2,1,0:T(8,128)(2,1)} %get-tuple-element.26), calls=%async_computation | async-start | bytes 1048576 | tf_op jit(solution)/shard_map/all_to_all | solution.py:60
  46.8 0.0 collective-permute-done.5.half
  46.9 4.7 %collective-permute-start.6 = (bf16[2,384,256]{2,1,0:T(8,128)(2,1)S(1)}, bf16[2,384,256]{2,1,0:T(8,128)(2,1)S(1)}, u32[]{:S(2)}, u32[]{:S(2)}) collective-permute-start(bf16[2,384,256]{2,1,0:T(8,128)(2,1)S(1)} %pad_maximum_fusion), channel_id=1, source_target_pairs={{0,16},{16,0},{32,48},{48,32},{64,80},{80,64},{96,112},{112,96},{1... | collective-permute-start | bytes 1179656 | tf_op jit(solution)/shard_map/ppermute | solution.py:280
  51.6 0.4 all-to-all-done.mixed
  52.0 0.9 collective-permute-done.6.got
  52.9 0.0 copy-done.4
  52.9 0.0 copy-done.9
  52.9 0.0 copy-done.7
  52.9 1.4 head_parts.1
  54.3 37.0 %all_to_all.25.got = bf16[16,128,640]{2,1,0:T(8,128)(2,1)S(1)} all-to-all(bf16[16,128,640]{2,1,0:T(8,128)(2,1)S(1)} %head_parts.1), channel_id=1, replica_groups={{0,1,2,3,4,5,6,7,8,9,10,11,12,13,14,15},{31,30,29,28,27,26,25,24,23,22,..., dimensions={0} | all-to-all | bytes 5242880 | tf_op jit(solution)/shard_map/all_to_all | solution.py:60
  91.3 1.5 head_sum.1
  92.8 2.3 %collective-permute-start.7 = (bf16[128,512]{1,0:T(8,128)(2,1)}, bf16[128,512]{1,0:T(8,128)(2,1)}, u32[]{:S(2)}, u32[]{:S(2)}) collective-permute-start(bf16[128,512]{1,0:T(8,128)(2,1)} %get-tuple-element.34), channel_id=1, source_target_pairs={{0,0},{1,32},{2,480},{3,64},{4,4},{5,36},{6,484},{7,68},{8,8},{9,4... | collective-permute-start | bytes 393224 | tf_op jit(solution)/shard_map/ppermute | solution.py:306
  95.1 0.0 copy-done.11
  95.1 0.6 reduce_sum.9
  95.8 0.6 dynamic_slice.6.length_ref
  97.0 0.0 copy-done.10
  97.0 0.1 copy.12.owners
  97.2 0.0 copy-done
  97.2 0.4 project.1.projected
  97.6 0.0 collective-permute-done.7.head
  97.6 0.0 copy-done.8
  97.7 2.4 %residue.1 = bf16[16,144,128]{2,1,0:T(8,128)(2,1)S(1)} custom-call(s32[5]{0:T(128)S(1)} %stack.23.place_ref, f32[1]{0:T(128)} %bitcast.scale_ref, s32[1]{0:T(128)} %dynamic_slice.6.length_ref, s32[128,1]{1,0:T(8,128)S(1)} %copy.12.owners, f32[128,512]{1,0:T(8,128)S(1)} %project.1.projected, bf16[128,512]{1,0:T(8,128)(2,1)S(1)} %copy-done.8, ...), custom_call_target="tpu_custom_call" | custom-call | flops 268435456 | bytes 2097152 | tf_op jit(solution)/shard_map/residue/pallas_call | solution.py:66
  100.1 0.0 copy-start.2
  100.1 18.3 %all_to_all.26.got = bf16[16,144,128]{2,1,0:T(8,128)(2,1)S(1)} all-to-all(bf16[16,144,128]{2,1,0:T(8,128)(2,1)S(1)} %residue.1), channel_id=1, replica_groups={{0,1,2,3,4,5,6,7,8,9,10,11,12,13,14,15},{31,30,29,28,27,26,25,24,23,22,..., dimensions={0} | all-to-all | bytes 1179648 | tf_op jit(solution)/shard_map/all_to_all | solution.py:60
  118.4 0.1 back_sum.1
  118.5 11.3 %all_to_all.27.blocks = bf16[16,128,128]{2,1,0:T(8,128)(2,1)S(1)} all-to-all(bf16[16,128,128]{2,1,0:T(8,128)(2,1)S(1)} %get-tuple-element.36), channel_id=1, replica_groups={{0,1,2,3,4,5,6,7,8,9,10,11,12,13,14,15},{31,30,29,28,27,26,25,24,23,22,..., dimensions={0} | all-to-all | bytes 1048576 | tf_op jit(solution)/shard_map/all_to_all | solution.py:60
  129.8 0.0 copy-done.2
  129.8 1.9 %grad_terms.1 = (bf16[16,192,128]{2,1,0:T(8,128)(2,1)S(1)}, bf16[16,192,128]{2,1,0:T(8,128)(2,1)S(1)}) custom-call(s32[5]{0:T(128)S(1)} %stack.23.place_ref, f32[1,128]{1,0:T(1,128)S(1)} %get-tuple-element.35.losses, bf16[16,128,128]{2,1,0:T(8,128)(2,1)S(1)} %all_to_all.27.blocks, bf16[128,176]{1,0:T(8,128)(2,1)S(1)} %get-tuple-element.37.hidden, ...), custom_call_target="tpu_custom_call" | custom-call | flops 276824064 | bytes 2097152 | tf_op jit(solution)/shard_map/grad_terms/pallas_call | solution.py:66
  131.7 11.3 %collective-permute-start.8 = (bf16[16,192,128]{2,1,0:T(8,128)(2,1)S(1)}, bf16[16,192,128]{2,1,0:T(8,128)(2,1)S(1)}, u32[]{:S(2)}, u32[]{:S(2)}) collective-permute-start(bf16[16,192,128]{2,1,0:T(8,128)(2,1)S(1)} %get-tuple-element.41), channel_id=1, source_target_pairs={{0,16},{16,0},{32,48},{48,32},{64,80},{80,64},{96,112},{112,96},{1... | collective-permute-start | bytes 2359304 | tf_op jit(solution)/shard_map/ppermute | solution.py:343
  143.0 1.9 %collective-permute-done.8 = bf16[16,192,128]{2,1,0:T(8,128)(2,1)S(1)} collective-permute-done((bf16[16,192,128]{2,1,0:T(8,128)(2,1)S(1)}, bf16[16,192,128]{2,1,0:T(8,128)(2,1)S(1)}, u32[]{:S(2)}, u32[]{:S(2)}) %collective-permute-start.8) | collective-permute-done | bytes 786464 | tf_op jit(solution)/shard_map/ppermute | solution.py:343
  144.9 0.2 add_convert_fusion
  145.2 3.9 %collective-permute-start.10 = (bf16[4,192,128]{2,1,0:T(8,128)(2,1)S(1)}, bf16[4,192,128]{2,1,0:T(8,128)(2,1)S(1)}, u32[]{:S(2)}, u32[]{:S(2)}) collective-permute-start(bf16[4,192,128]{2,1,0:T(8,128)(2,1)S(1)} %get-tuple-element.47), channel_id=1, source_target_pairs={{0,64},{16,464},{32,96},{48,496},{64,128},{80,16},{96,160},{112,48... | collective-permute-start | bytes 589832 | tf_op jit(solution)/shard_map/ppermute | solution.py:347
  149.1 1.9 %collective-permute-start.11 = (bf16[4,192,128]{2,1,0:T(8,128)(2,1)S(1)}, bf16[4,192,128]{2,1,0:T(8,128)(2,1)S(1)}, u32[]{:S(2)}, u32[]{:S(2)}) collective-permute-start(bf16[4,192,128]{2,1,0:T(8,128)(2,1)S(1)} %get-tuple-element.46), channel_id=1, source_target_pairs={{0,480},{16,48},{32,0},{48,80},{64,32},{80,112},{96,64},{112,144},... | collective-permute-start | bytes 589832 | tf_op jit(solution)/shard_map/ppermute | solution.py:347
  151.0 4.6 %collective-permute-start.9 = (bf16[4,192,128]{2,1,0:T(8,128)(2,1)S(1)}, bf16[4,192,128]{2,1,0:T(8,128)(2,1)S(1)}, u32[]{:S(2)}, u32[]{:S(2)}) collective-permute-start(bf16[4,192,128]{2,1,0:T(8,128)(2,1)S(1)} %get-tuple-element.45), channel_id=1, source_target_pairs={{0,32},{16,496},{32,64},{48,16},{64,96},{80,48},{96,128},{112,80},... | collective-permute-start | bytes 589832 | tf_op jit(solution)/shard_map/ppermute | solution.py:347
  155.6 0.0 collective-permute-done.10
  155.6 2.5 %collective-permute-done.11 = bf16[4,192,128]{2,1,0:T(8,128)(2,1)S(1)} collective-permute-done((bf16[4,192,128]{2,1,0:T(8,128)(2,1)S(1)}, bf16[4,192,128]{2,1,0:T(8,128)(2,1)S(1)}, u32[]{:S(2)}, u32[]{:S(2)}) %collective-permute-start.11) | collective-permute-done | bytes 196640 | tf_op jit(solution)/shard_map/ppermute | solution.py:347
  158.1 1.4 collective-permute-done.9
  159.5 0.1 add_convert_fusion.1
  159.6 23.3 %all_to_all.28.got = bf16[4,192,128]{2,1,0:T(8,128)(2,1)S(1)} all-to-all(bf16[4,192,128]{2,1,0:T(8,128)(2,1)S(1)} %add_convert_fusion.1), channel_id=1, replica_groups={{0,128,256,384},{400,272,144,16},{32,160,288,416},{432,304,176,48},{64,..., dimensions={0} | all-to-all | bytes 393216 | tf_op jit(solution)/shard_map/all_to_all | solution.py:60
  182.9 0.8 finish.1
  (8 shorter events, 0.1 us)
Async XLA Ops:
  0.6 10.0 %collective-permute-start.3 = (bf16[256,256]{1,0:T(8,128)(2,1)}, bf16[256,256]{1,0:T(8,128)(2,1)S(1)}, u32[]{:S(2)}, u32[]{:S(2)}) collective-permute-start(bf16[256,256]{1,0:T(8,128)(2,1)} %mine.1), channel_id=1, source_target_pairs={{0,16},{16,0},{32,48},{48,32},{64,80},{80,64},{96,112},{112,96},{1... | collective-permute-start | bytes 393224 | tf_op jit(solution)/shard_map/ppermute | solution.py:258
  10.6 0.9 copy-start.6
  11.5 41.4 %copy-start.4 = (bf16[128,2048]{1,0:T(8,128)(2,1)S(1)}, bf16[128,2048]{1,0:T(8,128)(2,1)}, u32[]{:S(2)}) copy-start(bf16[128,2048]{1,0:T(8,128)(2,1)} %student.1) | copy-start | bytes 1572868
  11.5 41.4 %copy-start.9 = (bf16[128,256]{1,0:T(8,128)(2,1)S(1)}, bf16[128,256]{1,0:T(8,128)(2,1)}, u32[]{:S(2)}) copy-start(bf16[128,256]{1,0:T(8,128)(2,1)} %own.2) | copy-start | bytes 196612
  11.5 20.9 %collective-permute-start.4 = (bf16[2,256,256]{2,1,0:T(8,128)(2,1)S(1)}, bf16[2,256,256]{2,1,0:T(8,128)(2,1)S(1)}, u32[]{:S(2)}, u32[]{:S(2)}) collective-permute-start(bf16[2,256,256]{2,1,0:T(8,128)(2,1)S(1)} %both_cores.1), channel_id=1, source_target_pairs={{0,384},{16,144},{32,416},{48,176},{64,448},{80,208},{96,480},{112... | collective-permute-start | bytes 786440 | tf_op jit(solution)/shard_map/ppermute | solution.py:260
  15.1 16.1 %collective-permute-start = (bf16[128,256]{1,0:T(8,128)(2,1)}, bf16[128,256]{1,0:T(8,128)(2,1)S(1)}, u32[]{:S(2)}, u32[]{:S(2)}) collective-permute-start(bf16[128,256]{1,0:T(8,128)(2,1)} %own.2), channel_id=1, source_target_pairs={{0,480},{16,48},{32,0},{48,80},{64,32},{80,112},{96,64},{112,144},... | collective-permute-start | bytes 196616 | tf_op jit(solution)/shard_map/ppermute | solution.py:257
  18.7 12.6 %collective-permute-start.1 = (bf16[128,256]{1,0:T(8,128)(2,1)}, bf16[128,256]{1,0:T(8,128)(2,1)S(1)}, u32[]{:S(2)}, u32[]{:S(2)}) collective-permute-start(bf16[128,256]{1,0:T(8,128)(2,1)} %own.2), channel_id=1, source_target_pairs={{0,32},{16,496},{32,64},{48,16},{64,96},{80,48},{96,128},{112,80},... | collective-permute-start | bytes 196616 | tf_op jit(solution)/shard_map/ppermute | solution.py:257
  21.6 10.8 %collective-permute-start.2 = (bf16[128,256]{1,0:T(8,128)(2,1)}, bf16[128,256]{1,0:T(8,128)(2,1)S(1)}, u32[]{:S(2)}, u32[]{:S(2)}) collective-permute-start(bf16[128,256]{1,0:T(8,128)(2,1)} %own.2), channel_id=1, source_target_pairs={{0,448},{16,80},{32,480},{48,112},{64,0},{80,144},{96,32},{112,176... | collective-permute-start | bytes 196616 | tf_op jit(solution)/shard_map/ppermute | solution.py:257
  25.7 1.1 copy-start.1
  26.8 1.0 copy-start.3
  27.8 1.1 copy-start.5
  28.9 24.0 %copy-start.7 = (bf16[256,256]{1,0:T(8,128)(2,1)S(1)}, bf16[256,256]{1,0:T(8,128)(2,1)}, u32[]{:S(2)}) copy-start(bf16[256,256]{1,0:T(8,128)(2,1)} %mine.1) | copy-start | bytes 393220
  32.4 14.4 %collective-permute-start.5 = (bf16[2,128,256]{2,1,0:T(8,128)(2,1)S(1)}, bf16[2,128,256]{2,1,0:T(8,128)(2,1)S(1)}, u32[]{:S(2)}, u32[]{:S(2)}) collective-permute-start(bf16[2,128,256]{2,1,0:T(8,128)(2,1)S(1)} %constant_dynamic-slice_fusion), channel_id=1, source_target_pairs={{0,384},{16,144},{32,416},{48,176},{64,448},{80,208},{96,480},{112... | collective-permute-start | bytes 393224 | tf_op jit(solution)/shard_map/ppermute | solution.py:279
  38.4 13.5 %all-to-all-start = ((bf16[16,128,128]{2,1,0:T(8,128)(2,1)}), bf16[16,128,128]{2,1,0:T(8,128)(2,1)S(1)}, u32[]{:S(2)}, u32[]{:S(2)}) async-start(bf16[16,128,128]{2,1,0:T(8,128)(2,1)} %get-tuple-element.26), calls=%async_computation | async-start | bytes 1048576 | tf_op jit(solution)/shard_map/all_to_all | solution.py:60
  46.9 6.0 %collective-permute-start.6 = (bf16[2,384,256]{2,1,0:T(8,128)(2,1)S(1)}, bf16[2,384,256]{2,1,0:T(8,128)(2,1)S(1)}, u32[]{:S(2)}, u32[]{:S(2)}) collective-permute-start(bf16[2,384,256]{2,1,0:T(8,128)(2,1)S(1)} %pad_maximum_fusion), channel_id=1, source_target_pairs={{0,16},{16,0},{32,48},{48,32},{64,80},{80,64},{96,112},{112,96},{1... | collective-permute-start | bytes 1179656 | tf_op jit(solution)/shard_map/ppermute | solution.py:280
  91.3 3.8 %copy-start.11 = (s32[32]{0:T(128)S(1)}, s32[32]{0:T(128)}, u32[]{:S(2)}) copy-start(s32[32]{0:T(128)} %param.13) | copy-start | bytes 388
  91.3 5.7 %copy-start.10 = (s32[128,1]{0,1:T(1,128)S(1)}, s32[128,1]{0,1:T(1,128)}, u32[]{:S(2)}) copy-start(s32[128,1]{0,1:T(1,128)} %param.12) | copy-start | bytes 1540
  91.3 5.9 %copy-start = (bf16[2048,512]{1,0:T(8,128)(2,1)S(1)}, bf16[2048,512]{1,0:T(8,128)(2,1)}, u32[]{:S(2)}) copy-start(bf16[2048,512]{1,0:T(8,128)(2,1)} %proj.3) | copy-start | bytes 6291460
  92.8 4.8 %copy-start.8 = (bf16[128,512]{1,0:T(8,128)(2,1)S(1)}, bf16[128,512]{1,0:T(8,128)(2,1)}, u32[]{:S(2)}) copy-start(bf16[128,512]{1,0:T(8,128)(2,1)} %resid.1) | copy-start | bytes 393220
  92.8 4.8 %collective-permute-start.7 = (bf16[128,512]{1,0:T(8,128)(2,1)}, bf16[128,512]{1,0:T(8,128)(2,1)}, u32[]{:S(2)}, u32[]{:S(2)}) collective-permute-start(bf16[128,512]{1,0:T(8,128)(2,1)} %get-tuple-element.34), channel_id=1, source_target_pairs={{0,0},{1,32},{2,480},{3,64},{4,4},{5,36},{6,484},{7,68},{8,8},{9,4... | collective-permute-start | bytes 393224 | tf_op jit(solution)/shard_map/ppermute | solution.py:306
  100.1 29.7 %copy-start.2 = (bf16[2048,176]{0,1:T(8,128)(2,1)S(1)}, bf16[2048,176]{0,1:T(8,128)(2,1)}, u32[]{:S(2)}) copy-start(bf16[2048,176]{0,1:T(8,128)(2,1)} %param.16) | copy-start | bytes 2162692
  131.7 13.2 %collective-permute-start.8 = (bf16[16,192,128]{2,1,0:T(8,128)(2,1)S(1)}, bf16[16,192,128]{2,1,0:T(8,128)(2,1)S(1)}, u32[]{:S(2)}, u32[]{:S(2)}) collective-permute-start(bf16[16,192,128]{2,1,0:T(8,128)(2,1)S(1)} %get-tuple-element.41), channel_id=1, source_target_pairs={{0,16},{16,0},{32,48},{48,32},{64,80},{80,64},{96,112},{112,96},{1... | collective-permute-start | bytes 2359304 | tf_op jit(solution)/shard_map/ppermute | solution.py:343
  145.2 10.4 %collective-permute-start.10 = (bf16[4,192,128]{2,1,0:T(8,128)(2,1)S(1)}, bf16[4,192,128]{2,1,0:T(8,128)(2,1)S(1)}, u32[]{:S(2)}, u32[]{:S(2)}) collective-permute-start(bf16[4,192,128]{2,1,0:T(8,128)(2,1)S(1)} %get-tuple-element.47), channel_id=1, source_target_pairs={{0,64},{16,464},{32,96},{48,496},{64,128},{80,16},{96,160},{112,48... | collective-permute-start | bytes 589832 | tf_op jit(solution)/shard_map/ppermute | solution.py:347
  149.1 9.0 %collective-permute-start.11 = (bf16[4,192,128]{2,1,0:T(8,128)(2,1)S(1)}, bf16[4,192,128]{2,1,0:T(8,128)(2,1)S(1)}, u32[]{:S(2)}, u32[]{:S(2)}) collective-permute-start(bf16[4,192,128]{2,1,0:T(8,128)(2,1)S(1)} %get-tuple-element.46), channel_id=1, source_target_pairs={{0,480},{16,48},{32,0},{48,80},{64,32},{80,112},{96,64},{112,144},... | collective-permute-start | bytes 589832 | tf_op jit(solution)/shard_map/ppermute | solution.py:347
  151.0 8.5 %collective-permute-start.9 = (bf16[4,192,128]{2,1,0:T(8,128)(2,1)S(1)}, bf16[4,192,128]{2,1,0:T(8,128)(2,1)S(1)}, u32[]{:S(2)}, u32[]{:S(2)}) collective-permute-start(bf16[4,192,128]{2,1,0:T(8,128)(2,1)S(1)} %get-tuple-element.45), channel_id=1, source_target_pairs={{0,32},{16,496},{32,64},{48,16},{64,96},{80,48},{96,128},{112,80},... | collective-permute-start | bytes 589832 | tf_op jit(solution)/shard_map/ppermute | solution.py:347
